TPU v7x, 32 devices: a whole 2x2x4 slice. The times are simulated.
32 devices in a mesh: dp: 8 (over y, x, core), tp: 4 (over z).
Axes of the slice: x: 2, y: 2, z: 4, core: 2. Of those that a mesh axis runs over, the one named last changes fastest.
Arguments:
- mel_frames: bfloat16 [16384, 100], P(('dp', 'tp')), may hold values from -6 to 6
- noise_frames: bfloat16 [16384, 100], P(('dp', 'tp')), may hold values from -6 to 6
- text_ids: int32 [16384], P(('dp', 'tp')), may hold values from 0 to 2559
- span_mask: int32 [16384], P(('dp', 'tp')), may hold values 0 or 1
- lengths: int32 [16], P('dp'), may hold values from 256 to 1024, as said below
- audio_drop: int32 [16], P('dp'), may hold values 0 or 1
- text_drop: int32 [16], P('dp'), may hold values 0 or 1
- flow_times: float32 [16], P('dp'), may hold values from 0.05 to 0.95
- in_proj: bfloat16 [712, 1024], replicated, may hold values from -0.21875 to 0.21875
- text_table: bfloat16 [2560, 512], replicated, may hold values from -6 to 6
- time_proj: bfloat16 [256, 1024], replicated, may hold values from -0.375 to 0.375
- mod_proj: bfloat16 [1024, 6144], P(None, 'tp'), may hold values from -0.1875 to 0.1875
- qkv_proj: bfloat16 [1024, 3, 1024], P(None, None, 'tp'), may hold values from -0.1875 to 0.1875
- out_proj: bfloat16 [1024, 1024], P('tp'), may hold values from -3 to 3
- up_proj: bfloat16 [1024, 2048], P(None, 'tp'), may hold values from -0.1875 to 0.1875
- down_proj: bfloat16 [2048, 1024], P('tp'), may hold values from -0.125 to 0.125
- cotangent: bfloat16 [16384, 1024], P(('dp', 'tp')), may hold values from -6 to 6
Outputs:
- layer_out: bfloat16 [16384, 1024], P(('dp', 'tp'))
- mel_grad: float32 [16384, 100], P(('dp', 'tp'))
- in_proj_grad: float32 [712, 1024], P('tp')
- table_grad: float32 [2560, 512], P('tp')
- time_grad: float32 [256, 1024], P('tp')
- mod_grad: float32 [1024, 6144], P(None, 'tp')
- qkv_grad: float32 [1024, 3, 1024], P(None, None, 'tp')
- out_proj_grad: float32 [1024, 1024], P('tp')
- up_grad: float32 [1024, 2048], P(None, 'tp')
- down_grad: float32 [2048, 1024], P('tp')
Inputs may be any that keep to these rules, and one draw needn't show every extreme that they name: Utterance lengths; in every draw one utterance has exactly 1024 frames.
All inputs are finite; a program needn't handle non-finite values. No bound on the sum of `span_mask` or of `audio_drop` or of `text_drop` on one device may be relied on, other than what follows from the above.
Results may differ from a plain program's by a relative error of at most 0.024.
Values may be sent and summed in bfloat16 or wider, within the bound.
A program may use at most 192 MiB of HBM per device.

v0:
```python
import math

import jax
import jax.numpy as jnp
from jax import lax
from jax.sharding import PartitionSpec as P

MODEL_WIDTH = 1024
HEAD_DIM = 64
MEL_BINS = 100
TIME_DIM = 256
VOCABULARY = 2560
MAX_FRAMES = 1024
QUERY_BLOCK = 512


PRECISE = lax.Precision.HIGHEST


def layer_norm(values):
    average = jnp.mean(values, axis=-1, keepdims=True)
    centered = values - average
    spread = jnp.mean(centered * centered, axis=-1, keepdims=True)
    return centered * lax.rsqrt(spread + 1e-06)


def modulate(values, scale_part, shift_part):
    return layer_norm(values) * (1.0 + scale_part) + shift_part


def time_features(flow_times, width):
    half_dim = width // 2
    frequency = jnp.exp(
        jnp.arange(half_dim, dtype=jnp.float32) * (-math.log(10000.0) / (half_dim - 1))
    )
    angles = 1000.0 * flow_times[:, None] * frequency[None, :]
    return jnp.concatenate([jnp.sin(angles), jnp.cos(angles)], axis=1)


def rope_tables(positions, head_dim):
    half_dim = head_dim // 2
    inverse = jnp.exp(
        jnp.arange(half_dim, dtype=jnp.float32) * (-2.0 * math.log(10000.0) / head_dim)
    )
    angles = positions.astype(jnp.float32)[:, None] * inverse[None, :]
    return (jnp.cos(angles), jnp.sin(angles))


def rotate(values, cosine, sine):
    paired = values.reshape(values.shape[:-1] + (values.shape[-1] // 2, 2))
    first_part = paired[..., 0]
    second_part = paired[..., 1]
    cos_part = cosine[:, None, :]
    sin_part = sine[:, None, :]
    turned = jnp.stack(
        [
            first_part * cos_part - second_part * sin_part,
            second_part * cos_part + first_part * sin_part,
        ],
        axis=-1,
    )
    return turned.reshape(values.shape)


def contract(left, right, left_dim, right_dim):
    return lax.dot_general(
        left, right, (((left_dim,), (right_dim,)), ((), ())), preferred_element_type=jnp.float32
    )


def exact_contract(left, right, left_dim, right_dim):
    return lax.dot_general(
        left,
        right,
        (((left_dim,), (right_dim,)), ((), ())),
        precision=PRECISE,
        preferred_element_type=jnp.float32,
    )


def body(
    mel_frames,
    noise_frames,
    text_ids,
    span_mask,
    lengths,
    audio_drop,
    text_drop,
    flow_times,
    in_proj,
    text_table,
    time_proj,
    mod_proj,
    qkv_proj,
    out_proj,
    up_proj,
    down_proj,
    cotangent,
):
    tp_size = lax.axis_size("tp")
    tp_rank = lax.axis_index("tp")
    local_rows = mel_frames.shape[0]
    group_rows = local_rows * tp_size
    utt_count = flow_times.shape[0]
    head_local = qkv_proj.shape[2] // HEAD_DIM
    head_width = head_local * HEAD_DIM
    unit_local = up_proj.shape[1]
    scale_factor = 1.0 / math.sqrt(HEAD_DIM)
    block_count = MAX_FRAMES // QUERY_BLOCK
    local_frame = tp_rank * local_rows + jnp.arange(local_rows, dtype=jnp.int32)
    select_local = (
        (local_frame // MAX_FRAMES)[:, None] == jnp.arange(utt_count, dtype=jnp.int32)[None, :]
    ).astype(jnp.float32)

    def per_frame(values):
        return exact_contract(select_local, values, 1, 0)

    sinus = time_features(flow_times, TIME_DIM).astype(jnp.bfloat16)
    time_embed = jnp.dot(sinus, time_proj, preferred_element_type=jnp.float32)
    time_act = jax.nn.silu(time_embed).astype(jnp.bfloat16)
    mod_cols = jnp.dot(time_act, mod_proj, preferred_element_type=jnp.float32)
    modulation = lax.all_gather(mod_cols, "tp", axis=1, tiled=True)
    frame_mod = per_frame(modulation)
    shift_attn, scale_attn, gate_attn, shift_mlp, scale_mlp, gate_mlp = jnp.split(
        frame_mod, 6, axis=1
    )
    times_frame = per_frame(flow_times[:, None])
    keep_audio = per_frame((1 - audio_drop).astype(jnp.float32)[:, None])
    keep_text = per_frame((1 - text_drop).astype(jnp.float32)[:, None])
    keep_cond = (1 - span_mask).astype(jnp.float32)[:, None] * keep_audio
    mel_float = mel_frames.astype(jnp.float32)
    noisy = (1.0 - times_frame) * noise_frames.astype(jnp.float32) + times_frame * mel_float
    cond = mel_float * keep_cond
    text_emb = jnp.take(text_table, text_ids, axis=0).astype(jnp.float32) * keep_text
    features = jnp.concatenate([noisy, cond, text_emb], axis=1).astype(jnp.bfloat16)
    hidden = jnp.dot(features, in_proj, preferred_element_type=jnp.float32)
    normed_attn = modulate(hidden, scale_attn, shift_attn).astype(jnp.bfloat16)
    attn_in = lax.all_gather(normed_attn, "tp", axis=0, tiled=True)
    qkv_flat = qkv_proj.reshape(MODEL_WIDTH, 3 * head_width)
    qkv_pre = jnp.dot(attn_in, qkv_flat, preferred_element_type=jnp.float32).reshape(
        group_rows, 3, head_local, HEAD_DIM
    )
    group_pos = jnp.arange(group_rows, dtype=jnp.int32) % MAX_FRAMES
    cos_table, sin_table = rope_tables(group_pos, HEAD_DIM)
    query_rot = rotate(qkv_pre[:, 0], cos_table, sin_table).astype(jnp.bfloat16)
    key_rot = rotate(qkv_pre[:, 1], cos_table, sin_table).astype(jnp.bfloat16)
    values = qkv_pre[:, 2].astype(jnp.bfloat16)
    utt_shape = (utt_count, MAX_FRAMES, head_local, HEAD_DIM)
    query_utt = query_rot.reshape(utt_shape)
    key_utt = key_rot.reshape(utt_shape)
    value_utt = values.reshape(utt_shape)
    key_pos = jnp.arange(MAX_FRAMES, dtype=jnp.int32)

    def attend_utt(inputs):
        queries, keys_here, values_here, length_here = inputs
        valid = (key_pos < length_here)[None, None, :]
        outputs = []
        totals = []
        for block in range(block_count):
            rows = queries[block * QUERY_BLOCK : (block + 1) * QUERY_BLOCK]
            scores = (
                jnp.einsum("qhd,khd->hqk", rows, keys_here, preferred_element_type=jnp.float32)
                * scale_factor
            )
            scores = jnp.where(valid, scores, -1e30)
            peak = jnp.max(scores, axis=2, keepdims=True)
            expd = jnp.exp(scores - peak)
            total = jnp.sum(expd, axis=2, keepdims=True)
            probs = (expd / total).astype(jnp.bfloat16)
            outputs.append(
                jnp.einsum("hqk,khd->qhd", probs, values_here, preferred_element_type=jnp.float32)
            )
            totals.append((peak + jnp.log(total))[..., 0])
        return (jnp.concatenate(outputs, axis=0), jnp.concatenate(totals, axis=1))

    heads_raw, log_total = lax.map(attend_utt, (query_utt, key_utt, value_utt, lengths))
    heads_out = heads_raw.reshape(group_rows, head_width).astype(jnp.bfloat16)
    rows = lax.slice_in_dim(heads_out, 0, local_rows * lax.axis_size("tp"), axis=0)
    attn_sum = lax.psum_scatter(
        jnp.dot(rows, out_proj, preferred_element_type=jnp.float32).astype(jnp.bfloat16),
        "tp",
        scatter_dimension=0,
        tiled=True,
    ).astype(jnp.float32)
    hidden_mid = hidden + gate_attn * attn_sum
    normed_mlp = modulate(hidden_mid, scale_mlp, shift_mlp).astype(jnp.bfloat16)
    mlp_in = lax.all_gather(normed_mlp, "tp", axis=0, tiled=True)
    up_act = jnp.dot(mlp_in, up_proj, preferred_element_type=jnp.float32)
    gelu_act = jax.nn.gelu(up_act, approximate=True).astype(jnp.bfloat16)
    rows = lax.slice_in_dim(gelu_act, 0, local_rows * lax.axis_size("tp"), axis=0)
    mlp_sum = lax.psum_scatter(
        jnp.dot(rows, down_proj, preferred_element_type=jnp.float32).astype(jnp.bfloat16),
        "tp",
        scatter_dimension=0,
        tiled=True,
    ).astype(jnp.float32)
    layer_out = (hidden_mid + gate_mlp * mlp_sum).astype(jnp.bfloat16)
    out_grad = cotangent.astype(jnp.float32)
    mlp_grad = (gate_mlp * out_grad).astype(jnp.bfloat16)
    gate_mlp_grad = out_grad * mlp_sum
    shard_rows = lax.all_gather(mlp_grad, "tp", axis=0, tiled=True)
    down_total = jnp.zeros((unit_local, MODEL_WIDTH), jnp.float32)
    count = shard_rows.shape[0]
    acts = lax.slice_in_dim(gelu_act, 0, count, axis=0)
    down_total = down_total + contract(acts, shard_rows, 0, 0)
    act_total = contract(shard_rows, down_proj, 1, 1)
    down_grad = down_total
    gelu_value, gelu_pull = jax.vjp(lambda inner: jax.nn.gelu(inner, approximate=True), up_act)
    up_act_grad = gelu_pull(act_total)[0].astype(jnp.bfloat16)
    up_grad = contract(mlp_in, up_act_grad, 0, 0)
    rows = lax.slice_in_dim(up_act_grad, 0, local_rows * lax.axis_size("tp"), axis=0)
    normed_mlp_grad = lax.psum_scatter(
        contract(rows, up_proj, 1, 1).astype(jnp.bfloat16), "tp", scatter_dimension=0, tiled=True
    ).astype(jnp.float32)
    mlp_value, mlp_pull = jax.vjp(modulate, hidden_mid, scale_mlp, shift_mlp)
    mid_part, scale_mlp_grad, shift_mlp_grad = mlp_pull(normed_mlp_grad)
    mid_grad = out_grad + mid_part
    attn_grad = (gate_attn * mid_grad).astype(jnp.bfloat16)
    shard_rows = lax.all_gather(attn_grad, "tp", axis=0, tiled=True)
    offset = jnp.int32(0)
    out_total = jnp.zeros((head_width, MODEL_WIDTH), jnp.float32)
    heads_total = jnp.zeros((group_rows, head_width), jnp.float32)
    count = shard_rows.shape[0]
    rows = lax.dynamic_slice_in_dim(heads_out, offset, count, 0)
    out_total = out_total + contract(rows, shard_rows, 0, 0)
    heads_total = lax.dynamic_update_slice_in_dim(
        heads_total, contract(shard_rows, out_proj, 1, 1), offset, 0
    )
    out_proj_grad = out_total
    heads_grad_utt = heads_total.astype(jnp.bfloat16).reshape(utt_shape)

    def attend_back(inputs):
        queries, keys_here, values_here, grads_here, totals_here, length_here = inputs
        valid = (key_pos < length_here)[None, None, :]
        query_parts = []
        key_total = jnp.zeros(keys_here.shape, jnp.float32)
        value_total = jnp.zeros(values_here.shape, jnp.float32)
        for block in range(block_count):
            lower = block * QUERY_BLOCK
            rows = queries[lower : lower + QUERY_BLOCK]
            row_grads = grads_here[lower : lower + QUERY_BLOCK]
            row_totals = totals_here[:, lower : lower + QUERY_BLOCK][..., None]
            scores = (
                jnp.einsum("qhd,khd->hqk", rows, keys_here, preferred_element_type=jnp.float32)
                * scale_factor
            )
            scores = jnp.where(valid, scores, -1e30)
            probs = jnp.exp(scores - row_totals)
            prob_grad = jnp.einsum(
                "qhd,khd->hqk", row_grads, values_here, preferred_element_type=jnp.float32
            )
            inner = jnp.sum(prob_grad * probs, axis=2, keepdims=True)
            score_grad = (probs * (prob_grad - inner)).astype(jnp.bfloat16)
            query_parts.append(
                jnp.einsum(
                    "hqk,khd->qhd", score_grad, keys_here, preferred_element_type=jnp.float32
                )
                * scale_factor
            )
            key_total = (
                key_total
                + jnp.einsum("hqk,qhd->khd", score_grad, rows, preferred_element_type=jnp.float32)
                * scale_factor
            )
            value_total = value_total + jnp.einsum(
                "hqk,qhd->khd",
                probs.astype(jnp.bfloat16),
                row_grads,
                preferred_element_type=jnp.float32,
            )
        return (jnp.concatenate(query_parts, axis=0), key_total, value_total)

    query_back, key_back, value_back = lax.map(
        attend_back, (query_utt, key_utt, value_utt, heads_grad_utt, log_total, lengths)
    )
    head_shape = (group_rows, head_local, HEAD_DIM)
    query_grad = rotate(query_back.reshape(head_shape), cos_table, -sin_table).astype(jnp.bfloat16)
    key_grad = rotate(key_back.reshape(head_shape), cos_table, -sin_table).astype(jnp.bfloat16)
    value_grad = value_back.reshape(head_shape).astype(jnp.bfloat16)
    qkv_act_grad = jnp.stack([query_grad, key_grad, value_grad], axis=1).reshape(
        group_rows, 3 * head_width
    )
    qkv_grad = contract(attn_in, qkv_act_grad, 0, 0).reshape(MODEL_WIDTH, 3, head_width)
    rows = qkv_act_grad
    normed_attn_grad = lax.psum_scatter(
        contract(rows, qkv_flat, 1, 1).astype(jnp.bfloat16), "tp", scatter_dimension=0, tiled=True
    ).astype(jnp.float32)
    attn_value, attn_pull = jax.vjp(modulate, hidden, scale_attn, shift_attn)
    hidden_part, scale_attn_grad, shift_attn_grad = attn_pull(normed_attn_grad)
    hidden_grad = (mid_grad + hidden_part).astype(jnp.bfloat16)
    in_share = contract(features, hidden_grad, 0, 0)
    feature_grad = contract(hidden_grad, in_proj, 1, 1)
    mel_grad = (
        times_frame * feature_grad[:, :MEL_BINS]
        + keep_cond * feature_grad[:, MEL_BINS : 2 * MEL_BINS]
    )
    text_grad = feature_grad[:, 2 * MEL_BINS :].astype(jnp.bfloat16) * keep_text.astype(
        jnp.bfloat16
    )
    one_hot = (text_ids[:, None] == jnp.arange(VOCABULARY, dtype=jnp.int32)[None, :]).astype(
        jnp.bfloat16
    )
    table_share = contract(one_hot, text_grad, 0, 0)
    frame_mod_grad = jnp.concatenate(
        [
            shift_attn_grad,
            scale_attn_grad,
            gate_attn * 0.0 + attn_sum * mid_grad,
            shift_mlp_grad,
            scale_mlp_grad,
            gate_mlp_grad,
        ],
        axis=1,
    )
    mod_local = exact_contract(select_local, frame_mod_grad, 0, 0)
    mod_grad_cols = lax.psum_scatter(
        mod_local.astype(jnp.bfloat16), "tp", scatter_dimension=1, tiled=True
    )
    act_grad_part = contract(mod_grad_cols, mod_proj, 1, 1)
    act_grad = lax.psum(act_grad_part, "tp")
    silu_value, silu_pull = jax.vjp(jax.nn.silu, time_embed)
    embed_grad = silu_pull(act_grad)[0].astype(jnp.bfloat16)
    in_part, table_part = (
        lax.psum_scatter(
            in_share.astype(jnp.bfloat16), "tp", scatter_dimension=0, tiled=True
        ).astype(jnp.float32),
        lax.psum_scatter(
            table_share.astype(jnp.bfloat16), "tp", scatter_dimension=0, tiled=True
        ).astype(jnp.float32),
    )
    time_rows = TIME_DIM // tp_size
    sinus_share = lax.dynamic_slice_in_dim(sinus, tp_rank * time_rows, time_rows, 1)
    time_part = contract(sinus_share, embed_grad, 0, 0)
    mod_part = contract(time_act, mod_grad_cols, 0, 0)
    summed = lax.psum(
        (qkv_grad, out_proj_grad, up_grad, down_grad, in_part, table_part, time_part, mod_part),
        "dp",
    )
    qkv_total, out_total, up_total, down_total, in_total, table_total, time_total, mod_total = (
        summed
    )
    return (
        layer_out,
        mel_grad,
        in_total,
        table_total,
        time_total,
        mod_total,
        qkv_total,
        out_total,
        up_total,
        down_total,
    )


def solution(mesh):
    return jax.shard_map(
        body,
        mesh=mesh,
        in_specs=(
            P(("dp", "tp"), None),
            P(("dp", "tp"), None),
            P(("dp", "tp")),
            P(("dp", "tp")),
            P("dp"),
            P("dp"),
            P("dp"),
            P("dp"),
            P(),
            P(),
            P(),
            P(None, "tp"),
            P(None, None, "tp"),
            P("tp", None),
            P(None, "tp"),
            P("tp", None),
            P(("dp", "tp"), None),
        ),
        out_specs=(
            P(("dp", "tp"), None),
            P(("dp", "tp"), None),
            P("tp", None),
            P("tp", None),
            P("tp", None),
            P(None, "tp"),
            P(None, None, "tp"),
            P("tp", None),
            P(None, "tp"),
            P("tp", None),
        ),
        check_vma=False,
    )
```

profile of v0, /device:TPU:0, one launch (start us, length us, event | category | flops | bytes accessed | tf_op | source)
XLA Modules:
  0.0 1415.6 jit_solution(9258092192366782970)
XLA Ops:
  14.3 14.7 %all_gather.15 = f32[2,6144]{1,0:T(2,128)S(1)} all-gather(f32[2,1536]{1,0:T(2,128)S(1)} %fusion.172), channel_id=1, replica_groups=mesh['dp'=8,'tp'=4] {'tp'}, dimensions={1}, use_global_device_ids=true | all-gather | bytes 61440 | tf_op jit(solution)/shard_map/all_gather | solution.py:122
  57.3 77.4 %all-gather.5.cloned.1.call-done = bf16[2048,1024]{1,0:T(8,128)(2,1)} async-done(((bf16[512,1024]{1,0:T(8,128)(2,1)}), bf16[2048,1024]{1,0:T(8,128)(2,1)}) %all-gather.5.cloned.1.call-update) | async-done | bytes 4194320 | tf_op jit(solution)/shard_map/all_gather | solution.py:138
  134.7 5.7 fusion.93
  155.8 7.5 subtract_convert_fusion.2
  183.5 33.7 %while.28 = (s32[]{:T(128)}, bf16[2,1024,4,64]{1,3,2,0:T(8,128)(2,1)}, f32[2,4,1024]{2,1,0:T(4,128)S(1)}, bf16[2,1024,4,64]{1,3,2,0:T(8,128)(2,1)}, s32[2]{0:T(1...) while((s32[]{:T(128)}, ...), condition=%wide.region_7.8_spmd.clone, body=%wide.region_2.0_spmd.clone.sunk | while | flops 1125123072 | bytes 71475976 | solution.py:176
  224.2 75.4 %reduce-scatter.11.cloned.1.call-done = bf16[512,1024]{1,0:T(8,128)(2,1)} async-done(((bf16[2048,1024]{1,0:T(8,128)(2,1)}), bf16[512,1024]{1,0:T(8,128)(2,1)}) %reduce-scatter.11.cloned.1.call-update) | async-done | bytes 1048592 | tf_op jit(solution)/shard_map/reduce_scatter | solution.py:179
  308.8 80.6 %all-gather.9.cloned.1.call-done = bf16[2048,1024]{1,0:T(8,128)(2,1)} async-done(((bf16[512,1024]{1,0:T(8,128)(2,1)}), bf16[2048,1024]{1,0:T(8,128)(2,1)}) %all-gather.9.cloned.1.call-update) | async-done | bytes 4194320 | tf_op jit(solution)/shard_map/all_gather | solution.py:201
  389.5 6.9 fusion.181
  396.3 74.5 %all-gather.7.cloned.1.call-done = bf16[2048,1024]{1,0:T(8,128)(2,1)} async-done(((bf16[512,1024]{1,0:T(8,128)(2,1)}), bf16[2048,1024]{1,0:T(8,128)(2,1)}) %all-gather.7.cloned.1.call-update) | async-done | bytes 4194320 | tf_op jit(solution)/shard_map/all_gather | solution.py:187
  470.9 10.6 fusion.92
  487.2 7.2 convolution_convert_fusion.3
  494.5 68.1 %reduce-scatter.15.cloned.1.call-done = bf16[512,1024]{1,0:T(8,128)(2,1)} async-done(((bf16[2048,1024]{1,0:T(8,128)(2,1)}), bf16[512,1024]{1,0:T(8,128)(2,1)}) %reduce-scatter.15.cloned.1.call-update) | async-done | bytes 1048592 | tf_op jit(solution)/shard_map/reduce_scatter | solution.py:212
  565.6 76.4 %reduce-scatter.13.cloned.1.call-done = bf16[512,1024]{1,0:T(8,128)(2,1)} async-done(((bf16[2048,1024]{1,0:T(8,128)(2,1)}), bf16[512,1024]{1,0:T(8,128)(2,1)}) %reduce-scatter.13.cloned.1.call-update) | async-done | bytes 1048592 | tf_op jit(solution)/shard_map/reduce_scatter | solution.py:191
  651.2 81.4 %all-gather.11.cloned.1.call-done = bf16[2048,1024]{1,0:T(8,128)(2,1)} async-done(((bf16[512,1024]{1,0:T(8,128)(2,1)}), bf16[2048,1024]{1,0:T(8,128)(2,1)}) %all-gather.11.cloned.1.call-update) | async-done | bytes 4194320 | tf_op jit(solution)/shard_map/all_gather | solution.py:219
  746.8 164.1 %while.29 = (s32[]{:T(128)}, f32[2,1024,4,64]{1,0,3,2:T(2,128)}, f32[2,1024,4,64]{1,0,3,2:T(2,128)}, bf16[2,1024,4,64]{1,3,2,0:T(8,128)(2,1)}, bf16[2,1024,4,64]...) while((s32[]{:T(128)}, f32[2,1024,4,64]{1,0,3,2:T(2,128)}, ...), condition=%wide.region_18.19_spmd.clone, body=%wide.region_15.18_spmd.clone.sunk | while | flops 2748576768 | bytes 207777072 | solution.py:273
  762.3 10.2 multiply_reduce_fusion.7
  772.5 10.0 multiply_convert_fusion.11
  791.3 18.8 %dynamic_update_slice.33 = f32[2,1024,4,64]{1,0,3,2:T(2,128)} dynamic-update-slice(f32[2,1024,4,64]{1,0,3,2:T(2,128)} %get-tuple-element.477, f32[1,1024,4,64]{1,0,3,2:T(1,128)} %copy.87, s32[]{:T(128)S(6)} %copy.107, s32[]{:T(128)} %constant.121.clone.1..sunk.1, s32[]{:T(128)} %constant.121.clone.1..sunk.1, s32[]{:T(128)} %constant.121.clone.1..sunk.1) | dynamic-update-slice | bytes 2097156 | tf_op jit(solution)/shard_map/while/body/jit(dynamic_update_index_in_dim)/dynamic_update_slice | solution.py:176
  810.1 18.8 %dynamic_update_slice.34 = f32[2,1024,4,64]{1,0,3,2:T(2,128)} dynamic-update-slice(f32[2,1024,4,64]{1,0,3,2:T(2,128)} %get-tuple-element.478, f32[1,1024,4,64]{1,0,3,2:T(1,128)} %copy.88, s32[]{:T(128)S(6)} %copy.107, s32[]{:T(128)} %constant.121.clone.1..sunk.1, s32[]{:T(128)} %constant.121.clone.1..sunk.1, s32[]{:T(128)} %constant.121.clone.1..sunk.1) | dynamic-update-slice | bytes 2097156 | tf_op jit(solution)/shard_map/while/body/jit(dynamic_update_index_in_dim)/dynamic_update_slice | solution.py:176
  844.1 10.2 multiply_reduce_fusion.7
  854.3 10.0 multiply_convert_fusion.11
  873.1 18.8 %dynamic_update_slice.33 = f32[2,1024,4,64]{1,0,3,2:T(2,128)} dynamic-update-slice(f32[2,1024,4,64]{1,0,3,2:T(2,128)} %get-tuple-element.477, f32[1,1024,4,64]{1,0,3,2:T(1,128)} %copy.87, s32[]{:T(128)S(6)} %copy.107, s32[]{:T(128)} %constant.121.clone.1..sunk.1, s32[]{:T(128)} %constant.121.clone.1..sunk.1, s32[]{:T(128)} %constant.121.clone.1..sunk.1) | dynamic-update-slice | bytes 2097156 | tf_op jit(solution)/shard_map/while/body/jit(dynamic_update_index_in_dim)/dynamic_update_slice | solution.py:176
  891.9 18.8 %dynamic_update_slice.34 = f32[2,1024,4,64]{1,0,3,2:T(2,128)} dynamic-update-slice(f32[2,1024,4,64]{1,0,3,2:T(2,128)} %get-tuple-element.478, f32[1,1024,4,64]{1,0,3,2:T(1,128)} %copy.88, s32[]{:T(128)S(6)} %copy.107, s32[]{:T(128)} %constant.121.clone.1..sunk.1, s32[]{:T(128)} %constant.121.clone.1..sunk.1, s32[]{:T(128)} %constant.121.clone.1..sunk.1) | dynamic-update-slice | bytes 2097156 | tf_op jit(solution)/shard_map/while/body/jit(dynamic_update_index_in_dim)/dynamic_update_slice | solution.py:176
  926.3 8.3 subtract_convert_fusion
  958.0 73.6 %reduce-scatter.17.cloned.1.call-done = bf16[512,1024]{1,0:T(8,128)(2,1)} async-done(((bf16[2048,1024]{1,0:T(8,128)(2,1)}), bf16[512,1024]{1,0:T(8,128)(2,1)}) %reduce-scatter.17.cloned.1.call-update) | async-done | bytes 1048592 | tf_op jit(solution)/shard_map/reduce_scatter | solution.py:285
  1056.7 7.0 fusion.184
  1075.2 47.0 %fusion.4 = bf16[184,1024]{1,0:T(8,128)(2,1)S(1)} fusion(bf16[712,1024]{1,0:T(8,128)(2,1)} %convolution_convert_fusion.7), kind=kCustom, calls=%all-reduce-scatter | all-reduce-scatter fusion | flops 753665 | bytes 1835520
  1122.2 5.8 collective-permute-start
  1140.8 15.6 %psum.65 = f32[2,1024]{1,0:T(2,128)S(1)} all-reduce(f32[2,1024]{1,0:T(2,128)S(1)} %fusion.112), channel_id=1, replica_groups=mesh['dp'=8,'tp'=4] {'tp'}, use_global_device_ids=true, to_apply=%region_27.28 | all-reduce | flops 2048 | bytes 16384 | tf_op jit(solution)/shard_map/psum | solution.py:320
  1164.6 77.4 %all-reduce.7 = f32[640,512]{1,0:T(8,128)} all-reduce(bf16[640,512]{1,0:T(8,128)(2,1)} %reduce-scatter.19.cloned.1.call-done), channel_id=1, replica_groups=mesh['dp'=8,'tp'=4] {'dp'}, use_global_device_ids=true, to_apply=%region_25.26 | all-reduce | flops 327680 | bytes 1966080 | tf_op jit(solution)/shard_map/psum | solution.py:335
  1242.0 150.8 %all-reduce.6.cloned.1.call-done = (f32[178,1024]{1,0:T(8,128)}, f32[64,1024]{1,0:T(8,128)}, f32[1024,1536]{1,0:T(8,128)}, f32[1024,3,256]{2,0,1:T(8,128)}, f32[...) async-done(((f32[178,1024]{1,0:T(8,128)}, f32[64,1024]{1,0:T(8,128)}, f32[1024,1536]{1,0:T(8,128)}, f32[1024,3,256]{2,0,1:T(8,128)}, ...) | async-done | bytes 15671312 | tf_op jit(solution)/shard_map/psum | solution.py:335
  1396.6 6.1 copy.133
  (359 shorter events, 304.7 us)
Async XLA Ops:
  7.2 127.5 %all-gather.5.cloned.1.call-start = ((), (), s32[]{:S(2)}) async-start(), calls=%async_computation.6 | async-start | bytes 5242880 | tf_op jit(solution)/shard_map/all_gather | solution.py:138
  9.5 31.9 %copy-start.47 = (s32[512]{0:T(512)}, s32[512]{0:T(512)S(1)}, u32[]{:S(2)}) copy-start(s32[512]{0:T(512)S(1)} %add_select_fusion.1) | copy-start | bytes 6148
  10.5 20.3 %copy-start.61 = (f32[1,512]{1,0:T(1,128)}, f32[1,512]{1,0:T(1,128)S(1)}, u32[]{:S(2)}) copy-start(f32[1,512]{1,0:T(1,128)S(1)} %fusion.121) | copy-start | bytes 6148
  11.5 25.0 %copy-start.65 = (f32[1,512]{1,0:T(1,128)}, f32[1,512]{1,0:T(1,128)S(1)}, u32[]{:S(2)}) copy-start(f32[1,512]{1,0:T(1,128)S(1)} %fusion.119) | copy-start | bytes 6148
  12.6 18.2 %copy-start.68 = (bf16[2,128]{1,0:T(2,128)(2,1)}, bf16[2,128]{1,0:T(2,128)(2,1)S(1)}, u32[]{:S(2)}) copy-start(bf16[2,128]{1,0:T(2,128)(2,1)S(1)} %get-tuple-element.293) | copy-start | bytes 1540
  12.6 18.2 %copy-start.70 = (bf16[2,128]{1,0:T(2,128)(2,1)}, bf16[2,128]{1,0:T(2,128)(2,1)S(1)}, u32[]{:S(2)}) copy-start(bf16[2,128]{1,0:T(2,128)(2,1)S(1)} %get-tuple-element.294) | copy-start | bytes 1540
  13.8 15.3 %copy-start.41 = (f32[2,1024]{1,0:T(2,128)}, f32[2,1024]{1,0:T(2,128)S(1)}, u32[]{:S(2)}) copy-start(f32[2,1024]{1,0:T(2,128)S(1)} %fusion.149) | copy-start | bytes 24580
  30.9 10.1 copy-start.43
  52.6 247.0 %reduce-scatter.11.cloned.1.call-start = ((), (), s32[]{:S(2)}) async-start(), calls=%async_computation.7 | async-start | bytes 5242880 | tf_op jit(solution)/shard_map/reduce_scatter | solution.py:179
  57.3 98.5 %copy-start.27 = (f32[2048,32]{0,1:T(8,128)}, f32[2048,32]{0,1:T(8,128)S(1)}, u32[]{:S(2)}) copy-start(f32[2048,32]{0,1:T(8,128)S(1)} %get-tuple-element.292) | copy-start | bytes 786436
  173.0 10.5 copy-start.77
  224.2 165.3 %all-gather.9.cloned.1.call-start = ((), (), s32[]{:S(2)}) async-start(), calls=%async_computation.10 | async-start | bytes 5242880 | tf_op jit(solution)/shard_map/all_gather | solution.py:201
  302.6 339.4 %copy-start.51 = (f32[512]{0:T(512)}, f32[512]{0:T(512)S(1)}, u32[]{:S(2)}) copy-start(f32[512]{0:T(512)S(1)} %broadcast_multiply_fusion) | copy-start | bytes 6148
  303.0 339.1 %copy-start.55 = (f32[512]{0:T(512)}, f32[512]{0:T(512)S(1)}, u32[]{:S(2)}) copy-start(f32[512]{0:T(512)S(1)} %fusion.146) | copy-start | bytes 6148
  308.0 162.8 %all-gather.7.cloned.1.call-start = ((), (), s32[]{:S(2)}) async-start(), calls=%async_computation.8 | async-start | bytes 5242880 | tf_op jit(solution)/shard_map/all_gather | solution.py:187
  308.6 254.0 %reduce-scatter.15.cloned.1.call-start = ((), (), s32[]{:S(2)}) async-start(), calls=%async_computation.11 | async-start | bytes 5242880 | tf_op jit(solution)/shard_map/reduce_scatter | solution.py:212
  470.9 11.9 copy-start.76
  487.1 154.9 %reduce-scatter.13.cloned.1.call-start = ((), (), s32[]{:S(2)}) async-start(), calls=%async_computation.9 | async-start | bytes 5242880 | tf_op jit(solution)/shard_map/reduce_scatter | solution.py:191
  494.5 238.2 %all-gather.11.cloned.1.call-start = ((), (), s32[]{:S(2)}) async-start(), calls=%async_computation.12 | async-start | bytes 5242880 | tf_op jit(solution)/shard_map/all_gather | solution.py:219
  651.2 380.4 %reduce-scatter.17.cloned.1.call-start = ((), (), s32[]{:S(2)}) async-start(), calls=%async_computation.13 | async-start | bytes 5242880 | tf_op jit(solution)/shard_map/reduce_scatter | solution.py:285
  916.8 9.5 copy-start.28
  956.1 77.1 %copy-start.50 = (f32[512]{0:T(512)S(1)}, f32[512]{0:T(512)}, u32[]{:S(2)}) copy-start(f32[512]{0:T(512)} %copy-done.49) | copy-start | bytes 6148
  956.1 77.1 %copy-start.54 = (f32[512]{0:T(512)S(1)}, f32[512]{0:T(512)}, u32[]{:S(2)}) copy-start(f32[512]{0:T(512)} %copy-done.53) | copy-start | bytes 6148
  956.1 182.8 %reduce-scatter.21.cloned.1.call-start = ((), (), s32[]{:S(2)}) async-start(), calls=%async_computation.15 | async-start | bytes 1966080
  958.0 77.7 %copy-start.58 = (f32[512]{0:T(512)S(1)}, f32[512]{0:T(512)}, u32[]{:S(2)}) copy-start(f32[512]{0:T(512)} %copy-done.57) | copy-start | bytes 6148
  1051.8 112.8 %reduce-scatter.19.cloned.1.call-start = ((), (), s32[]{:S(2)}) async-start(), calls=%async_computation.14 | async-start | bytes 3276800 | tf_op jit(solution)/shard_map/reduce_scatter | solution.py:327
  1056.4 336.5 %all-reduce.6.cloned.1.call-start = ((), (), s32[]{:S(2)}) async-start(), calls=%async_computation.16 | async-start | bytes 31391744 | tf_op jit(solution)/shard_map/psum | solution.py:335
  1056.7 7.0 copy-start.74
  1122.2 10.5 collective-permute-start
  1132.7 23.7 %copy-start.42 = (f32[2,1024]{1,0:T(2,128)S(1)}, f32[2,1024]{1,0:T(2,128)}, u32[]{:S(2)}) copy-start(f32[2,1024]{1,0:T(2,128)} %copy-done.41) | copy-start | bytes 24580
  1132.7 23.7 %copy-start.69 = (bf16[2,128]{1,0:T(2,128)(2,1)S(1)}, bf16[2,128]{1,0:T(2,128)(2,1)}, u32[]{:S(2)}) copy-start(bf16[2,128]{1,0:T(2,128)(2,1)} %copy-done.68) | copy-start | bytes 1540
  1132.7 23.7 %copy-start.71 = (bf16[2,128]{1,0:T(2,128)(2,1)S(1)}, bf16[2,128]{1,0:T(2,128)(2,1)}, u32[]{:S(2)}) copy-start(bf16[2,128]{1,0:T(2,128)(2,1)} %copy-done.70) | copy-start | bytes 1540
  (68 other events, 222.0 us)
Sparse Core Ops, SparseCore 0:
  52.7 81.9 all-gather.4
  224.3 75.2 reduce-scatter.10
  308.2 81.2 all-gather.8
  391.5 79.2 all-gather.6
  487.3 75.2 reduce-scatter.14
  564.8 77.2 reduce-scatter.12
  651.3 81.2 all-gather.10
  956.2 75.2 reduce-scatter.16
  1051.9 37.9 reduce-scatter.20
  1092.1 62.0 reduce-scatter.18
  1162.3 230.4 all-reduce.5
where the time goes:
time: 1430 us; the launch traced here: 1420 us
  waiting for transfers between devices  759 us (53%)
  local copies, waits for them, and re-layouts  196 us (14%)
  matrix products  183 us (13%)
  blocking collectives  155 us (11%)
  other arithmetic  98.3 us (7%)
  between operations  15.8 us (1%)
    psum x1, waiting for transfers between devices, body(): lax.psum((qkv_grad, out_proj_grad, up_grad, down_grad, in_part, table_par...  151 us
    dynamic_update_slice x8, local copies, waits for them, and re-layouts, body(): lax.map(attend_utt, (query_utt, key_utt, value_utt, lengths))  83.6 us
    all_gather x1, waiting for transfers between devices, body(): shard_rows = lax.all_gather(attn_grad, 'tp', axis=0, tiled=True)  81.4 us
    all_gather x1, waiting for transfers between devices, body(): shard_rows = lax.all_gather(mlp_grad, 'tp', axis=0, tiled=True)  80.6 us
    psum x1, blocking collectives, body(): lax.psum((qkv_grad, out_proj_grad, up_grad, down_grad, in_part, table_par...  77.4 us
    all_gather x1, waiting for transfers between devices, body(): attn_in = lax.all_gather(normed_attn, 'tp', axis=0, tiled=True)  77.4 us
    reduce_scatter x1, waiting for transfers between devices, body(): lax.psum_scatter(jnp.dot(rows, down_proj, preferred_element_type=jnp.floa...  76.4 us
    reduce_scatter x1, waiting for transfers between devices, body(): lax.psum_scatter(jnp.dot(rows, out_proj, preferred_element_type=jnp.float...  75.4 us
  transfers between devices with their start and end apart: 12, of which 9 were waited for; matrix products, arithmetic and copies ran while one was open for 8% of the time, Pallas kernels for 0%

commit v1 on v0

v1 whole, which is shorter than its diff:
```python
import functools
import math

import jax
import jax.numpy as jnp
from jax import lax
from jax.experimental import pallas as pl
from jax.experimental.pallas import tpu as pltpu
from jax.sharding import PartitionSpec as P

WIDTH = 1024
HEAD_DIM = 64
MEL_BINS = 100
TEXT_DIM = 512
TIME_DIM = 256
VOCABULARY = 2560
FFN_DIM = 2048
AXES = ("dp", "tp")
BF = jnp.bfloat16
F32 = jnp.float32


def dot(left, right, left_dim=1, right_dim=0):
    return lax.dot_general(
        left, right, (((left_dim,), (right_dim,)), ((), ())), preferred_element_type=F32
    )


def time_features(flow_times, width):
    half_dim = width // 2
    frequency = jnp.exp(
        jnp.arange(half_dim, dtype=F32) * (-math.log(10000.0) / (half_dim - 1))
    )
    angles = 1000.0 * flow_times[:, None] * frequency[None, :]
    return jnp.concatenate([jnp.sin(angles), jnp.cos(angles)], axis=1)


def rope_tables(positions):
    lane = jnp.arange(WIDTH, dtype=jnp.int32)
    pair = ((lane % HEAD_DIM) // 2).astype(F32)
    inverse = jnp.exp(pair * (-2.0 * math.log(10000.0) / HEAD_DIM))
    angles = positions.astype(F32)[:, None] * inverse[None, :]
    sign = jnp.where(lane % 2 == 0, -1.0, 1.0)
    return jnp.cos(angles), jnp.sin(angles) * sign[None, :]


def swap_pairs(values):
    shape = values.shape
    return jnp.flip(values.reshape(shape[0], shape[1] // 2, 2), axis=2).reshape(shape)


def norm_parts(values):
    average = jnp.mean(values, axis=-1, keepdims=True)
    centered = values - average
    spread = jnp.mean(centered * centered, axis=-1, keepdims=True)
    inverse = lax.rsqrt(spread + 1e-06)
    return centered * inverse, inverse


def norm_back(normed, inverse, scale_part, grad):
    inner = grad * (1.0 + scale_part)
    first = jnp.mean(inner, axis=-1, keepdims=True)
    second = jnp.mean(inner * normed, axis=-1, keepdims=True)
    return inverse * (inner - first - normed * second)


def head_masks(rows):
    lane = lax.broadcasted_iota(jnp.int32, (rows, 2 * HEAD_DIM), 1)
    return [lane < HEAD_DIM, lane >= HEAD_DIM]


def key_bias(info_ref, which, rows, lanes):
    position = lax.broadcasted_iota(jnp.int32, (rows, lanes), 0) + info_ref[1 + which]
    return position < info_ref[0]


def attend_kernel(info_ref, q_ref, k0_ref, v0_ref, k1_ref, v1_ref, o_ref, lse_ref):
    rows = q_ref.shape[0]
    keys = k0_ref.shape[0]
    query = q_ref[...] * jnp.asarray(1.0 / math.sqrt(HEAD_DIM), BF)
    masks = head_masks(rows)
    valid0 = key_bias(info_ref, 0, keys, rows)
    valid1 = key_bias(info_ref, 1, keys, rows)
    vt0 = v0_ref[...].T
    vt1 = v1_ref[...].T
    parts = []
    for head in range(2):
        masked = jnp.where(masks[head], query, jnp.zeros_like(query))
        s0 = jnp.where(valid0, dot(k0_ref[...], masked, 1, 1), -1e30)
        s1 = jnp.where(valid1, dot(k1_ref[...], masked, 1, 1), -1e30)
        peak = jnp.maximum(
            jnp.max(s0, axis=0, keepdims=True), jnp.max(s1, axis=0, keepdims=True)
        )
        e0 = jnp.exp(s0 - peak)
        e1 = jnp.exp(s1 - peak)
        total = jnp.sum(e0, axis=0, keepdims=True) + jnp.sum(e1, axis=0, keepdims=True)
        side = slice(head * HEAD_DIM, (head + 1) * HEAD_DIM)
        acc = dot(vt0[side], e0.astype(BF)) + dot(vt1[side], e1.astype(BF))
        parts.append(acc / total)
        lse_ref[head] = peak + jnp.log(total)
    o_ref[...] = jnp.concatenate(parts, axis=0).T.astype(BF)


def attend_back_kernel(
    info_ref, q_ref, k0_ref, v0_ref, k1_ref, v1_ref, do_ref, o_ref, lse_ref,
    dq_ref, dk0_ref, dv0_ref, dk1_ref, dv1_ref,
):
    rows = q_ref.shape[0]
    keys = k0_ref.shape[0]
    scale = 1.0 / math.sqrt(HEAD_DIM)
    query = q_ref[...] * jnp.asarray(scale, BF)
    grads = do_ref[...]
    masks = head_masks(rows)
    product = (grads.astype(F32) * o_ref[...].astype(F32)).T
    dq_parts = [None, None]
    for which, (k_ref, v_ref, dk_ref, dv_ref) in enumerate(
        ((k0_ref, v0_ref, dk0_ref, dv0_ref), (k1_ref, v1_ref, dk1_ref, dv1_ref))
    ):
        valid = key_bias(info_ref, which, keys, rows)
        kt = k_ref[...].T
        dk = jnp.zeros(k_ref.shape, F32)
        dv = jnp.zeros(v_ref.shape, F32)
        for head in range(2):
            side = slice(head * HEAD_DIM, (head + 1) * HEAD_DIM)
            masked = jnp.where(masks[head], query, jnp.zeros_like(query))
            gmask = jnp.where(masks[head], grads, jnp.zeros_like(grads))
            delta = jnp.sum(product[side], axis=0, keepdims=True)
            scores = jnp.where(valid, dot(k_ref[...], masked, 1, 1), -1e30)
            probs = jnp.exp(scores - lse_ref[head])
            prob_grad = dot(v_ref[...], gmask, 1, 1)
            score_grad = (probs * (prob_grad - delta)).astype(BF)
            dv += dot(probs.astype(BF), gmask)
            dk += dot(score_grad, masked)
            part = dot(kt[side], score_grad)
            dq_parts[head] = part if which == 0 else dq_parts[head] + part
        dk_ref[...] = dk.astype(dk_ref.dtype)
        dv_ref[...] = dv.astype(dv_ref.dtype)
    dq_ref[...] = jnp.concatenate(dq_parts, axis=0).T * scale


def attend(info, query, own, other):
    rows = query.shape[0]
    pairs = WIDTH // (2 * HEAD_DIM)
    tile = lambda offset: pl.BlockSpec((rows, 2 * HEAD_DIM), lambda i: (0, i + offset))
    return pl.pallas_call(
        attend_kernel,
        grid=(pairs,),
        in_specs=[pl.BlockSpec(memory_space=pltpu.SMEM), tile(0), tile(0), tile(pairs), tile(0), tile(pairs)],
        out_specs=[tile(0), pl.BlockSpec((2, 1, rows), lambda i: (i, 0, 0))],
        out_shape=[
            jax.ShapeDtypeStruct((rows, WIDTH), BF),
            jax.ShapeDtypeStruct((2 * pairs, 1, rows), F32),
        ],
        compiler_params=pltpu.CompilerParams(vmem_limit_bytes=48 * 1024 * 1024),
    )(info, query, own, own, other, other)


def attend_back(info, query, own, other, grads, outputs, lse):
    rows = query.shape[0]
    pairs = WIDTH // (2 * HEAD_DIM)
    tile = lambda offset: pl.BlockSpec((rows, 2 * HEAD_DIM), lambda i: (0, i + offset))
    return pl.pallas_call(
        attend_back_kernel,
        grid=(pairs,),
        in_specs=[
            pl.BlockSpec(memory_space=pltpu.SMEM),
            tile(0), tile(0), tile(pairs), tile(0), tile(pairs), tile(0), tile(0),
            pl.BlockSpec((2, 1, rows), lambda i: (i, 0, 0)),
        ],
        out_specs=[tile(0)] * 5,
        out_shape=[
            jax.ShapeDtypeStruct((rows, WIDTH), F32),
            jax.ShapeDtypeStruct((rows, WIDTH), F32),
            jax.ShapeDtypeStruct((rows, WIDTH), F32),
            jax.ShapeDtypeStruct((rows, WIDTH), BF),
            jax.ShapeDtypeStruct((rows, WIDTH), BF),
        ],
        compiler_params=pltpu.CompilerParams(vmem_limit_bytes=48 * 1024 * 1024),
    )(info, query, own, own, other, other, grads, outputs, lse)


def body(
    mel_frames, noise_frames, text_ids, span_mask, lengths, audio_drop, text_drop, flow_times,
    in_proj, text_table, time_proj, mod_proj, qkv_proj, out_proj, up_proj, down_proj, cotangent,
):
    dp_size = lax.axis_size("dp")
    tp_size = lax.axis_size("tp")
    dp_rank = lax.axis_index("dp")
    tp_rank = lax.axis_index("tp")
    local_rows = mel_frames.shape[0]
    per_group = flow_times.shape[0]
    utt_total = per_group * dp_size
    dp_low = dp_rank % 2
    tp_low = tp_rank % 2
    stay = dp_low == tp_low
    pairs = []
    for d in range(dp_size):
        for t in range(tp_size):
            if d % 2 != t % 2:
                pairs.append((d * tp_size + t, (d ^ 1) * tp_size + (t ^ 1)))

    def swap(values):
        return jnp.where(stay, values, lax.ppermute(values, AXES, pairs))

    sibling = [(d, d ^ 1) for d in range(dp_size)]
    source_dp = dp_rank - dp_low + tp_low
    utterance = source_dp * per_group + tp_rank // 2
    half = dp_low

    def gather(shard, axis):
        size = shard.shape[axis] // dp_size
        piece = lax.dynamic_slice_in_dim(shard, dp_rank * size, size, axis)
        return lax.all_gather(piece, AXES, axis=0, tiled=False).reshape(
            (dp_size, tp_size) + piece.shape
        )

    qkv_full = gather(qkv_proj, 0).transpose(0, 2, 3, 1, 4).reshape(WIDTH, 3 * WIDTH)
    out_full = gather(out_proj, 0).transpose(1, 0, 2, 3).reshape(WIDTH, WIDTH)
    up_full = gather(up_proj, 0).transpose(0, 2, 1, 3).reshape(WIDTH, FFN_DIM)
    down_full = gather(down_proj, 0).transpose(1, 0, 2, 3).reshape(FFN_DIM, WIDTH)

    facts = jnp.stack(
        [flow_times, lengths.astype(F32), 1.0 - audio_drop.astype(F32), 1.0 - text_drop.astype(F32)],
        axis=1,
    )
    facts_all = lax.all_gather(facts, "dp", axis=0, tiled=True)
    sinus = time_features(facts_all[:, 0], TIME_DIM).astype(BF)
    time_embed = dot(sinus, time_proj)
    time_act = jax.nn.silu(time_embed).astype(BF)
    first_utt = (dp_rank - dp_low) * per_group
    act_near = lax.dynamic_slice_in_dim(time_act, first_utt, 2 * per_group, 0)
    mod_cols = dot(act_near, mod_proj)
    modulation = lax.all_gather(mod_cols, "tp", axis=1, tiled=True)
    mod_row = lax.dynamic_slice_in_dim(modulation, utterance - first_utt, 1, 0)
    shift_attn, scale_attn, gate_attn, shift_mlp, scale_mlp, gate_mlp = jnp.split(mod_row, 6, axis=1)
    mine = lax.dynamic_slice_in_dim(facts_all, utterance, 1, 0)
    time_here = mine[0, 0]
    keep_audio = mine[0, 2]
    keep_text = mine[0, 3]
    length = mine[0, 1].astype(jnp.int32)

    mel = swap(mel_frames).astype(F32)
    noise = swap(noise_frames).astype(F32)
    ids = swap(text_ids)
    mask = swap(span_mask)
    out_grad = swap(cotangent).astype(F32)

    keep_cond = (1 - mask).astype(F32)[:, None] * keep_audio
    noisy = (1.0 - time_here) * noise + time_here * mel
    cond = mel * keep_cond
    text_emb = jnp.take(text_table, ids, axis=0).astype(F32) * keep_text
    features = jnp.concatenate([noisy, cond, text_emb], axis=1).astype(BF)
    hidden = dot(features, in_proj)
    norm_a, inv_a = norm_parts(hidden)
    normed_attn = (norm_a * (1.0 + scale_attn) + shift_attn).astype(BF)
    qkv = dot(normed_attn, qkv_full)
    positions = half * local_rows + jnp.arange(local_rows, dtype=jnp.int32)
    cosine, sine = rope_tables(positions)

    def rotate(values):
        return values * cosine + swap_pairs(values) * sine

    def rotate_back(values):
        return values * cosine - swap_pairs(values) * sine

    query = rotate(qkv[:, :WIDTH]).astype(BF)
    own = jnp.concatenate(
        [rotate(qkv[:, WIDTH : 2 * WIDTH]).astype(BF), qkv[:, 2 * WIDTH :].astype(BF)], axis=1
    )
    other = lax.ppermute(own, "dp", sibling)
    info = jnp.stack([length, half * local_rows, (1 - half) * local_rows])
    heads_out, lse = attend(info, query, own, other)
    attn_sum = dot(heads_out, out_full)
    hidden_mid = hidden + gate_attn * attn_sum
    norm_m, inv_m = norm_parts(hidden_mid)
    normed_mlp = (norm_m * (1.0 + scale_mlp) + shift_mlp).astype(BF)
    up_act = dot(normed_mlp, up_full)
    gelu_value, gelu_pull = jax.vjp(lambda inner: jax.nn.gelu(inner, approximate=True), up_act)
    gelu_act = gelu_value.astype(BF)
    mlp_sum = dot(gelu_act, down_full)
    layer_out = swap((hidden_mid + gate_mlp * mlp_sum).astype(BF))

    mlp_grad = (gate_mlp * out_grad).astype(BF)
    down_grad = dot(gelu_act, mlp_grad, 0, 0).astype(BF)
    up_act_grad = gelu_pull(dot(mlp_grad, down_full, 1, 1))[0].astype(BF)
    up_grad = dot(normed_mlp, up_act_grad, 0, 0).astype(BF)
    normed_mlp_grad = dot(up_act_grad, up_full, 1, 1)
    mid_grad = out_grad + norm_back(norm_m, inv_m, scale_mlp, normed_mlp_grad)
    attn_grad = (gate_attn * mid_grad).astype(BF)
    out_proj_grad = dot(heads_out, attn_grad, 0, 0).astype(BF)
    heads_grad = dot(attn_grad, out_full, 1, 1).astype(BF)
    dq, dk_own, dv_own, dk_other, dv_other = attend_back(
        info, query, own, other, heads_grad, heads_out, lse
    )
    dk_in = lax.ppermute(dk_other, "dp", sibling)
    dv_in = lax.ppermute(dv_other, "dp", sibling)
    qkv_act_grad = jnp.concatenate(
        [
            rotate_back(dq).astype(BF),
            rotate_back(dk_own + dk_in.astype(F32)).astype(BF),
            (dv_own + dv_in.astype(F32)).astype(BF),
        ],
        axis=1,
    )
    qkv_grad = dot(normed_attn, qkv_act_grad, 0, 0).astype(BF)
    normed_attn_grad = dot(qkv_act_grad, qkv_full, 1, 1)
    hidden_grad = (mid_grad + norm_back(norm_a, inv_a, scale_attn, normed_attn_grad)).astype(BF)
    in_grad = dot(features, hidden_grad, 0, 0).astype(BF)
    feature_grad = dot(hidden_grad, in_proj, 1, 1)
    mel_grad = swap(
        time_here * feature_grad[:, :MEL_BINS]
        + keep_cond * feature_grad[:, MEL_BINS : 2 * MEL_BINS]
    )
    text_grad = feature_grad[:, 2 * MEL_BINS :].astype(BF) * keep_text.astype(BF)
    one_hot = (ids[:, None] == jnp.arange(VOCABULARY, dtype=jnp.int32)[None, :]).astype(BF)
    table_grad = dot(one_hot, text_grad, 0, 0).astype(BF)

    column_sum = lambda values: jnp.sum(values, axis=0, keepdims=True)
    mod_part = jnp.concatenate(
        [
            column_sum(normed_attn_grad),
            column_sum(normed_attn_grad * norm_a),
            column_sum(attn_sum * mid_grad),
            column_sum(normed_mlp_grad),
            column_sum(normed_mlp_grad * norm_m),
            column_sum(out_grad * mlp_sum),
        ],
        axis=1,
    )
    slot = (jnp.arange(utt_total, dtype=jnp.int32) == utterance).astype(F32)[:, None]
    mod_sums = lax.psum(
        lax.psum_scatter(slot * mod_part, "tp", scatter_dimension=1, tiled=True), "dp"
    ).astype(BF)
    mod_grad = dot(time_act, mod_sums, 0, 0)
    act_grad = lax.psum(dot(mod_sums, mod_proj, 1, 1), "tp")
    embed_grad = jax.vjp(jax.nn.silu, time_embed)[1](act_grad)[0].astype(BF)
    time_rows = TIME_DIM // tp_size
    sinus_share = lax.dynamic_slice_in_dim(sinus, tp_rank * time_rows, time_rows, 1)
    time_grad = dot(sinus_share, embed_grad, 0, 0)

    def reduce(values, axis):
        small = lax.psum_scatter(values, "dp", scatter_dimension=axis + 1, tiled=True)
        piece = lax.psum_scatter(small, "tp", scatter_dimension=0, tiled=True)[0]
        return lax.all_gather(piece, "dp", axis=axis, tiled=True).astype(F32)

    head_cols = WIDTH // tp_size
    unit_cols = FFN_DIM // tp_size
    down_out = reduce(down_grad.reshape(tp_size, unit_cols, WIDTH), 0)
    up_out = reduce(up_grad.reshape(WIDTH, tp_size, unit_cols).transpose(1, 0, 2), 0)
    out_out = reduce(out_proj_grad.reshape(tp_size, head_cols, WIDTH), 0)
    qkv_out = reduce(
        qkv_grad.reshape(WIDTH, 3, tp_size, head_cols).transpose(2, 0, 1, 3), 0
    )
    in_out = reduce(in_grad.reshape(tp_size, in_grad.shape[0] // tp_size, WIDTH), 1)
    table_out = reduce(table_grad.reshape(tp_size, VOCABULARY // tp_size, TEXT_DIM), 0)
    return (
        layer_out, mel_grad, in_out, table_out, time_grad, mod_grad, qkv_out, out_out, up_out, down_out,
    )


def solution(mesh):
    frames = P(("dp", "tp"), None)
    frame = P(("dp", "tp"))
    return jax.shard_map(
        body,
        mesh=mesh,
        in_specs=(
            frames, frames, frame, frame, P("dp"), P("dp"), P("dp"), P("dp"),
            P(), P(), P(), P(None, "tp"), P(None, None, "tp"), P("tp", None), P(None, "tp"),
            P("tp", None), frames,
        ),
        out_specs=(
            frames, frames, P("tp", None), P("tp", None), P("tp", None), P(None, "tp"),
            P(None, None, "tp"), P("tp", None), P(None, "tp"), P("tp", None),
        ),
        check_vma=False,
    )
```

time: 1430 us -> 952 us (0.67)
  waiting for transfers between devices: 759 us -> 452 us
  matrix products: 183 us -> 83 us
  blocking collectives: 155 us -> 86.2 us
  Pallas kernels: 0 us -> 46.7 us
  other arithmetic: 98.3 us -> 62.6 us
  local copies, waits for them, and re-layouts: 196 us -> 181 us
    all_gather x4 -> x7, waiting for transfers between devices: 314 us -> 168 us  [the longest x4 109 us: gather(): lax.all_gather(piece, AXES, axis=0, tiled=False)]
    psum x1, waiting for transfers between devices: 151 us -> 27.3 us  [body(): act_grad = lax.psum(dot(mod_sums, mod_proj, 1, 1), 'tp')]
    dot_general x54 -> x21, matrix products: 183 us -> 83 us  [dot(): lax.dot_general(left, right, (((left_dim,), (right_dim,)), ((), ())), pre...]
    dynamic_update_slice x8 -> x0, local copies, waits for them, and re-layouts: 83.6 us -> none  [body(): lax.map(attend_utt, (query_utt, key_utt, value_utt, lengths))]
    reshape x1 -> x18, local copies, waits for them, and re-layouts: 4.45 us -> 80.4 us  [the longest x8 26.3 us: swap_pairs(): jnp.flip(values.reshape(shape[0], shape[1] // 2, 2), axis=2).reshape(shape)]
    reduce_scatter x5 -> x11, waiting for transfers between devices: 293 us -> 220 us  [the longest x5 108 us: reduce(): lax.psum_scatter(values, 'dp', scatter_dimension=axis + 1, tiled=True)]
    psum x2 -> x1, blocking collectives: 93 us -> 24.1 us  [body(): lax.psum(lax.psum_scatter(slot * mod_part, 'tp', scatter_dimension=1, til...]
    all_gather x0 -> x4, blocking collectives: none -> 48 us  [the longest x3 30.4 us: reduce(): return lax.all_gather(piece, 'dp', axis=axis, tiled=True).astype(F32)]
  transfers between devices with their start and end apart: 12 -> 31, of which waited for: 9 -> 18; matrix products, arithmetic and copies ran while one was open for 8% -> 32% of each run, Pallas kernels for 0% -> 5%
where the time goes in v1:
time: 952 us; the launch traced here: 939 us
  waiting for transfers between devices  452 us (47%)
  local copies, waits for them, and re-layouts  181 us (19%)
  blocking collectives  86.2 us (9%)
  matrix products  83 us (9%)
  other arithmetic  62.6 us (7%)
  Pallas kernels  46.7 us (5%)
  between operations  17.4 us (2%)
  starting transfers between devices  10.1 us (1%)
    all_gather x4, waiting for transfers between devices, gather(): lax.all_gather(piece, AXES, axis=0, tiled=False)  109 us
    reduce_scatter x5, waiting for transfers between devices, reduce(): lax.psum_scatter(values, 'dp', scatter_dimension=axis + 1, tiled=True)  108 us
    reduce_scatter x5, waiting for transfers between devices, reduce(): piece = lax.psum_scatter(small, 'tp', scatter_dimension=0, tiled=True)[0]  89.4 us
    dot_general x21, matrix products, dot(): lax.dot_general(left, right, (((left_dim,), (right_dim,)), ((), ())), pre...  83 us
    all_gather x3, waiting for transfers between devices, reduce(): return lax.all_gather(piece, 'dp', axis=axis, tiled=True).astype(F32)  59.3 us
    rev x4, local copies, waits for them, and re-layouts, swap_pairs(): jnp.flip(values.reshape(shape[0], shape[1] // 2, 2), axis=2).reshape(shape)  43.8 us
    unnamed x23, waiting for transfers between devices  36.4 us
    all_gather x3, blocking collectives, reduce(): return lax.all_gather(piece, 'dp', axis=axis, tiled=True).astype(F32)  30.4 us
  transfers between devices with their start and end apart: 31, of which 18 were waited for; matrix products, arithmetic and copies ran while one was open for 32% of the time, Pallas kernels for 5%

profile of v1, /device:TPU:0, one launch (start us, length us, event | category | flops | bytes accessed | tf_op | source)
XLA Modules:
  0.0 938.8 jit_solution(1274337125404145760)
XLA Ops:
  19.4 17.6 %all-gather.10 = f32[8,2,4]{2,1,0:T(2,128)S(1)} all-gather(f32[1,2,4]{2,1,0:T(2,128)S(1)} %bitcast.172), channel_id=1, replica_groups=mesh['dp'=8,'tp'=4] {'dp'}, dimensions={0}, use_global_device_ids=true | all-gather | bytes 288 | tf_op jit(solution)/shard_map/all_gather | solution.py:226
  40.2 14.1 %all_gather.49 = f32[4,6144]{1,0:T(4,128)S(1)} all-gather(f32[4,1536]{1,0:T(4,128)S(1)} %fusion.68), channel_id=1, replica_groups=mesh['dp'=8,'tp'=4] {'tp'}, dimensions={1}, use_global_device_ids=true | all-gather | bytes 122880 | tf_op jit(solution)/shard_map/all_gather | solution.py:233
  71.5 12.9 %all-gather.19.cloned.1.call-done = bf16[4096,3,256]{2,0,1:T(8,128)(2,1)} async-done(((bf16[128,3,256]{2,0,1:T(8,128)(2,1)}), bf16[4096,3,256]{2,0,1:T(8,128)(2,1)}) %all-gather.19.cloned.1.call-update) | async-done | bytes 6291472 | tf_op jit(solution)/shard_map/all_gather | solution.py:213
  110.5 10.9 %rev.14 = f32[512,512,2]{0,2,1:T(2,128)} reverse(f32[512,512,2]{0,2,1:T(2,128)} %reshape.193), dimensions={2} | reverse | bytes 4194304 | tf_op jit(solution)/shard_map/jit(_flip)/rev | solution.py:49
  134.3 10.9 %rev.13 = f32[512,512,2]{0,2,1:T(2,128)} reverse(f32[512,512,2]{0,2,1:T(2,128)} %reshape.191), dimensions={2} | reverse | bytes 4194304 | tf_op jit(solution)/shard_map/jit(_flip)/rev | solution.py:49
  151.7 11.1 %fusion.29 = (bf16[512,1024]{1,0:T(8,128)(2,1)S(1)}, bf16[512,1024]{1,0:T(8,128)(2,1)}) fusion(f32[512,1024]{1,0:T(8,128)} %copy.71, f32[1024]{0:T(1024)S(1)} %get-tuple-element.72, f32[1024]{0:T(1024)S(1)} %get-tuple-element.71, f32[512]{0:T(512)S(1)} %add_convert_fusion.5, f32[512,3072]{1,0:T(8,128)} %copy-done.11, f32[512,1024]{1,0:T(8,128)} %copy.69), kind=kLoop, calls=%fused_computation.45 | loop fusion | flops 5242880 | bytes 10496000 | tf_op jit(solution)/shard_map/convert_element_type | solution.py:268
  170.3 36.9 %all-gather.25.cloned.1.call-done = bf16[2048,1024]{1,0:T(8,128)(2,1)} async-done(((bf16[64,1024]{1,0:T(8,128)(2,1)}), bf16[2048,1024]{1,0:T(8,128)(2,1)}) %all-gather.25.cloned.1.call-update) | async-done | bytes 4194320 | tf_op jit(solution)/shard_map/all_gather | solution.py:213
  212.0 59.2 %all-gather.23.cloned.1.call-done = bf16[4096,512]{1,0:T(8,128)(2,1)} async-done(((bf16[128,512]{1,0:T(8,128)(2,1)}), bf16[4096,512]{1,0:T(8,128)(2,1)}) %all-gather.23.cloned.1.call-update) | async-done | bytes 4194320 | tf_op jit(solution)/shard_map/all_gather | solution.py:213
  280.1 19.0 %shard_map.240 = (bf16[512,1024]{1,0:T(8,128)(2,1)S(1)}, f32[16,1,512]{2,1,0:T(1,128)S(1)}) custom-call(s32[3]{0:T(128)S(1)} %pad_add_fusion.info_ref, bf16[512,1024]{1,0:T(8,128)(2,1)S(1)} %copy-done.1, bf16[512,2048]{1,0:T(8,128)(2,1)} %pad_maximum_fusion.1.k0_ref.v0_ref, bf16[512,2048]{1,0:T(8,128)(2,1)} %pad_maximum_fusion.1.k0_ref.v0_ref, ...), custom_call_target="tpu_custom_call" | custom-call | tf_op jit(solution)/shard_map/pallas_call | solution.py:145
  340.9 27.7 %shard_map.241 = (f32[512,1024]{1,0:T(8,128)}, f32[512,1024]{1,0:T(8,128)}, f32[512,1024]{1,0:T(8,128)}, bf16[512,1024]{1,0:T(8,128)(2,1)}, bf16[512,1024]{1,0:T(8,128)(2,1)}) custom-call(s32[3]{0:T(128)S(1)} %pad_add_fusion.info_ref, bf16[512,1024]{1,0:T(8,128)(2,1)S(1)} %copy-done.2, bf16[512,2048]{1,0:T(8,128)(2,1)} %pad_maximum_fusion.1.k0_ref.v0_ref, ...), custom_call_target="tpu_custom_call" | custom-call | tf_op jit(solution)/shard_map/pallas_call | solution.py:162
  375.5 11.0 %rev.15 = f32[512,512,2]{0,2,1:T(2,128)} reverse(f32[512,512,2]{0,2,1:T(2,128)} %reshape.201), dimensions={2} | reverse | bytes 4194304 | tf_op jit(solution)/shard_map/jit(_flip)/rev | solution.py:49
  403.6 11.0 %rev.16 = f32[512,512,2]{0,2,1:T(2,128)} reverse(f32[512,512,2]{0,2,1:T(2,128)} %reshape.203), dimensions={2} | reverse | bytes 4194304 | tf_op jit(solution)/shard_map/jit(_flip)/rev | solution.py:49
  424.4 10.0 %fusion.31 = (bf16[512,1024]{1,0:T(8,128)(2,1)S(1)}, bf16[512,1024]{1,0:T(8,128)(2,1)S(1)}) fusion(f32[512,1024]{1,0:T(8,128)S(1)} %copy-done.15, f32[512,1024]{1,0:T(8,128)} %copy.76, f32[1024]{0:T(1024)S(1)} %get-tuple-element.72, f32[1024]{0:T(1024)S(1)} %get-tuple-element.71, f32[512]{0:T(512)S(1)} %add_convert_fusion.5, f32[512,1024]{1,0:T(8,128)} %copy.78, ...), kind=kLoop, calls=%fused_computation.47 | loop fusion | flops 5242880 | bytes 10496000 | tf_op jit(solution)/shard_map/convert_element_type | solution.py:299
  442.2 12.2 %reshape.207 = bf16[1024,3,4,256]{3,2,1,0:T(4,128)(2,1)} reshape(bf16[1024,3072]{1,0:T(8,128)(2,1)} %convolution_convert_fusion) | data formatting | bytes 12582912 | tf_op jit(solution)/shard_map/reshape | solution.py:352
  460.9 9.9 %multiply_reduce_fusion.2 = (f32[1024]{0:T(1024)S(1)}, f32[512]{0:T(512)S(1)}, f32[512]{0:T(512)S(1)}, f32[1024]{0:T(1024)S(1)}, f32[512,1024]{1,0:T(8,128)}) fusion(f32[512,1024]{1,0:T(8,128)} %copy-done.5, f32[512]{0:T(512)S(1)} %add_rsqrt_fusion.1, f32[512]{0:T(512)S(1)} %broadcast_multiply_fusion.6, f32[1024]{0:T(1024)S(1)} %bitcast.158, ...), kind=kOutput, calls=%fused_computation.61 | convolution fusion | flops 3235378176 | bytes 13651968 | tf_op jit(solution)/shard_map/dot_general | solution.py:24
  503.9 17.1 %reduce-scatter.24.cloned.1.call-done = bf16[4,128,3,256]{3,1,2,0:T(8,128)(2,1)} async-done(((bf16[4,1024,3,256]{3,1,2,0:T(8,128)(2,1)}), bf16[4,128,3,256]{3,1,2,0:T(8,128)(2,1)}) %reduce-scatter.24.cloned.1.call-update) | async-done | bytes 786448 | tf_op jit(solution)/shard_map/reduce_scatter | solution.py:342
  521.1 22.9 %reduce-scatter.22.cloned.1.call-done = f32[16,1536]{1,0:T(8,128)} async-done(((f32[16,6144]{1,0:T(8,128)}), f32[16,1536]{1,0:T(8,128)}) %reduce-scatter.22.cloned.1.call-update) | async-done | bytes 98320 | tf_op jit(solution)/shard_map/reduce_scatter | solution.py:332
  544.0 24.1 %psum.14 = bf16[16,1536]{1,0:T(8,128)(2,1)S(1)} all-reduce(f32[16,1536]{1,0:T(8,128)} %reduce-scatter.22.cloned.1.call-done), channel_id=1, replica_groups=mesh['dp'=8,'tp'=4] {'dp'}, use_global_device_ids=true, to_apply=%region_19.20 | all-reduce | flops 24576 | bytes 147456 | tf_op jit(solution)/shard_map/psum | solution.py:331
  569.8 14.8 %reduce-scatter.40.cloned.1.call-done = bf16[128,712]{1,0:T(8,128)(2,1)} async-done(((bf16[1024,712]{1,0:T(8,128)(2,1)}), bf16[128,712]{1,0:T(8,128)(2,1)}) %reduce-scatter.40.cloned.1.call-update) | async-done | bytes 182288
  586.7 42.9 %reduce-scatter.28.cloned.1.call-done = bf16[4,32,1024]{2,1,0:T(8,128)(2,1)} async-done(((bf16[4,256,1024]{2,1,0:T(8,128)(2,1)}), bf16[4,32,1024]{2,1,0:T(8,128)(2,1)}) %reduce-scatter.28.cloned.1.call-update) | async-done | bytes 262160 | tf_op jit(solution)/shard_map/reduce_scatter | solution.py:342
  629.7 47.9 %reduce-scatter.18.cloned.1.call-done = bf16[4,80,512]{2,1,0:T(8,128)(2,1)} async-done(((bf16[4,640,512]{2,1,0:T(8,128)(2,1)}), bf16[4,80,512]{2,1,0:T(8,128)(2,1)}) %reduce-scatter.18.cloned.1.call-update) | async-done | bytes 327696 | tf_op jit(solution)/shard_map/reduce_scatter | solution.py:342
  677.6 23.8 %reduce-scatter.34.cloned.1.call-done = bf16[1,128,512]{2,1,0:T(8,128)(2,1)} async-done(((bf16[4,128,512]{2,1,0:T(8,128)(2,1)}), bf16[1,128,512]{2,1,0:T(8,128)(2,1)}) %reduce-scatter.34.cloned.1.call-update) | async-done | bytes 131088 | tf_op jit(solution)/shard_map/reduce_scatter | solution.py:343
  701.5 22.2 %reduce-scatter.38.cloned.1.call-done = bf16[1,64,1024]{2,1,0:T(8,128)(2,1)} async-done(((bf16[4,64,1024]{2,1,0:T(8,128)(2,1)}), bf16[1,64,1024]{2,1,0:T(8,128)(2,1)}) %reduce-scatter.38.cloned.1.call-update) | async-done | bytes 131088 | tf_op jit(solution)/shard_map/reduce_scatter | solution.py:343
  728.5 24.7 %reduce-scatter.26.cloned.1.call-done = bf16[1,128,3,256]{3,1,2,0:T(8,128)(2,1)} async-done(((bf16[4,128,3,256]{3,1,2,0:T(8,128)(2,1)}), bf16[1,128,3,256]{3,1,2,0:T(8,128)(2,1)}) %reduce-scatter.26.cloned.1.call-update) | async-done | bytes 196624 | tf_op jit(solution)/shard_map/reduce_scatter | solution.py:343
  761.8 27.3 %all-reduce.3.cloned.1.call-done = f32[16,1024]{1,0:T(8,128)} async-done(((f32[16,1024]{1,0:T(8,128)}), f32[16,1024]{1,0:T(8,128)}) %all-reduce.3.cloned.1.call-update) | async-done | bytes 65552 | tf_op jit(solution)/shard_map/psum | solution.py:335
  790.9 20.0 %reduce-scatter.42.cloned.1.call-done = bf16[1,178,128]{2,1,0:T(8,128)(2,1)} async-done(((bf16[4,178,128]{2,1,0:T(8,128)(2,1)}), bf16[1,178,128]{2,1,0:T(8,128)(2,1)}) %reduce-scatter.42.cloned.1.call-update) | async-done | bytes 45584
  810.9 9.8 %all-gather.4 = bf16[1,178,1024]{2,1,0:T(8,128)(2,1)S(1)} all-gather(bf16[1,178,128]{2,1,0:T(8,128)(2,1)} %reduce-scatter.42.cloned.1.call-done), channel_id=6, replica_groups=mesh['dp'=8,'tp'=4] {'dp'}, dimensions={2}, use_global_device_ids=true | all-gather | bytes 410112 | tf_op jit(solution)/shard_map/all_gather | solution.py:344
  831.1 10.1 %all-gather.7 = bf16[1,256,1024]{2,1,0:T(8,128)(2,1)S(1)} all-gather(bf16[1,32,1024]{2,1,0:T(8,128)(2,1)} %reduce-scatter.30.cloned.1.call-done), channel_id=9, replica_groups=mesh['dp'=8,'tp'=4] {'dp'}, dimensions={1}, use_global_device_ids=true | all-gather | bytes 589824 | tf_op jit(solution)/shard_map/all_gather | solution.py:344
  851.5 10.5 %all-gather.5 = bf16[1,640,512]{2,1,0:T(8,128)(2,1)S(1)} all-gather(bf16[1,80,512]{2,1,0:T(8,128)(2,1)} %reduce-scatter.20.cloned.1.call-done), channel_id=7, replica_groups=mesh['dp'=8,'tp'=4] {'dp'}, dimensions={1}, use_global_device_ids=true | all-gather | bytes 737280 | tf_op jit(solution)/shard_map/all_gather | solution.py:344
  863.2 12.0 %all-gather.29.cloned.1.call-done = bf16[1,1024,512]{2,1,0:T(8,128)(2,1)} async-done(((bf16[1,128,512]{2,1,0:T(8,128)(2,1)}), bf16[1,1024,512]{2,1,0:T(8,128)(2,1)}) %all-gather.29.cloned.1.call-update) | async-done | bytes 1048592 | tf_op jit(solution)/shard_map/all_gather | solution.py:344
  878.1 22.4 %all-gather.31.cloned.1.call-done = bf16[1,512,1024]{2,1,0:T(8,128)(2,1)} async-done(((bf16[1,64,1024]{2,1,0:T(8,128)(2,1)}), bf16[1,512,1024]{2,1,0:T(8,128)(2,1)}) %all-gather.31.cloned.1.call-update) | async-done | bytes 1048592 | tf_op jit(solution)/shard_map/all_gather | solution.py:344
  903.3 24.8 %all-gather.27.cloned.1.call-done = bf16[1,1024,3,256]{3,1,2,0:T(8,128)(2,1)} async-done(((bf16[1,128,3,256]{3,1,2,0:T(8,128)(2,1)}), bf16[1,1024,3,256]{3,1,2,0:T(8,128)(2,1)}) %all-gather.27.cloned.1.call-update) | async-done | bytes 1572880 | tf_op jit(solution)/shard_map/all_gather | solution.py:344
  (268 shorter events, 269.6 us)
Async XLA Ops:
  7.2 77.1 %all-gather.19.cloned.1.call-start = ((), (), s32[]{:S(2)}) async-start(), calls=%async_computation.25 | async-start | bytes 6488064 | tf_op jit(solution)/shard_map/all_gather | solution.py:213
  9.0 158.1 %all-gather.21.cloned.1.call-start = ((), (), s32[]{:S(2)}) async-start(), calls=%async_computation.26 | async-start | bytes 2162688 | tf_op jit(solution)/shard_map/all_gather | solution.py:213
  10.6 196.6 %all-gather.25.cloned.1.call-start = ((), (), s32[]{:S(2)}) async-start(), calls=%async_computation.28 | async-start | bytes 4325376 | tf_op jit(solution)/shard_map/all_gather | solution.py:213
  12.2 259.0 %all-gather.23.cloned.1.call-start = ((), (), s32[]{:S(2)}) async-start(), calls=%async_computation.27 | async-start | bytes 4325376 | tf_op jit(solution)/shard_map/all_gather | solution.py:213
  12.3 43.4 %collective-permute-start.3 = (s32[512]{0:T(512)}, s32[512]{0:T(512)S(1)}, u32[]{:S(2)}, u32[]{:S(2)}) collective-permute-start(s32[512]{0:T(512)} %param.19), channel_id=1, source_target_pairs={{1,4},{3,6},{4,1},{6,3},{9,12},{11,14},{12,9},{14,11},{17,20},{19,... | collective-permute-start | bytes 6152 | tf_op jit(solution)/shard_map/ppermute | solution.py:203
  13.0 50.2 %collective-permute-start.2 = (s32[512]{0:T(512)}, s32[512]{0:T(512)S(1)}, u32[]{:S(2)}, u32[]{:S(2)}) collective-permute-start(s32[512]{0:T(512)} %param.20), channel_id=1, source_target_pairs={{1,4},{3,6},{4,1},{6,3},{9,12},{11,14},{12,9},{14,11},{17,20},{19,... | collective-permute-start | bytes 6152 | tf_op jit(solution)/shard_map/ppermute | solution.py:203
  13.6 50.2 %collective-permute-start.1 = (bf16[512,100]{0,1:T(8,128)(2,1)}, bf16[512,100]{0,1:T(8,128)(2,1)S(1)}, u32[]{:S(2)}, u32[]{:S(2)}) collective-permute-start(bf16[512,100]{0,1:T(8,128)(2,1)} %param.17), channel_id=1, source_target_pairs={{1,4},{3,6},{4,1},{6,3},{9,12},{11,14},{12,9},{14,11},{17,20},{19,... | collective-permute-start | bytes 307208 | tf_op jit(solution)/shard_map/ppermute | solution.py:203
  14.3 50.2 %collective-permute-start = (bf16[512,100]{0,1:T(8,128)(2,1)}, bf16[512,100]{0,1:T(8,128)(2,1)}, u32[]{:S(2)}, u32[]{:S(2)}) collective-permute-start(bf16[512,100]{0,1:T(8,128)(2,1)} %param.18), channel_id=1, source_target_pairs={{1,4},{3,6},{4,1},{6,3},{9,12},{11,14},{12,9},{14,11},{17,20},{19,... | collective-permute-start | bytes 307208 | tf_op jit(solution)/shard_map/ppermute | solution.py:203
  17.2 485.4 %reduce-scatter.32.cloned.1.call-start = ((), (), s32[]{:S(2)}) async-start(), calls=%async_computation.21 | async-start | bytes 4718592 | tf_op jit(solution)/shard_map/reduce_scatter | solution.py:342
  164.3 114.5 %collective-permute-start.4 = (bf16[512,2048]{1,0:T(8,128)(2,1)}, bf16[512,2048]{1,0:T(8,128)(2,1)}, u32[]{:S(2)}, u32[]{:S(2)}) collective-permute-start(bf16[512,2048]{1,0:T(8,128)(2,1)} %pad_maximum_fusion.1.k0_ref.v0_ref), channel_id=1, source_target_pairs={{0,4},{4,0},{8,12},{12,8},{16,20},{20,16},{24,28},{28,24},{1,5},{5... | collective-permute-start | bytes 6291464 | tf_op jit(solution)/shard_map/ppermute | solution.py:270
  164.6 140.4 %collective-permute-start.6 = (bf16[512,1024]{1,0:T(8,128)(2,1)}, bf16[512,1024]{1,0:T(8,128)(2,1)}, u32[]{:S(2)}, u32[]{:S(2)}) collective-permute-start(bf16[512,1024]{1,0:T(8,128)(2,1)} %param.33), channel_id=1, source_target_pairs={{1,4},{3,6},{4,1},{6,3},{9,12},{11,14},{12,9},{14,11},{17,20},{19,... | collective-permute-start | bytes 3145736 | tf_op jit(solution)/shard_map/ppermute | solution.py:203
  321.4 181.9 %reduce-scatter.36.cloned.1.call-start = ((), (), s32[]{:S(2)}) async-start(), calls=%async_computation.23 | async-start | bytes 4718592 | tf_op jit(solution)/shard_map/reduce_scatter | solution.py:342
  329.0 192.0 %reduce-scatter.24.cloned.1.call-start = ((), (), s32[]{:S(2)}) async-start(), calls=%async_computation.17 | async-start | bytes 7077888 | tf_op jit(solution)/shard_map/reduce_scatter | solution.py:342
  368.6 24.6 %collective-permute-start.7 = (bf16[512,1024]{1,0:T(8,128)(2,1)}, bf16[512,1024]{1,0:T(8,128)(2,1)}, u32[]{:S(2)}, u32[]{:S(2)}) collective-permute-start(bf16[512,1024]{1,0:T(8,128)(2,1)} %get-tuple-element.21), channel_id=1, source_target_pairs={{0,4},{4,0},{8,12},{12,8},{16,20},{20,16},{24,28},{28,24},{1,5},{5... | collective-permute-start | bytes 3145736 | tf_op jit(solution)/shard_map/ppermute | solution.py:295
  368.9 52.2 %collective-permute-start.8 = (bf16[512,1024]{1,0:T(8,128)(2,1)}, bf16[512,1024]{1,0:T(8,128)(2,1)}, u32[]{:S(2)}, u32[]{:S(2)}) collective-permute-start(bf16[512,1024]{1,0:T(8,128)(2,1)} %get-tuple-element.23), channel_id=1, source_target_pairs={{0,4},{4,0},{8,12},{12,8},{16,20},{20,16},{24,28},{28,24},{1,5},{5... | collective-permute-start | bytes 3145736 | tf_op jit(solution)/shard_map/ppermute | solution.py:296
  460.8 83.2 %reduce-scatter.22.cloned.1.call-start = ((), (), s32[]{:S(2)}) async-start(), calls=%async_computation.15 | async-start | bytes 491520 | tf_op jit(solution)/shard_map/reduce_scatter | solution.py:332
  471.7 112.9 %reduce-scatter.40.cloned.1.call-start = ((), (), s32[]{:S(2)}) async-start(), calls=%async_computation.32 | async-start | bytes 1769472
  491.2 138.4 %reduce-scatter.28.cloned.1.call-start = ((), (), s32[]{:S(2)}) async-start(), calls=%async_computation.19 | async-start | bytes 2359296 | tf_op jit(solution)/shard_map/reduce_scatter | solution.py:342
  495.8 181.8 %reduce-scatter.18.cloned.1.call-start = ((), (), s32[]{:S(2)}) async-start(), calls=%async_computation.13 | async-start | bytes 2949120 | tf_op jit(solution)/shard_map/reduce_scatter | solution.py:342
  502.6 198.9 %reduce-scatter.34.cloned.1.call-start = ((), (), s32[]{:S(2)}) async-start(), calls=%async_computation.22 | async-start | bytes 655360 | tf_op jit(solution)/shard_map/reduce_scatter | solution.py:343
  503.1 220.6 %reduce-scatter.38.cloned.1.call-start = ((), (), s32[]{:S(2)}) async-start(), calls=%async_computation.24 | async-start | bytes 655360 | tf_op jit(solution)/shard_map/reduce_scatter | solution.py:343
  503.9 249.4 %reduce-scatter.26.cloned.1.call-start = ((), (), s32[]{:S(2)}) async-start(), calls=%async_computation.18 | async-start | bytes 983040 | tf_op jit(solution)/shard_map/reduce_scatter | solution.py:343
  521.0 268.0 %all-reduce.3.cloned.1.call-start = ((), (), s32[]{:S(2)}) async-start(), calls=%async_computation.16 | async-start | bytes 131072 | tf_op jit(solution)/shard_map/psum | solution.py:335
  568.1 157.3 %copy-start.40 = (f32[512]{0:T(512)S(1)}, f32[512]{0:T(512)}, u32[]{:S(2)}) copy-start(f32[512]{0:T(512)} %copy-done.39) | copy-start | bytes 6148
  569.7 241.2 %reduce-scatter.42.cloned.1.call-start = ((), (), s32[]{:S(2)}) async-start(), calls=%async_computation.33 | async-start | bytes 235520
  586.7 244.5 %reduce-scatter.30.cloned.1.call-start = ((), (), s32[]{:S(2)}) async-start(), calls=%async_computation.20 | async-start | bytes 327680 | tf_op jit(solution)/shard_map/reduce_scatter | solution.py:343
  629.6 221.9 %reduce-scatter.20.cloned.1.call-start = ((), (), s32[]{:S(2)}) async-start(), calls=%async_computation.14 | async-start | bytes 409600 | tf_op jit(solution)/shard_map/reduce_scatter | solution.py:343
  677.6 197.7 %all-gather.29.cloned.1.call-start = ((), (), s32[]{:S(2)}) async-start(), calls=%async_computation.30 | async-start | bytes 1179648 | tf_op jit(solution)/shard_map/all_gather | solution.py:344
  701.5 199.0 %all-gather.31.cloned.1.call-start = ((), (), s32[]{:S(2)}) async-start(), calls=%async_computation.31 | async-start | bytes 1179648 | tf_op jit(solution)/shard_map/all_gather | solution.py:344
  723.7 204.4 %all-gather.27.cloned.1.call-start = ((), (), s32[]{:S(2)}) async-start(), calls=%async_computation.29 | async-start | bytes 1769472 | tf_op jit(solution)/shard_map/all_gather | solution.py:344
  723.8 29.5 %collective-permute-start.5 = (bf16[512,1024]{1,0:T(8,128)(2,1)}, bf16[512,1024]{1,0:T(8,128)(2,1)}, u32[]{:S(2)}, u32[]{:S(2)}) collective-permute-start(bf16[512,1024]{1,0:T(8,128)(2,1)} %get-tuple-element.44), channel_id=1, source_target_pairs={{1,4},{3,6},{4,1},{6,3},{9,12},{11,14},{12,9},{14,11},{17,20},{19,... | collective-permute-start | bytes 3145736 | tf_op jit(solution)/shard_map/ppermute | solution.py:203
  727.2 28.5 %collective-permute-start.9 = (f32[512,100]{0,1:T(8,128)S(1)}, f32[512,100]{0,1:T(8,128)}, u32[]{:S(2)}, u32[]{:S(2)}) collective-permute-start(f32[512,100]{0,1:T(8,128)S(1)} %fusion.53), channel_id=1, source_target_pairs={{1,4},{3,6},{4,1},{6,3},{9,12},{11,14},{12,9},{14,11},{17,20},{19,... | collective-permute-start | bytes 614408 | tf_op jit(solution)/shard_map/ppermute | solution.py:203
  (46 other events, 373.9 us)
Sparse Core Ops, SparseCore 0:
  11.6 72.6 all-gather.18
  87.2 55.3 all-gather.20
  145.7 61.4 all-gather.24
  210.6 60.6 all-gather.22
  321.5 49.9 reduce-scatter.31
  375.0 51.3 reduce-scatter.35
  460.9 60.0 reduce-scatter.23
  523.4 20.5 reduce-scatter.21
  547.9 36.7 reduce-scatter.39
  588.3 41.2 reduce-scatter.27
  633.8 43.6 reduce-scatter.17
  679.8 21.6 reduce-scatter.33
  703.8 19.8 reduce-scatter.37
  726.0 27.2 reduce-scatter.25
  756.1 32.8 all-reduce.2
  791.8 19.1 reduce-scatter.41
  813.1 17.9 reduce-scatter.29
  833.3 18.1 reduce-scatter.19
  853.4 21.8 all-gather.28
  877.0 23.4 all-gather.30
  902.4 25.6 all-gather.26

commit v2 on v1

v2 whole, which is shorter than its diff:
```python
import functools
import math

import jax
import jax.numpy as jnp
from jax import lax
from jax.experimental import pallas as pl
from jax.experimental.pallas import tpu as pltpu
from jax.sharding import PartitionSpec as P

WIDTH = 1024
HEAD_DIM = 64
MEL_BINS = 100
TEXT_DIM = 512
TIME_DIM = 256
VOCABULARY = 2560
FFN_DIM = 2048
AXES = ("dp", "tp")
BF = jnp.bfloat16
F32 = jnp.float32
MESH = pl.DeviceIdType.MESH
VMEM_LIMIT = 60 * 1024 * 1024
ANY = pl.BlockSpec(memory_space=pl.ANY)


def dot(left, right, left_dim=1, right_dim=0):
    return lax.dot_general(
        left, right, (((left_dim,), (right_dim,)), ((), ())), preferred_element_type=F32
    )


def flip(index, bit):
    return index + bit - 2 * bit * ((index // bit) % 2)


class Place:
    def __init__(self):
        self.dp = lax.axis_index("dp")
        self.tp = lax.axis_index("tp")
        self.core = self.dp % 2
        self.x = (self.dp // 2) % 2
        self.y = self.dp // 4

    def plane(self, bit):
        return (flip(self.dp, bit), self.tp)

    def ahead(self, step):
        return (self.dp, (self.tp + step) % 4)


def greet(devices):
    barrier = pltpu.get_barrier_semaphore()
    for device in devices:
        pl.semaphore_signal(barrier, inc=1, device_id=device, device_id_type=MESH)
    pl.semaphore_wait(barrier, len(devices))


def remote(source, target, sems, index, device):
    return pltpu.make_async_remote_copy(
        src_ref=source,
        dst_ref=target,
        send_sem=sems[0].at[index],
        recv_sem=sems[1].at[index],
        device_id=device,
        device_id_type=MESH,
    )


GATHER_COPIES = 13


class Gather:
    def __init__(self, place, shard, full, scratch, slots=(1, 2, 3), part=slice(None)):
        self.p, self.shard, self.full = place, shard, full
        self.sems, self.held = scratch[:2], (scratch[2:] or [None])[0]
        self.slots, self.part = slots, part

    @staticmethod
    def scratch(shape=None):
        dma = pltpu.SemaphoreType.DMA
        held = [] if shape is None else [pltpu.VMEM(shape, BF)]
        return [dma((GATHER_COPIES,)), dma((GATHER_COPIES,))] + held

    def view(self, *index):
        return self.full.at[(slice(self.slots[0], self.slots[-1] + 1), self.part) + index]

    def copy(self, kind):
        p = self.p
        dp = p.dp
        beside, above = flip(dp, 2), flip(dp, 4)
        across = flip(above, 2)
        if kind[0] == "z":
            step = int(kind[1])
            return remote(
                self.shard.at[self.part, dp],
                self.full.at[step, self.part, dp],
                self.sems,
                step - 1,
                p.ahead(4 - step),
            )
        index, bit, sem = {
            "x": ((dp,), 2, 3),
            "y": ((dp,), 4, 4),
            "c": ((dp,), 1, 5),
            "ya": ((beside, 0), 4, 6),
            "xb": ((above, 1), 2, 7),
            "cx": ((beside,), 1, 8),
            "cy": ((above,), 1, 9),
            "cd": ((across,), 1, 10),
        }[kind]
        return remote(self.view(*index), self.view(*index), self.sems, sem, p.plane(bit))

    def fetch(self):
        return pltpu.make_async_copy(self.shard.at[self.part], self.held, self.sems[0].at[11])

    def keep(self):
        return pltpu.make_async_copy(self.held, self.full.at[0, self.part], self.sems[0].at[12])

    def start(self, *kinds):
        for kind in kinds:
            self.copy(kind).start()

    def arrived(self, *kinds):
        for kind in kinds:
            self.copy(kind).wait_recv()

    def lines(self):
        return ["z%d" % slot for slot in self.slots]

    def stage0(self):
        self.start(*self.lines())
        if self.held is not None:
            self.fetch().start()

    def stage1(self):
        if self.held is not None:
            self.fetch().wait()
            self.keep().start()
        self.arrived(*self.lines())
        self.start("x", "y", "c")

    def stage2(self):
        self.arrived("x")
        self.start("ya", "cx")
        self.arrived("y")
        self.start("xb", "cy")

    def stage3(self):
        self.arrived("ya", "xb")
        self.start("cd")

    def stage4(self):
        self.arrived("c", "cx", "cy", "cd")

    def finish(self):
        if self.held is not None:
            self.keep().wait()
        for kind in self.lines() + ["x", "y", "c", "ya", "xb", "cx", "cy", "cd"]:
            self.copy(kind).wait_send()

    stages = property(lambda s: [s.stage0, s.stage1, s.stage2, s.stage3, s.stage4])


REDUCE_COPIES = 18


def add_into(target, source):
    for index in range(4):
        target[index] = (target[index].astype(F32) + source[index].astype(F32)).astype(BF)


class Reduce:
    @staticmethod
    def scratch(rows, columns, held=False):
        r = rows // 16
        shapes = [
            (4, 2, 2, 2, r, columns),
            (4, 2, r, columns),
            (4, 2, r, columns),
            (4, r, columns),
            (4, r, columns),
            (3, 2, r, columns),
            (2, r, columns),
        ]
        if not held:
            shapes.append((4, 2, 2, 2, r, columns))
        return [
            pltpu.SemaphoreType.DMA((REDUCE_COPIES,)),
            pltpu.SemaphoreType.DMA((REDUCE_COPIES,)),
        ] + [pltpu.VMEM(shape, BF) for shape in shapes]

    def __init__(self, place, grads, out, scratch, held=False, absolute=False):
        self.p, self.grads, self.out, self.held = place, grads, out, held
        self.sems = scratch[:2]
        self.rc, self.rx, self.ry, self.ra, self.rb, self.rz, self.fin = scratch[2:9]
        self.acc = grads.at[:, place.core] if held else scratch[9]
        self.first = place.tp if absolute else 0

    def slot(self, step):
        return (self.first + step) % 4

    def copy(self, kind):
        p, acc, out, fin = self.p, self.acc, self.out, self.fin
        c, x, y = p.core, p.x, p.y
        if kind in ("z1", "z2", "z3"):
            step = int(kind[1])
            return remote(
                acc.at[self.slot(step), x, y], self.rz.at[step - 1], self.sems, 4 + step, p.ahead(step)
            )
        table = {
            "c": (lambda: self.grads.at[:, 1 - c], lambda: self.rc, 1, 0),
            "x": (lambda: acc.at[:, 1 - x, :, 0], lambda: self.rx, 2, 1),
            "y": (lambda: acc.at[:, :, 1 - y, 1], lambda: self.ry, 4, 2),
            "ya": (lambda: acc.at[:, x, 1 - y, 0], lambda: self.ra, 4, 3),
            "xb": (lambda: acc.at[:, 1 - x, y, 1], lambda: self.rb, 2, 4),
            "gx": (lambda: fin, lambda: out.at[c, x, y], 2, 8),
            "gy": (lambda: fin, lambda: out.at[c, x, y], 4, 9),
            "gc": (lambda: fin, lambda: out.at[c, x, y], 1, 10),
            "gya": (lambda: out.at[c, 1 - x, y, 0], lambda: out.at[c, 1 - x, y, 0], 4, 11),
            "gxb": (lambda: out.at[c, x, 1 - y, 1], lambda: out.at[c, x, 1 - y, 1], 2, 12),
            "gcx": (lambda: out.at[c, 1 - x, y], lambda: out.at[c, 1 - x, y], 1, 13),
            "gcy": (lambda: out.at[c, x, 1 - y], lambda: out.at[c, x, 1 - y], 1, 14),
            "gcd": (lambda: out.at[c, 1 - x, 1 - y], lambda: out.at[c, 1 - x, 1 - y], 1, 15),
        }
        source, target, bit, index = table[kind]
        return remote(source(), target(), self.sems, index, p.plane(bit))

    def load(self):
        return pltpu.make_async_copy(self.grads.at[:, self.p.core], self.acc, self.sems[0].at[16])

    def keep(self):
        p = self.p
        return pltpu.make_async_copy(self.fin, self.out.at[p.core, p.x, p.y], self.sems[0].at[17])

    def start(self, *kinds):
        for kind in kinds:
            self.copy(kind).start()

    def arrived(self, *kinds):
        for kind in kinds:
            self.copy(kind).wait_recv()

    def stage0(self):
        self.start("c")
        if not self.held:
            self.load().start()

    def stage1(self):
        if not self.held:
            self.load().wait()
        self.arrived("c")
        add_into(self.acc, self.rc)
        self.start("x", "y")

    def stage2(self):
        p = self.p
        self.arrived("x")
        add_into(self.acc.at[:, p.x, :, 0], self.rx)
        self.start("ya")
        self.arrived("y")
        add_into(self.acc.at[:, :, p.y, 1], self.ry)
        self.start("xb")

    def stage3(self):
        p = self.p
        self.arrived("ya")
        add_into(self.acc.at[:, p.x, p.y, 0], self.ra)
        self.arrived("xb")
        add_into(self.acc.at[:, p.x, p.y, 1], self.rb)
        self.start("z1", "z2", "z3")

    def stage4(self):
        p = self.p
        self.arrived("z1", "z2", "z3")
        total = self.acc[self.slot(0), p.x, p.y].astype(F32)
        for step in range(3):
            total += self.rz[step].astype(F32)
        self.fin[...] = total.astype(BF)
        self.keep().start()
        self.start("gx", "gy", "gc")

    def stage5(self):
        self.arrived("gx")
        self.start("gya", "gcx")
        self.arrived("gy")
        self.start("gxb", "gcy")

    def stage6(self):
        self.arrived("gya", "gxb")
        self.start("gcd")

    def stage7(self):
        self.arrived("gc", "gcx", "gcy", "gcd")
        self.keep().wait()
        for kind in (
            "c", "x", "y", "ya", "xb", "z1", "z2", "z3", "gx", "gy", "gc", "gya", "gxb", "gcx", "gcy", "gcd",
        ):
            self.copy(kind).wait_send()

    stages = property(
        lambda s: [s.stage0, s.stage1, s.stage2, s.stage3, s.stage4, s.stage5, s.stage6, s.stage7]
    )


def pipeline(items, first=0):
    stages = [item.stages[first:] for item in items]
    depth = max(len(held) for held in stages)
    beats = []
    for beat in range(len(items) + depth - 1):
        beats.append(
            [held[beat - j] for j, held in enumerate(stages) if 0 <= beat - j < len(held)][::-1]
        )
    return beats


class Flow:
    def __init__(self):
        self.items = []

    def add(self, item):
        self.items.append(list(item.stages))

    def beat(self):
        for stages in self.items[::-1]:
            if stages:
                stages.pop(0)()
        return any(self.items)


def plane_and_line(place):
    return [place.plane(bit) for bit in (1, 2, 4)] + [place.ahead(step) for step in (1, 2, 3)]


def flip3(index, mask):
    for bit in (1, 2, 4):
        if mask & bit:
            index = flip(index, bit)
    return index


def comm_params(collective_id):
    return pltpu.CompilerParams(
        vmem_limit_bytes=VMEM_LIMIT, collective_id=collective_id, has_side_effects=True
    )


def pieces(shape):
    return tuple(shape[:-2]) + (8, 2, shape[-2] // 16, shape[-1])


def blocks(shape):
    return tuple(shape[:-2]) + (2, 2, 2, 2, shape[-2] // 16, shape[-1])


def head_masks(rows):
    lane = lax.broadcasted_iota(jnp.int32, (rows, 2 * HEAD_DIM), 1)
    return [lane < HEAD_DIM, lane >= HEAD_DIM]


def key_bias(length, start, rows):
    position = lax.broadcasted_iota(jnp.int32, (rows, 1), 0) + start
    return jnp.where(position < length, 0.0, -1e30)


def attend_pair(bias0, bias1, q_ref, k0_ref, v0_ref, k1_ref, v1_ref):
    rows = q_ref.shape[0]
    query = q_ref[...] * jnp.asarray(1.0 / math.sqrt(HEAD_DIM), BF)
    masks = head_masks(rows)
    vt0 = v0_ref[...].T
    vt1 = v1_ref[...].T
    parts, totals = [], []
    for head in range(2):
        masked = jnp.where(masks[head], query, jnp.zeros_like(query))
        s0 = dot(k0_ref[...], masked, 1, 1) + bias0
        s1 = dot(k1_ref[...], masked, 1, 1) + bias1
        peak = jnp.maximum(
            jnp.max(s0, axis=0, keepdims=True), jnp.max(s1, axis=0, keepdims=True)
        )
        e0 = jnp.exp(s0 - peak)
        e1 = jnp.exp(s1 - peak)
        total = jnp.sum(e0, axis=0, keepdims=True) + jnp.sum(e1, axis=0, keepdims=True)
        side = slice(head * HEAD_DIM, (head + 1) * HEAD_DIM)
        acc = dot(vt0[side], e0.astype(BF)) + dot(vt1[side], e1.astype(BF))
        parts.append(acc / total)
        totals.append(peak + jnp.log(total))
    return jnp.concatenate(parts, axis=0).T.astype(BF), totals


def attend_back_pair(info_ref, q_ref, k0_ref, v0_ref, k1_ref, v1_ref, do_ref, o_ref, lse_ref):
    rows = q_ref.shape[0]
    keys = k0_ref.shape[0]
    scale = 1.0 / math.sqrt(HEAD_DIM)
    query = q_ref[...] * jnp.asarray(scale, BF)
    grads = do_ref[...]
    masks = head_masks(rows)
    product = (grads.astype(F32) * o_ref[...].astype(F32)).T
    dq_parts = [None, None]
    results = []
    for which, (k_ref, v_ref) in enumerate(((k0_ref, v0_ref), (k1_ref, v1_ref))):
        bias = key_bias(info_ref[0], info_ref[1 + which], keys)
        kt = k_ref[...].T
        dk = jnp.zeros(k_ref.shape, F32)
        dv = jnp.zeros(v_ref.shape, F32)
        for head in range(2):
            side = slice(head * HEAD_DIM, (head + 1) * HEAD_DIM)
            masked = jnp.where(masks[head], query, jnp.zeros_like(query))
            gmask = jnp.where(masks[head], grads, jnp.zeros_like(grads))
            delta = jnp.sum(product[side], axis=0, keepdims=True)
            scores = dot(k_ref[...], masked, 1, 1) + bias
            probs = jnp.exp(scores - lse_ref[head])
            prob_grad = dot(v_ref[...], gmask, 1, 1)
            score_grad = (probs * (prob_grad - delta)).astype(BF)
            dv += dot(probs.astype(BF), gmask)
            dk += dot(score_grad, masked)
            part = dot(kt[side], score_grad)
            dq_parts[head] = part if which == 0 else dq_parts[head] + part
        results.append((dk, dv))
    return jnp.concatenate(dq_parts, axis=0).T * scale, results


def turn(values, cosine, sine):
    lane = lax.broadcasted_iota(jnp.int32, values.shape, 1)
    width = values.shape[1]
    other = jnp.where(
        lane % 2 == 0, pltpu.roll(values, width - 1, 1), pltpu.roll(values, 1, 1)
    )
    return values * cosine + other * sine


def attend_kernel(info_ref, q, k0, v0, k1, v1, o_ref, lse_ref):
    keys = k0.shape[0]
    biases = [key_bias(info_ref[0], info_ref[1 + which], keys) for which in range(2)]
    o_ref[...], (lse_ref[0], lse_ref[1]) = attend_pair(*biases, q, k0, v0, k1, v1)


def attend(info, query, own, other):
    rows = query.shape[0]
    pairs = WIDTH // (2 * HEAD_DIM)
    tile = pl.BlockSpec((rows, 2 * HEAD_DIM), lambda i: (0, i))
    return pl.pallas_call(
        attend_kernel,
        grid=(pairs,),
        in_specs=[pl.BlockSpec(memory_space=pltpu.SMEM)] + [tile] * 5,
        out_specs=[tile, pl.BlockSpec((2, 1, rows), lambda i: (i, 0, 0))],
        out_shape=[
            jax.ShapeDtypeStruct((rows, WIDTH), BF),
            jax.ShapeDtypeStruct((2 * pairs, 1, rows), F32),
        ],
        compiler_params=pltpu.CompilerParams(vmem_limit_bytes=VMEM_LIMIT),
        name="attend",
    )(info, query, *own, *other)


def attend_back_kernel(reduces, spread, info_ref, q, k0, v0, k1, v1, do, o, lse, cos, sin, *refs):
    grads = refs[:reduces]
    dq_ref, dk_ref, dv_ref, dk_in, dv_in = refs[reduces : reduces + 5]
    outs = refs[reduces + 5 : 2 * reduces + 5]
    sent, send_sems, recv_sems = refs[2 * reduces + 5 : 2 * reduces + 8]
    scratch = refs[2 * reduces + 8 :]
    step = pl.program_id(0)
    last = pl.num_programs(0) - 1
    width = 2 * HEAD_DIM
    sibling = (flip(lax.axis_index("dp"), 1), lax.axis_index("tp"))
    beats = []
    if reduces:
        place = Place()
        items = []
        for j in range(reduces):
            for h in range(grads[j].shape[1]):
                index = 10 * len(items)
                items.append(
                    Reduce(place, grads[j].at[:, h], outs[j].at[h], scratch[index : index + 10])
                )
        beats = pipeline(items)

    @pl.when(step == 0)
    def _():
        greet(plane_and_line(place) if reduces else [sibling])

    for index, beat in enumerate(beats):
        if spread[index] <= 7:

            @pl.when(step == spread[index])
            def _(beat=beat):
                for stage in beat:
                    stage()

    dq, results = attend_back_pair(info_ref, q, k0, v0, k1, v1, do, o, lse)
    dq_ref[...] = turn(dq, cos[...], -sin[...]).astype(BF)
    dk_ref[...], dv_ref[...] = results[0]

    def copies(index):
        columns = pl.ds(pl.multiple_of(index * width, width), width)
        made = []
        for kind, target in ((0, dk_in), (1, dv_in)):
            made.append(
                pltpu.make_async_remote_copy(
                    src_ref=sent.at[kind, index],
                    dst_ref=target.at[:, columns],
                    send_sem=send_sems.at[kind, index],
                    recv_sem=recv_sems.at[kind, index],
                    device_id=sibling,
                    device_id_type=MESH,
                )
            )
        return made

    sent[0, step] = results[1][0].astype(BF)
    sent[1, step] = results[1][1].astype(BF)
    for copy in copies(step):
        copy.start()

    @pl.when(step == last)
    def _():
        for index, beat in enumerate(beats):
            if spread[index] > 7:
                for stage in beat:
                    stage()
        for index in range(WIDTH // width):
            for copy in copies(index):
                copy.wait()


def attend_back(info, query, own, other, heads_grad, outputs, lse, cosine, sine, grads):
    rows = query.shape[0]
    pairs = WIDTH // (2 * HEAD_DIM)
    width = 2 * HEAD_DIM
    tile = pl.BlockSpec((rows, width), lambda i: (0, i))
    fixed = pl.BlockSpec((rows, width), lambda i: (0, 0))
    reduces = len(grads)
    dma = pltpu.SemaphoreType.DMA
    spread = (0, 1, 2, 4, 5, 6, 7) + (8,) * 8
    scratch = []
    for grad in grads:
        for _ in range(grad.shape[1]):
            scratch += Reduce.scratch(*grad.shape[2:])
    outs = pl.pallas_call(
        functools.partial(attend_back_kernel, reduces, spread),
        grid=(pairs,),
        in_specs=[pl.BlockSpec(memory_space=pltpu.SMEM)]
        + [tile] * 7
        + [pl.BlockSpec((2, 1, rows), lambda i: (i, 0, 0)), fixed, fixed]
        + [ANY] * reduces,
        out_specs=[tile] * 3 + [ANY] * 2 + [ANY] * reduces,
        out_shape=[
            jax.ShapeDtypeStruct((rows, WIDTH), BF),
            jax.ShapeDtypeStruct((rows, WIDTH), F32),
            jax.ShapeDtypeStruct((rows, WIDTH), F32),
            jax.ShapeDtypeStruct((rows, WIDTH), BF),
            jax.ShapeDtypeStruct((rows, WIDTH), BF),
        ]
        + [jax.ShapeDtypeStruct(blocks(g.shape[1:]), BF) for g in grads],
        scratch_shapes=[
            pltpu.VMEM((2, pairs, rows, width), BF),
            dma((2, pairs)),
            dma((2, pairs)),
        ]
        + scratch,
        compiler_params=comm_params(3),
        name="attend_back",
    )(
        info, query, *own, *other, heads_grad, outputs, lse, cosine, sine,
        *[g.reshape(blocks(g.shape)) for g in grads],
    )
    return outs[:5], [o.reshape((-1,) + g.shape[3:]) for o, g in zip(outs[5:], grads)]


def forward_kernel(
    mel, noise, extra, facts, mods, cot, qkv, out_w, up_w, down_w, table, mel_w, text_w, cos, sin,
    facts_all, mod_row, mine_out, extra_out, cot_in, qkv_full, out_full, up_full, down_full,
    sum_out, mid_out, normed_out, feats_out, text_out, hidden_out, x_out, q_out, k_out, v_out, ki_out, vi_out, heads_out, lse_out,
    mel_in, noise_in, extra_in, facts_v, mods_v, table_v, mel_wv, text_wv, cos_v, sin_v,
    feats_v, text_v, hidden_v, x_v, q_v, k_v, v_v, ki_v, vi_v, heads_v, lse_v, full_v, outw_v, sum_v, mid_v, normed_v, rows_v, mine_v,
    load_sems, save_sems, fact_sends, fact_recvs, mod_sends, mod_recvs, swap_sends, swap_recvs,
    kv_sends, kv_recvs, *scratch
):
    step = pl.program_id(0)
    last = pl.num_programs(0) - 1
    place = Place()
    dp, tp = place.dp, place.tp
    rows = x_v.shape[0]
    width = full_v.shape[-1]
    partner = (flip(dp, 1), flip(tp, 1))
    sibling = place.plane(1)
    moves = place.core != tp % 2
    stays = jnp.logical_not(moves)
    gathers = [
        Gather(place, qkv, full_v, scratch[2 * j : 2 * j + 2], (j + 1,)) for j in range(3)
    ] + [Gather(place, out_w, outw_v, scratch[6:8])] + [
        Gather(place, shard, full, scratch[8 + 3 * j : 11 + 3 * j], part=j % 2)
        for j, (shard, full) in enumerate(
            ((up_w, up_full), (up_w, up_full), (down_w, down_full), (down_w, down_full))
        )
    ]
    swaps = [
        remote(source, target, (swap_sends, swap_recvs), index, partner)
        for index, (source, target) in enumerate(
            ((mel, mel_in), (noise, noise_in), (extra, extra_in), (cot, cot_in))
        )
    ]
    own_qkv = pltpu.make_async_copy(qkv, full_v.at[0], load_sems.at[0])
    own_out = pltpu.make_async_copy(out_w, outw_v.at[0], load_sems.at[11])
    loads = [
        pltpu.make_async_copy(source, target, load_sems.at[index + 1])
        for index, (source, target) in enumerate(
            (
                (facts, facts_v.at[dp]),
                (mods, mods_v.at[place.core, tp]),
                (table, table_v),
                (mel_w, mel_wv),
                (text_w, text_wv),
                (cos, cos_v),
                (sin, sin_v),
            )
        )
    ]
    frames_own = [
        pltpu.make_async_copy(source, target, load_sems.at[8 + index])
        for index, (source, target) in enumerate(((mel, mel_in), (noise, noise_in), (extra, extra_in)))
    ]
    early_saves = [(feats_v, feats_out), (text_v, text_out), (hidden_v, hidden_out), (x_v, x_out)]
    early_saves += [(facts_v, facts_all), (rows_v, mod_row), (mine_v, mine_out), (extra_in, extra_out)]
    late_saves = [(q_v, q_out), (k_v, k_out), (v_v, v_out), (ki_v, ki_out), (vi_v, vi_out)]
    late_saves += [(full_v, qkv_full), (outw_v, out_full)]
    final_saves = [(heads_v, heads_out), (lse_v, lse_out)]
    final_saves += [(sum_v, sum_out), (mid_v, mid_out), (normed_v, normed_out)]
    saves = [
        pltpu.make_async_copy(source, target, save_sems.at[index])
        for index, (source, target) in enumerate(early_saves + late_saves + final_saves)
    ]
    n_early, n_late = len(early_saves), len(late_saves)

    def kv_copies(rank):
        columns = pl.ds(pl.multiple_of(rank * width, width), width)
        return [
            remote(
                source.at[:, columns], target.at[:, columns],
                (kv_sends.at[kind], kv_recvs.at[kind]), rank, sibling,
            )
            for kind, (source, target) in enumerate(((k_v, ki_v), (v_v, vi_v)))
        ]

    @pl.when(step == 0)
    def _():
        for copy in loads:
            copy.start()
        own_qkv.start()
        own_out.start()
        greet(
            [(flip3(dp, k), tp) for k in range(1, 8)]
            + [place.ahead(step) for step in (1, 2, 3)]
            + [(flip(dp, 1), (tp + step) % 4) for step in (1, 2, 3)]
        )
        fact_copies = [
            remote(facts, facts_v.at[dp], (fact_sends, fact_recvs), k - 1, (flip3(dp, k), tp))
            for k in range(1, 8)
        ]
        mod_copies = []
        for index in range(1, 8):
            target = (flip(dp, 1) if index >= 4 else dp, (tp + index) % 4)
            mod_copies.append(
                remote(mods, mods_v.at[place.core, tp], (mod_sends, mod_recvs), index - 1, target)
            )
        @pl.when(moves)
        def _():
            for copy in swaps[:3]:
                copy.start()

        @pl.when(stays)
        def _():
            for copy in frames_own:
                copy.start()

        for copy in fact_copies + mod_copies:
            copy.start()
        gathers[0].stage0()

        @pl.when(moves)
        def _():
            for copy in swaps[:3]:
                copy.wait()

        @pl.when(stays)
        def _():
            for copy in frames_own:
                copy.wait()

        gathers[1].stage0()
        gathers[0].stage1()
        for copy in loads[:2] + fact_copies + mod_copies:
            copy.wait()
        gathers[2].stage0()
        pick = lambda pair: jnp.where(tp // 2 == 0, pair[0:1], pair[1:2])
        source = dp - place.core + tp % 2
        mine = pick(facts_v[source, 0:8, TIME_DIM : TIME_DIM + 128])
        mine_v[...] = jnp.broadcast_to(mine, mine_v.shape)
        time_here, keep_audio, keep_text = mine[:, 0:1], mine[:, 2:3], mine[:, 3:4]
        chunk = WIDTH // 2
        per_rank = mods_v.shape[-1] // chunk
        for index in range(12):
            lane = index % per_rank * chunk
            rows_v[index // 2 : index // 2 + 1, index % 2 * chunk : (index % 2 + 1) * chunk] = pick(
                mods_v[tp % 2, index // per_rank, 0:8, lane : lane + chunk]
            )
        bins = mel_wv.shape[0] // 2
        extras = extra_in[...].astype(F32)
        mel_f = mel_in[...].astype(F32)
        keep_cond = (1.0 - extras[0:1]) * keep_audio
        feats_v[0:bins] = ((1.0 - time_here) * noise_in[...].astype(F32) + time_here * mel_f).astype(BF)
        feats_v[bins : 2 * bins] = (mel_f * keep_cond).astype(BF)
        ids = (extras[1:2] * 256.0 + extras[2:3]).astype(jnp.int32)
        ids = jnp.broadcast_to(ids, (8, rows)).T[:, 0:1]
        for copy in loads[2:]:
            copy.wait()
        vocabulary = table_v.shape[0]
        span = 512
        for first in range(0, vocabulary, span):
            lane = lax.broadcasted_iota(jnp.int32, (rows, span), 1) + first
            one_hot = (lane == ids).astype(F32).astype(BF)
            term = dot(one_hot, table_v[first : first + span])
            if first == 0:
                hidden_v[:, :TEXT_DIM] = term
            else:
                hidden_v[:, :TEXT_DIM] += term
        text_v[...] = (hidden_v[:, :TEXT_DIM] * keep_text).astype(BF)
        gathers[1].stage1()
        gathers[3].stage0()
        hidden_v[...] = dot(text_v[...], text_wv[...]) + dot(feats_v[...], mel_wv[...], 0, 0)
        gathers[0].stage2()
        block = 128
        for first in range(0, rows, block):
            values = hidden_v[first : first + block]
            normed, _ = norm_parts(values)
            x_v[first : first + block] = (normed * (1.0 + rows_v[1:2]) + rows_v[0:1]).astype(BF)
        gathers[2].stage1()
        gathers[4].stage0()
        gathers[5].stage0()
        for copy in saves[:n_early]:
            copy.start()
        own_qkv.wait()

    g = gathers
    schedule = {
        1: [g[0].stage3, g[1].stage2, g[3].stage1, g[6].stage0, g[7].stage0],
        2: [g[0].stage4, g[2].stage2, g[1].stage3],
        3: [g[3].stage2, g[2].stage3, g[4].stage1],
        4: [g[1].stage4, g[5].stage1, g[3].stage3],
        5: [g[2].stage4, g[4].stage2],
        6: [g[3].stage4, g[6].stage1, g[4].stage3, g[5].stage2],
        7: [g[7].stage1, g[5].stage3],
    }
    for index, stages in schedule.items():

        @pl.when(step == index)
        def _(stages=stages):
            for stage in stages:
                stage()

    @pl.when(step % 2 == 0)
    def _():
        rank = step // 2
        columns = pl.ds(pl.multiple_of(rank * width, width), width)
        x = x_v[...]
        wide = lambda v: jnp.concatenate([v, v], axis=1)
        cosine, sine = wide(cos_v[...]), wide(sin_v[...])
        weight = lambda part: full_v[rank, part].reshape(WIDTH, width)
        k_v[:, columns] = turn(dot(x, weight(1)), cosine, sine).astype(BF)
        v_v[:, columns] = dot(x, weight(2)).astype(BF)
        for copy in kv_copies(rank):
            copy.start()
        q_v[:, columns] = turn(dot(x, weight(0)), cosine, sine).astype(BF)

        @pl.when(jnp.logical_and(step == 4, moves))
        def _():
            swaps[3].start()

        for copy in kv_copies(rank):
            copy.wait()

    @pl.when(step == last - 1)
    def _():
        own_out.wait()
        for copy in saves[n_early : n_early + n_late]:
            copy.start()

    length = mine_v[0:1, 1:2].astype(jnp.int32)
    biases = [
        key_bias(length, place.core * rows, rows),
        key_bias(length, (1 - place.core) * rows, rows),
    ]
    columns = pl.ds(pl.multiple_of(step * 2 * HEAD_DIM, 2 * HEAD_DIM), 2 * HEAD_DIM)
    output, totals = attend_pair(
        *biases, *[ref.at[:, columns] for ref in (q_v, k_v, v_v, ki_v, vi_v)]
    )
    heads_v[:, columns] = output
    lse_v[2 * step], lse_v[2 * step + 1] = totals

    @pl.when(step == last)
    def _():
        g[6].stage2()
        sum_v[...] = dot(heads_v[...], outw_v[...].reshape(WIDTH, WIDTH))
        g[7].stage2()
        block = 128
        for first in range(0, rows, block):
            here = slice(first, first + block)
            values = hidden_v[here] + rows_v[2:3] * sum_v[here]
            mid_v[here] = values
            normed, _ = norm_parts(values)
            normed_v[here] = (normed * (1.0 + rows_v[4:5]) + rows_v[3:4]).astype(BF)
        for copy in saves[n_early + n_late :]:
            copy.start()
        g[6].stage3()
        g[7].stage3()
        g[4].stage4()
        g[5].stage4()
        g[6].stage4()
        g[7].stage4()

        @pl.when(moves)
        def _():
            swaps[3].wait()

        for gather in gathers:
            gather.finish()
        for copy in saves:
            copy.wait()


def forward(mel, noise, extra, facts, mods, cot, qkv, out_w, up_w, down_w, table, mel_w, text_w, cosine, sine):
    rows = cot.shape[0]
    width = qkv.shape[2]
    dma = pltpu.SemaphoreType.DMA
    shape = lambda s, t=BF: jax.ShapeDtypeStruct(s, t)
    full = (4, 3) + pieces(qkv.shape)[1:]
    parted = [
        out_w.reshape((1,) + pieces(out_w.shape)),
        up_w.reshape((2,) + pieces((up_w.shape[0] // 2, up_w.shape[1]))),
        down_w.reshape((2,) + pieces((down_w.shape[0] // 2, down_w.shape[1]))),
    ]
    head_count = WIDTH // HEAD_DIM
    frames = (rows, WIDTH)
    feats = (mel_w.shape[0], rows)
    text = (rows, TEXT_DIM)
    all_facts = (8,) + facts.shape
    lse = (head_count, 1, rows)
    scratch = Gather.scratch() * 4
    for w in parted[1:]:
        scratch += Gather.scratch(w.shape[1:]) * 2
    outs = pl.pallas_call(
        forward_kernel,
        grid=(WIDTH // (2 * HEAD_DIM),),
        in_specs=[ANY] * 15,
        out_specs=[ANY] * 23,
        out_shape=[
            shape(all_facts, F32), shape((8, WIDTH), F32), shape((8, 128), F32), shape(extra.shape),
            shape(cot.shape), shape(full),
        ]
        + [shape((4,) + w.shape) for w in parted]
        + [shape(frames, F32), shape(frames, F32), shape(frames)]
        + [shape(feats), shape(text), shape(frames, F32), shape(frames)]
        + [shape(frames)] * 6
        + [shape(lse, F32)],
        scratch_shapes=[
            *[pltpu.VMEM(v.shape, BF) for v in (mel, noise, extra)], pltpu.VMEM(all_facts, F32),
            pltpu.VMEM((2, 4) + mods.shape, F32), pltpu.VMEM(table.shape, BF),
            pltpu.VMEM(mel_w.shape, BF), pltpu.VMEM(text_w.shape, BF),
            pltpu.VMEM(cosine.shape, F32), pltpu.VMEM(sine.shape, F32),
            pltpu.VMEM(feats, BF), pltpu.VMEM(text, BF), pltpu.VMEM(frames, F32), pltpu.VMEM(frames, BF),
        ]
        + [pltpu.VMEM(frames, BF)] * 6
        + [
            pltpu.VMEM(lse, F32), pltpu.VMEM(full, BF), pltpu.VMEM((4,) + parted[0].shape, BF),
            pltpu.VMEM(frames, F32), pltpu.VMEM(frames, F32), pltpu.VMEM(frames, BF),
            pltpu.VMEM((8, WIDTH), F32), pltpu.VMEM((8, 128), F32),
            dma((12,)), dma((20,)), dma((7,)), dma((7,)), dma((7,)), dma((7,)), dma((4,)), dma((4,)),
            dma((2, 4)), dma((2, 4)),
        ]
        + scratch,
        compiler_params=comm_params(0),
        name="forward",
    )(
        mel, noise, extra, facts, mods, cot, qkv.reshape(pieces(qkv.shape)), *parted, table, mel_w,
        text_w, cosine, sine,
    )
    outs = list(outs)
    outs[5] = outs[5].reshape(4, 3, WIDTH, width)
    outs[6:9] = [f.reshape((4,) + w.shape) for f, w in zip(outs[6:9], (out_w, up_w, down_w))]
    return outs


def qkv_kernel(x_ref, w_ref, cos_ref, sin_ref, q_ref, k_ref, v_ref, ko_ref, vo_ref, sent, send_sems, recv_sems):
    step = pl.program_id(0)
    last = pl.num_programs(0) - 1
    width = q_ref.shape[1]
    sibling = (flip(lax.axis_index("dp"), 1), lax.axis_index("tp"))

    def copies(index):
        columns = pl.ds(pl.multiple_of(index * width, width), width)
        return [
            pltpu.make_async_remote_copy(
                src_ref=sent.at[kind, index],
                dst_ref=target.at[:, columns],
                send_sem=send_sems.at[kind, index],
                recv_sem=recv_sems.at[kind, index],
                device_id=sibling,
                device_id_type=MESH,
            )
            for kind, target in ((0, ko_ref), (1, vo_ref))
        ]

    @pl.when(step == 0)
    def _():
        greet([sibling])

    x = x_ref[...]
    key = turn(dot(x, w_ref[0, 1]), cos_ref[...], sin_ref[...]).astype(BF)
    value = dot(x, w_ref[0, 2]).astype(BF)
    k_ref[...] = key
    v_ref[...] = value
    sent[0, step] = key
    sent[1, step] = value
    for copy in copies(step):
        copy.start()
    q_ref[...] = turn(dot(x, w_ref[0, 0]), cos_ref[...], sin_ref[...]).astype(BF)

    @pl.when(step == last)
    def _():
        for index in range(WIDTH // width):
            for copy in copies(index):
                copy.wait()


def project_qkv(x, weights, cosine, sine):
    rows = x.shape[0]
    ranks, width = weights.shape[0], weights.shape[3]
    tile = pl.BlockSpec((rows, width), lambda r: (0, r))
    whole = lambda shape: pl.BlockSpec(shape, lambda r: (0, 0))
    dma = pltpu.SemaphoreType.DMA
    return pl.pallas_call(
        qkv_kernel,
        grid=(ranks,),
        in_specs=[
            whole(x.shape),
            pl.BlockSpec((1, 3, WIDTH, width), lambda r: (r, 0, 0, 0)),
            whole((rows, width)),
            whole((rows, width)),
        ],
        out_specs=[tile] * 3 + [ANY] * 2,
        out_shape=[jax.ShapeDtypeStruct((rows, WIDTH), BF)] * 5,
        scratch_shapes=[pltpu.VMEM((2, ranks, rows, width), BF), dma((2, ranks)), dma((2, ranks))],
        compiler_params=comm_params(1),
        name="project_qkv",
    )(x, weights, cosine, sine)


def qkv_back_kernel(
    x_ref, w_ref, cos_ref, sin_ref, dq_ref, dk_ref, dv_ref, dki_ref, dvi_ref, grad_ref, dx_ref, xt
):
    step = pl.program_id(0)

    @pl.when(step == 0)
    def _():
        xt[...] = x_ref[...].T

    dq = dq_ref[...]
    dk = turn(dk_ref[...] + dki_ref[...].astype(F32), cos_ref[...], -sin_ref[...]).astype(BF)
    dv = (dv_ref[...] + dvi_ref[...].astype(F32)).astype(BF)
    total = None
    for part, grad in enumerate((dq, dk, dv)):
        grad_ref[0, part] = dot(xt[...], grad).astype(BF)
        term = dot(grad, w_ref[0, part], 1, 1)
        total = term if total is None else total + term

    @pl.when(step == 0)
    def _():
        dx_ref[...] = total

    @pl.when(step > 0)
    def _():
        dx_ref[...] += total


def project_qkv_back(x, weights, cosine, sine, dq, dk, dv, dk_in, dv_in):
    rows = x.shape[0]
    ranks, width = weights.shape[0], weights.shape[3]
    tile = pl.BlockSpec((rows, width), lambda r: (0, r))
    whole = lambda shape: pl.BlockSpec(shape, lambda r: (0, 0))
    wide = pl.BlockSpec((1, 3, WIDTH, width), lambda r: (r, 0, 0, 0))
    return pl.pallas_call(
        qkv_back_kernel,
        grid=(ranks,),
        in_specs=[whole(x.shape), wide, whole((rows, width)), whole((rows, width))] + [tile] * 5,
        out_specs=[wide, whole((rows, WIDTH))],
        out_shape=[
            jax.ShapeDtypeStruct(weights.shape, BF),
            jax.ShapeDtypeStruct((rows, WIDTH), F32),
        ],
        scratch_shapes=[pltpu.VMEM((WIDTH, rows), BF)],
        compiler_params=pltpu.CompilerParams(vmem_limit_bytes=VMEM_LIMIT),
        name="project_qkv_back",
    )(x, weights, cosine, sine, dq, dk, dv, dk_in, dv_in)


def mlp_kernel(x_ref, g_ref, wu_ref, wd_ref, y_ref, dx_ref, du_ref, dd_ref, xt):
    step = pl.program_id(0)

    @pl.when(step == 0)
    def _():
        xt[...] = x_ref[...].T

    up = dot(x_ref[...], wu_ref[0])
    root = math.sqrt(2.0 / math.pi)
    square = up * up
    bent = jnp.tanh(root * (up + 0.044715 * up * square))
    half = 0.5 * (1.0 + bent)
    slope = half + 0.5 * up * (1.0 - bent * bent) * root * (1.0 + 3 * 0.044715 * square)
    act = (up * half).astype(BF)
    grad = g_ref[...]
    up_grad = (dot(grad, wd_ref[0], 1, 1) * slope).astype(BF)
    dd_ref[0] = dot(act, grad, 0, 0).astype(BF)
    du_ref[0] = dot(xt[...], up_grad).astype(BF)
    y = dot(act, wd_ref[0])
    dx = dot(up_grad, wu_ref[0], 1, 1)

    @pl.when(step == 0)
    def _():
        y_ref[...] = y
        dx_ref[...] = dx

    @pl.when(step > 0)
    def _():
        y_ref[...] += y
        dx_ref[...] += dx


def mlp(x, grad, up_full, down_full):
    rows = x.shape[0]
    ranks, _, units = up_full.shape
    whole = pl.BlockSpec((rows, WIDTH), lambda r: (0, 0))
    up_spec = pl.BlockSpec((1, WIDTH, units), lambda r: (r, 0, 0))
    down_spec = pl.BlockSpec((1, units, WIDTH), lambda r: (r, 0, 0))
    return pl.pallas_call(
        mlp_kernel,
        grid=(ranks,),
        in_specs=[whole, whole, up_spec, down_spec],
        out_specs=[whole, whole, up_spec, down_spec],
        out_shape=[
            jax.ShapeDtypeStruct((rows, WIDTH), F32),
            jax.ShapeDtypeStruct((rows, WIDTH), F32),
            jax.ShapeDtypeStruct(up_full.shape, BF),
            jax.ShapeDtypeStruct(down_full.shape, BF),
        ],
        scratch_shapes=[pltpu.VMEM((WIDTH, rows), BF)],
        compiler_params=pltpu.CompilerParams(vmem_limit_bytes=VMEM_LIMIT),
        name="mlp",
    )(x, grad, up_full, down_full)


def tail_kernel(
    info_ref, x_ref, w_ref, cos_ref, sin_ref, dq_ref, dk_ref, dv_ref, dki_ref, dvi_ref,
    value_ref, mid_ref, scale_ref, feat_ref, mel_w_ref, text_w_ref, ids_ref, keep_ref,
    mod_in_ref, proj_ref,
    sums_ref, act_ref, mel_ref, mel_in_ref, qkv_out, misc_out,
    xt, weights, total_ref, hidden_ref, text_ref, qkv_grads, misc_grads,
    mod_ref, line, every, part_ref, load_sems, line_sends, line_recvs, every_sends, every_recvs,
    act_sends, act_recvs, mel_sems, *scratch
):
    place = Place()
    dp, tp = place.dp, place.tp
    partner = (flip(dp, 1), flip(tp, 1))
    moves = place.core != tp % 2
    rows = x_ref.shape[0]
    ranks, width = w_ref.shape[0], w_ref.shape[3]
    loads = [
        pltpu.make_async_copy(w_ref.at[:, part], weights.at[part % 2], load_sems.at[part])
        for part in range(3)
    ]
    loads[0].start()
    loads[1].start()
    greet(
        [(flip3(dp, k), tp) for k in range(1, 8)]
        + [place.ahead(step) for step in (1, 2, 3)]
        + [(flip(dp, 1), flip(tp, 1))]
    )
    size = 9
    items = [
        Reduce(place, qkv_grads.at[part], qkv_out.at[part], scratch[size * part : size * part + size], True)
        for part in range(3)
    ] + [
        Reduce(
            place, misc_grads.at[h], misc_out.at[h],
            scratch[size * (3 + h) : size * (4 + h)], True, True,
        )
        for h in range(2)
    ]
    flow = Flow()
    xt[...] = x_ref[...].T
    for part in range(3):
        loads[part].wait()
        for rank in range(ranks):
            side = slice(rank * width, (rank + 1) * width)
            if part == 0:
                grad = dq_ref[:, side]
            elif part == 1:
                grad = turn(
                    dk_ref[:, side] + dki_ref[:, side].astype(F32), cos_ref[...], -sin_ref[...]
                ).astype(BF)
            else:
                grad = (dv_ref[:, side] + dvi_ref[:, side].astype(F32)).astype(BF)
            qkv_grads[part, rank] = (
                dot(xt[...], grad).astype(BF).reshape(qkv_grads.shape[2:])
            )
            term = dot(grad, weights[part % 2, rank], 1, 1)
            if part == 0 and rank == 0:
                total_ref[...] = term
            else:
                total_ref[...] += term
        if part == 0:
            loads[2].start()
        flow.add(items[part])
        flow.beat()

    normed_grad = total_ref[...]
    normed, inverse = norm_parts(value_ref[...])
    inner = normed_grad * (1.0 + scale_ref[...])
    first = jnp.mean(inner, axis=-1, keepdims=True)
    second = jnp.mean(inner * normed, axis=-1, keepdims=True)
    hidden_ref[...] = (
        mid_ref[...] + inverse * (inner - first - normed * second)
    ).astype(BF)
    chunks = mod_ref.shape[1]
    lanes = mod_ref.shape[2]
    mod_ref[...] = mod_in_ref[...]
    for index, sums in enumerate(
        (jnp.sum(normed_grad, axis=0, keepdims=True), jnp.sum(normed_grad * normed, axis=0, keepdims=True))
    ):
        for chunk in range(WIDTH // lanes):
            row = index * (WIDTH // lanes) + chunk
            mod_ref[row // chunks, row % chunks : row % chunks + 1, :] = sums[
                :, chunk * lanes : (chunk + 1) * lanes
            ]
    line_copies = [
        remote(
            mod_ref.at[(tp + step) % 4], line.at[tp], (line_sends, line_recvs), step - 1, place.ahead(step)
        )
        for step in (1, 2, 3)
    ]
    every_copies = [
        remote(line, every.at[dp], (every_sends, every_recvs), k - 1, (flip3(dp, k), tp))
        for k in range(1, 8)
    ]
    act_copies = [
        remote(part_ref, act_ref.at[tp], (act_sends, act_recvs), step - 1, place.ahead(step))
        for step in (1, 2, 3)
    ]
    for copy in line_copies:
        copy.start()
    line[tp] = mod_ref[tp]
    flow.beat()

    hidden = hidden_ref[...]
    text_ref[...] = dot(hidden, text_w_ref[...], 1, 1).astype(BF) * info_ref[2].astype(BF)
    table_rows = VOCABULARY // ranks
    split = misc_grads.shape[-2] * 16
    block = misc_grads.shape[2:]
    for rank in range(ranks):
        row = lax.broadcasted_iota(jnp.int32, (split, rows), 0) + rank * table_rows
        one_hot = (row == ids_ref[...]).astype(F32).astype(BF)
        misc_grads[0, rank] = dot(one_hot, text_ref[...]).astype(BF).reshape(block)
    flow.add(items[3])
    flow.beat()
    for copy in line_copies:
        copy.wait()
    every[dp] = line[...]
    for copy in every_copies:
        copy.start()
    feat_rows = feat_ref.shape[1] // ranks
    rest = table_rows - split
    for rank in range(ranks):
        row = lax.broadcasted_iota(jnp.int32, (rest, rows), 0) + (rank * table_rows + split)
        one_hot = (row == ids_ref[...]).astype(F32).astype(BF)
        table = dot(one_hot, text_ref[...]).astype(BF)
        share = dot(feat_ref[:, rank * feat_rows : (rank + 1) * feat_rows], hidden, 0, 0).astype(BF)
        misc_grads[1, rank] = jnp.concatenate(
            [table, share[:, :TEXT_DIM], share[:, TEXT_DIM:]], axis=0
        ).reshape(block)
    flow.add(items[4])
    flow.beat()
    mel_part = dot(mel_w_ref[...], hidden, 1, 1)
    bins = mel_part.shape[0] // 2
    mel_ref[...] = info_ref[0] * mel_part[:bins] + keep_ref[...] * mel_part[bins:]
    mel_copy = pltpu.make_async_remote_copy(
        src_ref=mel_ref, dst_ref=mel_in_ref, send_sem=mel_sems.at[0], recv_sem=mel_sems.at[1],
        device_id=partner, device_id_type=MESH,
    )

    @pl.when(moves)
    def _():
        mel_copy.start()

    flow.beat()
    for copy in every_copies:
        copy.wait()
    for pair in range(4):
        sums_ref[pair] = every[2 * pair] + every[2 * pair + 1]
    total = None
    for chunk in range(chunks):
        held = sums_ref[:, :, chunk, :].reshape(16, lanes).astype(BF)
        term = dot(held, proj_ref[:, chunk * lanes : (chunk + 1) * lanes], 1, 1)
        total = term if total is None else total + term
    part_ref[...] = total
    act_ref[tp] = total
    for copy in act_copies:
        copy.start()
    while flow.beat():
        pass
    for copy in act_copies:
        copy.wait()

    @pl.when(moves)
    def _():
        mel_copy.wait()


def tail(
    info, x, weights, cosine, sine, dq, dk, dv, dk_in, dv_in, values, mid_grad, scale,
    feats, mel_w, text_w, ids, keep, mod_part, mod_proj,
):
    rows = x.shape[0]
    ranks, width = weights.shape[0], weights.shape[3]
    table_rows = VOCABULARY // ranks
    misc_rows = table_rows + 2 * (feats.shape[1] // ranks)
    chunks = mod_part.shape[1]
    qkv_block = blocks((WIDTH, width))
    misc_block = blocks((misc_rows // 2, TEXT_DIM))
    dma = pltpu.SemaphoreType.DMA
    vmem = pl.BlockSpec(memory_space=pltpu.VMEM)
    smem = pl.BlockSpec(memory_space=pltpu.SMEM)
    scratch = []
    for _ in range(3):
        scratch += Reduce.scratch(WIDTH, width, True)
    for _ in range(2):
        scratch += Reduce.scratch(misc_rows // 2, TEXT_DIM, True)
    mel_shape = jax.ShapeDtypeStruct((mel_w.shape[0] // 2, rows), F32)
    outs = pl.pallas_call(
        tail_kernel,
        in_specs=[smem, vmem, ANY] + [vmem] * 17,
        out_specs=[vmem] * 3 + [ANY] * 3,
        out_shape=[
            jax.ShapeDtypeStruct((4, 4, chunks, 128), F32),
            jax.ShapeDtypeStruct((4, 16, WIDTH), F32),
            mel_shape,
            mel_shape,
            jax.ShapeDtypeStruct((3,) + qkv_block, BF),
            jax.ShapeDtypeStruct((2,) + misc_block, BF),
        ],
        scratch_shapes=[
            pltpu.VMEM((WIDTH, rows), BF),
            pltpu.VMEM((2, ranks, WIDTH, width), BF),
            pltpu.VMEM((rows, WIDTH), F32),
            pltpu.VMEM((rows, WIDTH), BF),
            pltpu.VMEM((rows, TEXT_DIM), BF),
            pltpu.VMEM((3, ranks) + qkv_block, BF),
            pltpu.VMEM((2, ranks) + misc_block, BF),
            pltpu.VMEM((4, chunks, 128), F32),
            pltpu.VMEM((4, chunks, 128), F32),
            pltpu.VMEM((8, 4, chunks, 128), F32),
            pltpu.VMEM((16, WIDTH), F32),
            dma((3,)), dma((3,)), dma((3,)), dma((7,)), dma((7,)), dma((3,)), dma((3,)), dma((2,)),
        ]
        + scratch,
        compiler_params=comm_params(4),
        name="tail",
    )(
        info, x, weights, cosine, sine, dq, dk, dv, dk_in, dv_in, values, mid_grad, scale,
        feats, mel_w, text_w, ids, keep, mod_part, mod_proj,
    )
    return list(outs[:4]) + [
        outs[4].reshape(3, WIDTH, width), outs[5].reshape(misc_rows, TEXT_DIM)
    ]


def time_features(flow_times, width):
    half_dim = width // 2
    frequency = jnp.exp(
        jnp.arange(half_dim, dtype=F32) * (-math.log(10000.0) / (half_dim - 1))
    )
    angles = 1000.0 * flow_times[:, None] * frequency[None, :]
    return jnp.concatenate([jnp.sin(angles), jnp.cos(angles)], axis=1)


def rope_tables(positions, width):
    lane = jnp.arange(width, dtype=jnp.int32)
    pair = ((lane % HEAD_DIM) // 2).astype(F32)
    inverse = jnp.exp(pair * (-2.0 * math.log(10000.0) / HEAD_DIM))
    angles = positions.astype(F32)[:, None] * inverse[None, :]
    sign = jnp.where(lane % 2 == 0, -1.0, 1.0)
    return jnp.cos(angles), jnp.sin(angles) * sign[None, :]


def norm_parts(values):
    average = jnp.mean(values, axis=-1, keepdims=True)
    centered = values - average
    spread = jnp.mean(centered * centered, axis=-1, keepdims=True)
    inverse = lax.rsqrt(spread + 1e-06)
    return centered * inverse, inverse


def norm_back(normed, inverse, scale_part, grad):
    inner = grad * (1.0 + scale_part)
    first = jnp.mean(inner, axis=-1, keepdims=True)
    second = jnp.mean(inner * normed, axis=-1, keepdims=True)
    return inverse * (inner - first - normed * second)


def body(
    mel_frames, noise_frames, text_ids, span_mask, lengths, audio_drop, text_drop, flow_times,
    in_proj, text_table, time_proj, mod_proj, qkv_proj, out_proj, up_proj, down_proj, cotangent,
):
    dp_size = lax.axis_size("dp")
    tp_size = lax.axis_size("tp")
    dp_rank = lax.axis_index("dp")
    tp_rank = lax.axis_index("tp")
    local_rows = mel_frames.shape[0]
    per_group = flow_times.shape[0]
    utt_total = per_group * dp_size
    dp_low = dp_rank % 2
    tp_low = tp_rank % 2
    stay = dp_low == tp_low
    direct = dp_size == 8 and tp_size == 4
    pairs = []
    for d in range(dp_size):
        for t in range(tp_size):
            if d % 2 != t % 2:
                pairs.append((d * tp_size + t, (d ^ 1) * tp_size + (t ^ 1)))

    def swap(values):
        return jnp.where(stay, values, lax.ppermute(values, AXES, pairs))

    source_dp = dp_rank - dp_low + tp_low
    utterance = source_dp * per_group + tp_rank // 2
    half = dp_low

    def relative(values):
        return jnp.roll(values, -tp_rank, axis=0)

    def gather(shard):
        return relative(lax.all_gather(shard, "tp", axis=0))

    sinus_own = time_features(flow_times, TIME_DIM)
    facts = jnp.concatenate(
        [
            sinus_own,
            flow_times[:, None],
            lengths.astype(F32)[:, None],
            1.0 - audio_drop.astype(F32)[:, None],
            1.0 - text_drop.astype(F32)[:, None],
            jnp.zeros((per_group, 124), F32),
        ],
        axis=1,
    )
    act_own = jax.nn.silu(dot(sinus_own.astype(BF), time_proj)).astype(BF)
    mod_cols = dot(act_own, mod_proj)
    spare = -MEL_BINS % 16
    bins = MEL_BINS + spare
    extra = jnp.stack(
        [span_mask.astype(BF), (text_ids // 256).astype(BF), (text_ids % 256).astype(BF)]
        + [jnp.zeros((local_rows,), BF)] * 13,
        axis=0,
    )
    padded = lambda v: jnp.pad(v, ((0, spare), (0, 0)))
    mel, noise = padded(mel_frames.T), padded(noise_frames.T)
    mel_w = jnp.concatenate(
        [padded(in_proj[:MEL_BINS]), padded(in_proj[MEL_BINS : 2 * MEL_BINS])], axis=0
    )
    text_w = in_proj[2 * MEL_BINS :]
    qkv_shard = qkv_proj.transpose(1, 0, 2)
    positions = half * local_rows + jnp.arange(local_rows, dtype=jnp.int32)
    cosine, sine = rope_tables(positions, WIDTH // tp_size)
    narrow = lambda table: table[:, : 2 * HEAD_DIM]
    if direct:
        pad = ((0, 8 - per_group), (0, 0))
        (
            facts_all, mod_rows, mine, extra, cot, qkv_full, out_full, up_full, down_full,
            attn_sum, hidden_mid, normed_mlp, feats, text_emb, hidden, normed_attn, query, key, value, key_in, value_in, heads_out, lse,
        ) = forward(
            mel, noise, extra, jnp.pad(facts, pad), jnp.pad(mod_cols, pad), cotangent, qkv_shard, out_proj, up_proj,
            down_proj, text_table, mel_w, text_w, narrow(cosine), narrow(sine),
        )
        cot = jnp.where(stay, cotangent, cot)
        facts_all = facts_all[:, :per_group].reshape(utt_total, -1)
        mod_row = mod_rows[:6].reshape(1, 6 * WIDTH)
        mine = mine[:1]
    else:
        facts_all = lax.all_gather(facts, "dp", axis=0, tiled=True)
        near = lax.all_gather(lax.all_gather(mod_cols, "tp", axis=1, tiled=True), "dp", axis=0, tiled=True)
        mod_row = lax.dynamic_slice_in_dim(near, utterance, 1, 0)
        mel, noise, extra, cot = swap(mel), swap(noise), swap(extra), swap(cotangent)
        mine = lax.dynamic_slice_in_dim(facts_all, utterance, 1, 0)[:, TIME_DIM:]
    shift_attn, scale_attn, gate_attn, shift_mlp, scale_mlp, gate_mlp = jnp.split(mod_row, 6, axis=1)
    time_here, length, keep_audio, keep_text = (mine[0, i] for i in range(4))
    length = length.astype(jnp.int32)
    extra = extra[:3].astype(jnp.int32)
    ids = extra[1] * 256 + extra[2]
    out_grad = cot.astype(F32)
    keep_cond = (1.0 - extra[0].astype(F32))[None, :] * keep_audio
    info = jnp.stack([length, half * local_rows, (1 - half) * local_rows])
    if not direct:
        mel, noise = mel.astype(F32), noise.astype(F32)
        noisy = (1.0 - time_here) * noise + time_here * mel
        feats = jnp.concatenate([noisy, mel * keep_cond], axis=0).astype(BF)
        text_emb = (jnp.take(text_table, ids, axis=0).astype(F32) * keep_text).astype(BF)
    features = jnp.concatenate([feats[:MEL_BINS].T, feats[bins : bins + MEL_BINS].T, text_emb], axis=1)
    if not direct:
        qkv_full = gather(qkv_shard)
        hidden = dot(features, in_proj)
        norm_a, inv_a = norm_parts(hidden)
        normed_attn = (norm_a * (1.0 + scale_attn) + shift_attn).astype(BF)
        query, key, value, key_in, value_in = project_qkv(normed_attn, qkv_full, cosine, sine)
        heads_out, lse = attend(info, query, (key, value), (key_in, value_in))
        out_full, up_full, down_full = (gather(shard) for shard in (out_proj, up_proj, down_proj))
    own, other = (key, value), (key_in, value_in)
    out_full = out_full.reshape(WIDTH, WIDTH)
    if not direct:
        attn_sum = dot(heads_out, out_full)
        hidden_mid = hidden + gate_attn * attn_sum
    norm_m, inv_m = norm_parts(hidden_mid)
    if not direct:
        normed_mlp = (norm_m * (1.0 + scale_mlp) + shift_mlp).astype(BF)
    mlp_grad = (gate_mlp * out_grad).astype(BF)
    mlp_sum, normed_mlp_grad, up_grad, down_grad = mlp(normed_mlp, mlp_grad, up_full, down_full)
    layer_out = swap((hidden_mid + gate_mlp * mlp_sum).astype(BF))
    mid_grad = out_grad + norm_back(norm_m, inv_m, scale_mlp, normed_mlp_grad)
    attn_grad = (gate_attn * mid_grad).astype(BF)
    out_grad_w = dot(heads_out, attn_grad, 0, 0).astype(BF).reshape(tp_size, -1, WIDTH)
    heads_grad = dot(attn_grad, out_full, 1, 1).astype(BF)
    halves = lambda v, count: v.reshape((tp_size, count, v.shape[1] // count) + v.shape[2:])
    early = (halves(up_grad, 2), halves(down_grad, 2), halves(out_grad_w, 1))
    (dq, dk, dv, dk_in, dv_in), early_out = attend_back(
        info, query, own, other, heads_grad, heads_out, lse, narrow(cosine), narrow(sine),
        early if direct else (),
    )
    column_sum = lambda values: jnp.sum(values, axis=0, keepdims=True)
    mod_rest = jnp.concatenate(
        [
            column_sum(attn_sum * mid_grad),
            column_sum(normed_mlp_grad),
            column_sum(normed_mlp_grad * norm_m),
            column_sum(out_grad * mlp_sum),
        ],
        axis=1,
    )
    sinus = facts_all[:, :TIME_DIM].astype(BF)
    time_embed = dot(sinus, time_proj)
    time_act = jax.nn.silu(time_embed).astype(BF)
    in_rows = in_proj.shape[0] // tp_size
    in_pad = -in_rows % 64
    table_rows = VOCABULARY // tp_size
    spaced = lambda v, axis: jnp.concatenate(
        [
            jnp.pad(
                lax.slice_in_dim(v, i * in_rows, (i + 1) * in_rows, axis=axis),
                [(0, in_pad if d == axis else 0) for d in range(2)],
            )
            for i in range(tp_size)
        ],
        axis=axis,
    )
    if direct:
        sums, act_parts, mel_own, mel_came, qkv_out, misc_out = tail(
            jnp.stack([time_here, keep_audio, keep_text, keep_text]),
            normed_attn, qkv_full, cosine, sine, dq, dk, dv, dk_in, dv_in, hidden, mid_grad,
            scale_attn, spaced(features, 1), mel_w, text_w, ids[None, :], keep_cond,
            jnp.pad(mod_rest, ((0, 0), (2 * WIDTH, 0))).reshape(tp_size, -1, 128), mod_proj,
        )
        mel_grad = jnp.where(stay, mel_own, mel_came)[:MEL_BINS].T
        order = lambda v: v.reshape((4, 2, 2) + v.shape[2:]).swapaxes(1, 2)
        mod_sums = order(sums).reshape(utt_total, -1).astype(BF)
        act_grad = jnp.sum(act_parts, axis=0)
        act_grad = order(act_grad.reshape(4, 4, WIDTH)).reshape(utt_total, WIDTH)
    else:
        qkv_grad, normed_attn_grad = project_qkv_back(
            normed_attn, qkv_full, cosine, sine, dq, dk, dv, dk_in, dv_in
        )
        hidden_grad = (mid_grad + norm_back(norm_a, inv_a, scale_attn, normed_attn_grad)).astype(BF)
        in_grad = dot(features, hidden_grad, 0, 0).astype(BF)
        mel_part = dot(in_proj[: 2 * MEL_BINS], hidden_grad, 1, 1)
        mel_grad = swap(
            (time_here * mel_part[:MEL_BINS] + keep_cond * mel_part[MEL_BINS:]).T
        )
        text_grad = dot(hidden_grad, in_proj[2 * MEL_BINS :], 1, 1).astype(BF) * keep_text.astype(BF)
        one_hot = (ids[None, :] == jnp.arange(VOCABULARY, dtype=jnp.int32)[:, None]).astype(BF)
        table_grad = dot(one_hot, text_grad).astype(BF).reshape(tp_size, table_rows, TEXT_DIM)
        in_grad = spaced(in_grad, 0).reshape(tp_size, in_rows + in_pad, WIDTH)
        misc = jnp.concatenate(
            [table_grad, in_grad[:, :, :TEXT_DIM], in_grad[:, :, TEXT_DIM:]], axis=1
        )
        mod_part = jnp.concatenate(
            [column_sum(normed_attn_grad), column_sum(normed_attn_grad * norm_a), mod_rest], axis=1
        )
        slot = (jnp.arange(utt_total, dtype=jnp.int32) == utterance).astype(F32)[:, None]
        mod_sums = lax.psum(
            lax.psum_scatter(slot * mod_part, "tp", scatter_dimension=1, tiled=True), "dp"
        ).astype(BF)
        act_grad = lax.psum(dot(mod_sums, mod_proj, 1, 1), "tp")

        def reduce(values):
            return lax.psum(
                lax.psum_scatter(values, "tp", scatter_dimension=0, tiled=True)[0], "dp"
            )

        absolute = lambda values: jnp.roll(values, tp_rank, axis=0)
        early_out = [reduce(absolute(values)) for values in (up_grad, down_grad, out_grad_w)]
        qkv_out = reduce(absolute(qkv_grad))
        misc_out = reduce(misc)
    mod_grad = dot(time_act, mod_sums, 0, 0)
    embed_grad = jax.vjp(jax.nn.silu, time_embed)[1](act_grad)[0].astype(BF)
    time_rows = TIME_DIM // tp_size
    sinus_share = lax.dynamic_slice_in_dim(sinus, tp_rank * time_rows, time_rows, 1)
    time_grad = dot(sinus_share, embed_grad, 0, 0)
    up_out, down_out, out_out = (values.astype(F32) for values in early_out)
    misc_out = misc_out.astype(F32)
    right = table_rows + in_rows + in_pad
    in_out = jnp.concatenate(
        [misc_out[table_rows : table_rows + in_rows], misc_out[right : right + in_rows]], axis=1
    )
    return (
        layer_out, mel_grad, in_out, misc_out[:table_rows], time_grad, mod_grad,
        qkv_out.astype(F32).transpose(1, 0, 2), out_out, up_out, down_out,
    )


def solution(mesh):
    frames = P(("dp", "tp"), None)
    frame = P(("dp", "tp"))
    return jax.shard_map(
        body,
        mesh=mesh,
        in_specs=(
            frames, frames, frame, frame, P("dp"), P("dp"), P("dp"), P("dp"),
            P(), P(), P(), P(None, "tp"), P(None, None, "tp"), P("tp", None), P(None, "tp"),
            P("tp", None), frames,
        ),
        out_specs=(
            frames, frames, P("tp", None), P("tp", None), P("tp", None), P(None, "tp"),
            P(None, None, "tp"), P("tp", None), P(None, "tp"), P("tp", None),
        ),
        check_vma=False,
    )
```

time: 952 us -> 345 us (0.36); the launches traced: 939 us -> 342 us
  waiting for transfers between devices: 452 us -> 0.01 us
  Pallas kernels: 46.7 us -> 271 us
  local copies, waits for them, and re-layouts: 181 us -> 17.9 us
  blocking collectives: 86.2 us -> 0 us
  matrix products: 83 us -> 14 us
  other arithmetic: 62.6 us -> 35 us
  between operations: 17.4 us -> 2.01 us
    pallas_call x2 -> x4, Pallas kernels: 46.7 us -> 271 us  [the longest x1 91.6 us: forward(): pl.pallas_call(forward_kernel, grid=(WIDTH // (2 * HEAD_DIM),), in_specs=...]
    reduce_scatter x11 -> x0, waiting for transfers between devices: 220 us -> none  [the longest x5 108 us: reduce(): lax.psum_scatter(values, 'dp', scatter_dimension=axis + 1, tiled=True)]
    all_gather x7 -> x0, waiting for transfers between devices: 168 us -> none  [the longest x4 109 us: gather(): lax.all_gather(piece, AXES, axis=0, tiled=False)]
    reshape x18 -> x3, local copies, waits for them, and re-layouts: 80.4 us -> 0.66 us  [the longest x1 0.6 us: body(): jnp.pad(mod_rest, ((0, 0), (2 * WIDTH, 0))).reshape(tp_size, -1, 128)]
    dot_general x21 -> x6, matrix products: 83 us -> 14 us  [dot(): lax.dot_general(left, right, (((left_dim,), (right_dim,)), ((), ())), pre...]
    all_gather x5 -> x0, blocking collectives: 62.1 us -> none  [the longest x3 30.4 us: reduce(): return lax.all_gather(piece, 'dp', axis=axis, tiled=True).astype(F32)]
    rev x4 -> x0, local copies, waits for them, and re-layouts: 43.8 us -> none  [swap_pairs(): jnp.flip(values.reshape(shape[0], shape[1] // 2, 2), axis=2).reshape(shape)]
    unnamed x23 -> x0, waiting for transfers between devices: 36.4 us -> none
  transfers between devices with their start and end apart: 31 -> 1, of which waited for: 18 -> 0; matrix products, arithmetic and copies ran while one was open for 32% -> 10% of each run, Pallas kernels for 5% -> 46%
where the time goes in v2:
time: 345 us; the launch traced here: 342 us
  Pallas kernels  271 us (79%)
  other arithmetic  35 us (10%)
  local copies, waits for them, and re-layouts  17.9 us (5%)
  matrix products  14 us (4%)
    pallas_call x1, Pallas kernels, forward(): pl.pallas_call(forward_kernel, grid=(WIDTH // (2 * HEAD_DIM),), in_specs=...  91.6 us
    pallas_call x1, Pallas kernels, tail(): pl.pallas_call(tail_kernel, in_specs=[smem, vmem, ANY] + [vmem] * 17, out...  84.2 us
    pallas_call x1, Pallas kernels, attend_back(): pl.pallas_call(functools.partial(attend_back_kernel, reduces, spread), gr...  73.2 us
    pallas_call x1, Pallas kernels, mlp(): pl.pallas_call(mlp_kernel, grid=(ranks,), in_specs=[whole, whole, up_spec...  21.8 us
    dot_general x6, matrix products, dot(): lax.dot_general(left, right, (((left_dim,), (right_dim,)), ((), ())), pre...  14 us
  transfers between devices with their start and end apart: 1, of which 0 were waited for; matrix products, arithmetic and copies ran while one was open for 10% of the time, Pallas kernels for 46%

profile of v2, /device:TPU:0, one launch (start us, length us, event | category | flops | bytes accessed | tf_op | source)
XLA Modules:
  0.0 341.5 jit_solution(9270240598729365068)
XLA Ops:
  0.8 1.0 slice.92
  1.8 2.3 slice.93.text_w.text_w_ref
  5.4 2.5 fusion.27
  9.9 1.0 slice_select_fusion
  10.9 1.9 fusion.8
  15.3 1.2 stack.38.extra
  16.5 91.6 %forward.1 = (f32[8,8,384]{2,1,0:T(8,128)}, f32[8,1024]{1,0:T(8,128)}, f32[8,128]{1,0:T(8,128)}, bf16[16,512]{1,0:T(8,128)(2,1)}, bf16[512,1024]{1,0:T(8,128)(2,...) custom-call(bf16[112,512]{1,0:T(8,128)(2,1)} %pad.39.mel, ...), custom_call_target="tpu_custom_call" | custom-call | tf_op jit(solution)/shard_map/forward/pallas_call | solution.py:849
  109.7 1.8 reduce_sum.81
  113.0 1.9 fusion
  114.9 21.8 %mlp.1 = (f32[512,1024]{1,0:T(8,128)}, f32[512,1024]{1,0:T(8,128)}, bf16[4,1024,512]{2,1,0:T(8,128)(2,1)}, bf16[4,512,1024]{2,1,0:T(8,128)(2,1)}) custom-call(bf16[512,1024]{1,0:T(8,128)(2,1)} %get-tuple-element.53.x_ref, bf16[512,1024]{1,0:T(8,128)(2,1)} %get-tuple-element.98.g_ref, bf16[4,1024,512]{2,1,0:T(8,128)(2,1)} %bitcast.77, ...), custom_call_target="tpu_custom_call" | custom-call | tf_op jit(solution)/shard_map/mlp/pallas_call | solution.py:1042
  136.7 2.6 multiply_reduce_fusion
  139.3 4.2 %fusion.1 = (f32[1024]{0:T(1024)S(1)}, bf16[512,1024]{1,0:T(8,128)(2,1)}, f32[1024]{0:T(1024)S(1)}, f32[512,1024]{1,0:T(8,128)}) fusion(f32[512,1024]{1,0:T(8,128)} %get-tuple-element.57, bf16[512,1024]{1,0:T(8,128)(2,1)S(1)} %copy-done.6, f32[512,1024]{1,0:T(8,128)S(1)} %copy-done.2, f32[1024]{0:T(1024)S(1)} %bitcast.95, f32[512,1024]{1,0:T(8,128)} %get-tuple-element.81, ...), kind=kLoop, calls=%fused_computation.7 | loop fusion | flops 8386560 | bytes 12607488 | tf_op jit(solution)/shard_map/reduce_sum | solution.py:1443
  143.5 1.8 collective-permute-start
  149.0 1.2 fusion.34.keep_ref
  151.1 0.9 fusion.57
  152.6 3.9 %convolution_convert_fusion.1.do = bf16[512,1024]{1,0:T(8,128)(2,1)} fusion(bf16[1024,1024]{1,0:T(8,128)(2,1)} %bitcast.102, f32[512,1024]{1,0:T(8,128)S(1)} %copy-done.3, f32[1024]{0:T(1024)S(1)} %bitcast.100), kind=kOutput, calls=%fused_computation.21 | convolution fusion | flops 1075314688 | bytes 5246976 | tf_op jit(solution)/shard_map/dot_general | solution.py:27
  156.6 2.6 convolution_convert_fusion
  159.9 2.4 pad_maximum_fusion.2.info_ref
  162.6 1.2 fusion.7.feat_ref
  163.8 73.2 %attend_back.1 = (bf16[512,1024]{1,0:T(8,128)(2,1)}, f32[512,1024]{1,0:T(8,128)}, f32[512,1024]{1,0:T(8,128)}, bf16[512,1024]{1,0:T(8,128)(2,1)}, bf16[512,1024]...) custom-call(s32[3]{0:T(128)} %pad_add_fusion.info_ref, ...), custom_call_target="tpu_custom_call" | custom-call | tf_op jit(solution)/shard_map/attend_back/pallas_call | solution.py:537
  237.0 84.2 %tail.1 = (f32[4,4,12,128]{3,2,1,0:T(8,128)}, f32[4,16,1024]{2,1,0:T(8,128)}, f32[112,512]{1,0:T(8,128)}, f32[112,512]{1,0:T(8,128)}, bf16[3,2,2,2,2,64,256]{6,5...) custom-call(f32[4]{0:T(128)} %pad_maximum_fusion.2.info_ref, bf16[512,1024]{1,0:T(8,128)(2,1)} %get-tuple-element.59.x_ref, ...), custom_call_target="tpu_custom_call" | custom-call | tf_op jit(solution)/shard_map/tail/pallas_call | solution.py:1245
  321.2 1.0 reduce_sum.89
  322.4 1.1 bitcast_convert_fusion.3
  325.1 1.7 bitcast_convert_fusion.1
  326.8 1.6 fusion.14
  328.5 1.0 fusion.21
  329.5 0.9 pad_maximum_fusion
  330.4 1.1 slice.128
  331.6 1.6 bitcast_convert_fusion
  333.2 2.0 convert_bitcast_fusion
  335.3 3.7 %fusion.18 = f32[1024,1536]{1,0:T(8,128)} fusion(bf16[2,8,12,128]{3,2,1,0:T(8,128)(2,1)S(1)} %bitcast.88, f32[16,1024]{1,0:T(8,128)S(1)} %fusion.54), kind=kOutput, calls=%fused_computation.54 | convolution fusion | flops 50413568 | bytes 6406144 | tf_op jit(solution)/shard_map/dot_general | solution.py:27
  339.0 2.3 broadcast_select_fusion
  (129 shorter events, 16.0 us)
Async XLA Ops:
  0.6 4.7 %copy-start = (bf16[256,1024]{1,0:T(8,128)(2,1)S(1)}, bf16[256,1024]{1,0:T(8,128)(2,1)}, u32[]{:S(2)}) copy-start(bf16[256,1024]{1,0:T(8,128)(2,1)} %param.27) | copy-start | bytes 1572868
  0.7 3.4 %copy-start.31 = (s32[2]{0:T(128)S(1)}, s32[2]{0:T(128)}, u32[]{:S(2)}) copy-start(s32[2]{0:T(128)} %param.21) | copy-start | bytes 28
  0.7 3.5 %copy-start.32 = (s32[2]{0:T(128)S(1)}, s32[2]{0:T(128)}, u32[]{:S(2)}) copy-start(s32[2]{0:T(128)} %param.22) | copy-start | bytes 28
  0.7 3.6 %copy-start.33 = (s32[2]{0:T(128)S(1)}, s32[2]{0:T(128)}, u32[]{:S(2)}) copy-start(s32[2]{0:T(128)} %param.23) | copy-start | bytes 28
  0.7 3.7 %copy-start.34 = (f32[2]{0:T(128)S(1)}, f32[2]{0:T(128)}, u32[]{:S(2)}) copy-start(f32[2]{0:T(128)} %param.24) | copy-start | bytes 28
  0.7 3.7 %copy-start.26 = (s32[512]{0:T(512)S(1)}, s32[512]{0:T(512)}, u32[]{:S(2)}) copy-start(s32[512]{0:T(512)} %param.20) | copy-start | bytes 6148
  0.7 3.8 %copy-start.27 = (s32[512]{0:T(512)S(1)}, s32[512]{0:T(512)}, u32[]{:S(2)}) copy-start(s32[512]{0:T(512)} %param.19) | copy-start | bytes 6148
  4.1 4.5 %copy-start.23 = (bf16[512,100]{0,1:T(8,128)(2,1)S(1)}, bf16[512,100]{0,1:T(8,128)(2,1)}, u32[]{:S(2)}) copy-start(bf16[512,100]{0,1:T(8,128)(2,1)} %param.17) | copy-start | bytes 307204
  4.1 5.1 %copy-start.24 = (bf16[512,100]{0,1:T(8,128)(2,1)S(1)}, bf16[512,100]{0,1:T(8,128)(2,1)}, u32[]{:S(2)}) copy-start(bf16[512,100]{0,1:T(8,128)(2,1)} %param.18) | copy-start | bytes 307204
  5.4 4.5 %copy-start.30 = (pred[112]{0:T(512)(128)(4,1)S(1)}, pred[112]{0:T(512)(128)(4,1)}, u32[]{:S(2)}) copy-start(pred[112]{0:T(512)(128)(4,1)} %constant.120.clone.1) | copy-start | bytes 340
  12.8 95.3 %copy-start.7 = (f32[512,256]{1,0:T(8,128)}, f32[512,256]{1,0:T(8,128)S(1)}, u32[]{:S(2)}) copy-start(f32[512,256]{1,0:T(8,128)S(1)} %get-tuple-element.120.sin_ref) | copy-start | bytes 1572868
  108.1 3.4 copy-start.2
  136.6 2.6 copy-start.4
  136.7 2.6 copy-start.6
  139.3 7.1 %copy-start.28 = (f32[8,128]{1,0:T(8,128)S(1)}, f32[8,128]{1,0:T(8,128)}, u32[]{:S(2)}) copy-start(f32[8,128]{1,0:T(8,128)} %get-tuple-element.58) | copy-start | bytes 12292
  139.3 10.9 %copy-start.20 = (bf16[224,512]{1,0:T(8,128)(2,1)S(1)}, bf16[224,512]{1,0:T(8,128)(2,1)}, u32[]{:S(2)}) copy-start(bf16[224,512]{1,0:T(8,128)(2,1)} %get-tuple-element.78) | copy-start | bytes 688132
  139.3 11.7 %copy-start.9 = (bf16[512,512]{1,0:T(8,128)(2,1)S(1)}, bf16[512,512]{1,0:T(8,128)(2,1)}, u32[]{:S(2)}) copy-start(bf16[512,512]{1,0:T(8,128)(2,1)} %get-tuple-element.79) | copy-start | bytes 1572868
  143.5 9.1 %copy-start.3 = (f32[512,1024]{1,0:T(8,128)S(1)}, f32[512,1024]{1,0:T(8,128)}, u32[]{:S(2)}) copy-start(f32[512,1024]{1,0:T(8,128)} %get-tuple-element.105.mid_ref) | copy-start | bytes 6291460
  143.5 195.5 %collective-permute-start = (bf16[512,1024]{1,0:T(8,128)(2,1)}, bf16[512,1024]{1,0:T(8,128)(2,1)}, u32[]{:S(2)}, u32[]{:S(2)}) collective-permute-start(bf16[512,1024]{1,0:T(8,128)(2,1)} %get-tuple-element.103), channel_id=1, source_target_pairs={{1,4},{3,6},{4,1},{6,3},{9,12},{11,14},{12,9},{14,11},{17,20},{19,... | collective-permute-start | bytes 3145736 | tf_op jit(solution)/shard_map/ppermute | solution.py:1338
  146.2 10.3 %copy-start.25 = (bf16[16,384]{1,0:T(8,128)(2,1)}, bf16[16,384]{1,0:T(8,128)(2,1)S(1)}, u32[]{:S(2)}) copy-start(bf16[16,384]{1,0:T(8,128)(2,1)S(1)} %reshape.157) | copy-start | bytes 36868
  152.6 3.9 %copy-start.16 = (bf16[512,1024]{1,0:T(8,128)(2,1)S(1)}, bf16[512,1024]{1,0:T(8,128)(2,1)}, u32[]{:S(2)}) copy-start(bf16[512,1024]{1,0:T(8,128)(2,1)} %get-tuple-element.68.o) | copy-start | bytes 3145732
  156.6 5.7 %copy-start.18 = (bf16[512,100]{1,0:T(8,128)(2,1)S(1)}, bf16[512,100]{1,0:T(8,128)(2,1)}, u32[]{:S(2)}) copy-start(bf16[512,100]{1,0:T(8,128)(2,1)} %get-tuple-element.108) | copy-start | bytes 307204
  156.6 5.7 %copy-start.19 = (bf16[512,100]{1,0:T(8,128)(2,1)S(1)}, bf16[512,100]{1,0:T(8,128)(2,1)}, u32[]{:S(2)}) copy-start(bf16[512,100]{1,0:T(8,128)(2,1)} %get-tuple-element.109) | copy-start | bytes 307204
  156.6 5.7 %copy-start.29 = (pred[192]{0:T(512)(128)(4,1)S(1)}, pred[192]{0:T(512)(128)(4,1)}, u32[]{:S(2)}) copy-start(pred[192]{0:T(512)(128)(4,1)} %constant.128.clone.1) | copy-start | bytes 580
  156.6 6.0 %copy-start.15 = (bf16[512,178]{1,0:T(8,128)(2,1)S(1)}, bf16[512,178]{1,0:T(8,128)(2,1)}, u32[]{:S(2)}) copy-start(bf16[512,178]{1,0:T(8,128)(2,1)} %get-tuple-element.107) | copy-start | bytes 546820
  237.0 85.3 %copy-start.17 = (bf16[1,2,2,2,2,16,1024]{6,5,4,3,2,1,0:T(8,128)(2,1)S(1)}, bf16[1,2,2,2,2,16,1024]{6,5,4,3,2,1,0:T(8,128)(2,1)}, u32[]{:S(2)}) copy-start(bf16[1,2,2,2,2,16,1024]{6,5,4,3,2,1,0:T(8,128)(2,1)} %get-tuple-element.89) | copy-start | bytes 1572868
  324.3 2.5 copy-start.21
  324.3 4.1 %slice-start = ((bf16[16,384]{1,0:T(8,128)(2,1)}), bf16[16,256]{1,0:T(8,128)(2,1)S(1)}, s32[]{:S(2)}) async-start(bf16[16,384]{1,0:T(8,128)(2,1)} %copy-done.25), calls=%async_computation | async-start | bytes 16384 | tf_op jit(solution)/shard_map/slice | solution.py:1453
  329.5 2.1 copy-start.22
  329.5 2.1 copy-start.11
  331.5 1.7 copy-start.10
  335.3 6.0 %copy-start.1 = (bf16[256,1024]{1,0:T(8,128)(2,1)S(1)}, bf16[256,1024]{1,0:T(8,128)(2,1)}, u32[]{:S(2)}) copy-start(bf16[256,1024]{1,0:T(8,128)(2,1)} %param.27) | copy-start | bytes 1572868
  (5 other events, 6.4 us)

commit v3 on v2

--- a/solution.py
+++ b/solution.py
@@ -171,7 +171,7 @@
 
 class Reduce:
     @staticmethod
-    def scratch(rows, columns, held=False):
+    def scratch(rows, columns):
         r = rows // 16
         shapes = [
             (4, 2, 2, 2, r, columns),
@@ -182,18 +182,16 @@
             (3, 2, r, columns),
             (2, r, columns),
         ]
-        if not held:
-            shapes.append((4, 2, 2, 2, r, columns))
         return [
             pltpu.SemaphoreType.DMA((REDUCE_COPIES,)),
             pltpu.SemaphoreType.DMA((REDUCE_COPIES,)),
         ] + [pltpu.VMEM(shape, BF) for shape in shapes]
 
-    def __init__(self, place, grads, out, scratch, held=False, absolute=False):
-        self.p, self.grads, self.out, self.held = place, grads, out, held
+    def __init__(self, place, grads, out, scratch, buffer=None, absolute=False):
+        self.p, self.grads, self.out, self.buffer = place, grads, out, buffer
         self.sems = scratch[:2]
         self.rc, self.rx, self.ry, self.ra, self.rb, self.rz, self.fin = scratch[2:9]
-        self.acc = grads.at[:, place.core] if held else scratch[9]
+        self.acc = grads.at[:, place.core] if buffer is None else self.rc
         self.first = place.tp if absolute else 0
 
     def slot(self, step):
@@ -226,7 +224,7 @@
         return remote(source(), target(), self.sems, index, p.plane(bit))
 
     def load(self):
-        return pltpu.make_async_copy(self.grads.at[:, self.p.core], self.acc, self.sems[0].at[16])
+        return pltpu.make_async_copy(self.grads.at[:, self.p.core], self.buffer, self.sems[0].at[16])
 
     def keep(self):
         p = self.p
@@ -242,14 +240,16 @@
 
     def stage0(self):
         self.start("c")
-        if not self.held:
+        if self.buffer is not None:
             self.load().start()
 
     def stage1(self):
-        if not self.held:
+        self.arrived("c")
+        if self.buffer is None:
+            add_into(self.acc, self.rc)
+        else:
             self.load().wait()
-        self.arrived("c")
-        add_into(self.acc, self.rc)
+            add_into(self.rc, self.buffer)
         self.start("x", "y")
 
     def stage2(self):
@@ -313,17 +313,26 @@
     return beats
 
 
+LAGS = (0, 1, 4, 7, 9, 12, 14, 15)
+JOINS = (0, 1, 3, 5, 7)
+
+
 class Flow:
     def __init__(self):
         self.items = []
+        self.now = 0
 
     def add(self, item):
-        self.items.append(list(item.stages))
+        self.items.append([(self.now + lag, stage) for lag, stage in zip(LAGS, item.stages)])
+
+    def take(self):
+        due = [held.pop(0)[1] for held in self.items[::-1] if held and held[0][0] <= self.now]
+        self.now += 1
+        return due
 
     def beat(self):
-        for stages in self.items[::-1]:
-            if stages:
-                stages.pop(0)()
+        for stage in self.take():
+            stage()
         return any(self.items)
 
 
@@ -386,36 +395,39 @@
     return jnp.concatenate(parts, axis=0).T.astype(BF), totals
 
 
-def attend_back_pair(info_ref, q_ref, k0_ref, v0_ref, k1_ref, v1_ref, do_ref, o_ref, lse_ref):
+def attend_back_pair(biases, q_ref, k0_ref, v0_ref, k1_ref, v1_ref, do_ref, o_ref, lse_ref):
     rows = q_ref.shape[0]
     keys = k0_ref.shape[0]
+    width = 2 * HEAD_DIM
     scale = 1.0 / math.sqrt(HEAD_DIM)
     query = q_ref[...] * jnp.asarray(scale, BF)
     grads = do_ref[...]
-    masks = head_masks(rows)
     product = (grads.astype(F32) * o_ref[...].astype(F32)).T
-    dq_parts = [None, None]
-    results = []
-    for which, (k_ref, v_ref) in enumerate(((k0_ref, v0_ref), (k1_ref, v1_ref))):
-        bias = key_bias(info_ref[0], info_ref[1 + which], keys)
-        kt = k_ref[...].T
-        dk = jnp.zeros(k_ref.shape, F32)
-        dv = jnp.zeros(v_ref.shape, F32)
-        for head in range(2):
-            side = slice(head * HEAD_DIM, (head + 1) * HEAD_DIM)
-            masked = jnp.where(masks[head], query, jnp.zeros_like(query))
-            gmask = jnp.where(masks[head], grads, jnp.zeros_like(grads))
-            delta = jnp.sum(product[side], axis=0, keepdims=True)
-            scores = dot(k_ref[...], masked, 1, 1) + bias
-            probs = jnp.exp(scores - lse_ref[head])
+    sides = ((k0_ref, v0_ref), (k1_ref, v1_ref))
+    turned = [k_ref[...].T for k_ref, _ in sides]
+
+    def one_head(head, carry):
+        dq, sums = carry[0], list(carry[1:])
+        lane = lax.broadcasted_iota(jnp.int32, (rows, width), 1) // HEAD_DIM
+        line = lax.broadcasted_iota(jnp.int32, (width, 1), 0) // HEAD_DIM
+        masked = jnp.where(lane == head, query, jnp.zeros_like(query))
+        gmask = jnp.where(lane == head, grads, jnp.zeros_like(grads))
+        delta = jnp.sum(jnp.where(line == head, product, 0.0), axis=0, keepdims=True)
+        total = lse_ref[head]
+        for which, (k_ref, v_ref) in enumerate(sides):
+            scores = dot(k_ref[...], masked, 1, 1) + biases[which]
+            probs = jnp.exp(scores - total)
             prob_grad = dot(v_ref[...], gmask, 1, 1)
             score_grad = (probs * (prob_grad - delta)).astype(BF)
-            dv += dot(probs.astype(BF), gmask)
-            dk += dot(score_grad, masked)
-            part = dot(kt[side], score_grad)
-            dq_parts[head] = part if which == 0 else dq_parts[head] + part
-        results.append((dk, dv))
-    return jnp.concatenate(dq_parts, axis=0).T * scale, results
+            sums[2 * which] += dot(score_grad, masked)
+            sums[2 * which + 1] += dot(probs.astype(BF), gmask)
+            kt = jnp.where(line == head, turned[which].astype(F32), 0.0).astype(BF)
+            dq += dot(kt, score_grad)
+        return (dq, *sums)
+
+    start = (jnp.zeros((width, rows), F32),) + (jnp.zeros((keys, width), F32),) * 4
+    dq, *sums = lax.fori_loop(0, 2, one_head, start)
+    return dq.T * scale, [sums[:2], sums[2:]]
 
 
 def turn(values, cosine, sine):
@@ -451,60 +463,40 @@
     )(info, query, *own, *other)
 
 
-def attend_back_kernel(reduces, spread, info_ref, q, k0, v0, k1, v1, do, o, lse, cos, sin, *refs):
-    grads = refs[:reduces]
-    dq_ref, dk_ref, dv_ref, dk_in, dv_in = refs[reduces : reduces + 5]
-    outs = refs[reduces + 5 : 2 * reduces + 5]
-    sent, send_sems, recv_sems = refs[2 * reduces + 5 : 2 * reduces + 8]
-    scratch = refs[2 * reduces + 8 :]
+def sibling_copies(sent, targets, sems, index, width, slots):
+    columns = pl.ds(pl.multiple_of(index * width, width), width)
+    return [
+        pltpu.make_async_remote_copy(
+            src_ref=sent.at[kind, index % slots],
+            dst_ref=target.at[:, columns],
+            send_sem=sems[0].at[kind, index],
+            recv_sem=sems[1].at[kind, index],
+            device_id=(flip(lax.axis_index("dp"), 1), lax.axis_index("tp")),
+            device_id_type=MESH,
+        )
+        for kind, target in enumerate(targets)
+    ]
+
+
+def attend_back_kernel(
+    info_ref, q, k0, v0, k1, v1, do, o, lse, cos, sin,
+    dq_ref, dk_ref, dv_ref, dk_in, dv_in, sent, *sems
+):
     step = pl.program_id(0)
     last = pl.num_programs(0) - 1
     width = 2 * HEAD_DIM
-    sibling = (flip(lax.axis_index("dp"), 1), lax.axis_index("tp"))
-    beats = []
-    if reduces:
-        place = Place()
-        items = []
-        for j in range(reduces):
-            for h in range(grads[j].shape[1]):
-                index = 10 * len(items)
-                items.append(
-                    Reduce(place, grads[j].at[:, h], outs[j].at[h], scratch[index : index + 10])
-                )
-        beats = pipeline(items)
+    steps = WIDTH // width
+    copies = lambda index: sibling_copies(sent, (dk_in, dv_in), sems, index, width, steps)
 
     @pl.when(step == 0)
     def _():
-        greet(plane_and_line(place) if reduces else [sibling])
-
-    for index, beat in enumerate(beats):
-        if spread[index] <= 7:
-
-            @pl.when(step == spread[index])
-            def _(beat=beat):
-                for stage in beat:
-                    stage()
-
-    dq, results = attend_back_pair(info_ref, q, k0, v0, k1, v1, do, o, lse)
+        greet([(flip(lax.axis_index("dp"), 1), lax.axis_index("tp"))])
+
+    keys = k0.shape[0]
+    biases = [key_bias(info_ref[0], info_ref[1 + which], keys) for which in range(2)]
+    dq, results = attend_back_pair(biases, q, k0, v0, k1, v1, do, o, lse)
     dq_ref[...] = turn(dq, cos[...], -sin[...]).astype(BF)
     dk_ref[...], dv_ref[...] = results[0]
-
-    def copies(index):
-        columns = pl.ds(pl.multiple_of(index * width, width), width)
-        made = []
-        for kind, target in ((0, dk_in), (1, dv_in)):
-            made.append(
-                pltpu.make_async_remote_copy(
-                    src_ref=sent.at[kind, index],
-                    dst_ref=target.at[:, columns],
-                    send_sem=send_sems.at[kind, index],
-                    recv_sem=recv_sems.at[kind, index],
-                    device_id=sibling,
-                    device_id_type=MESH,
-                )
-            )
-        return made
-
     sent[0, step] = results[1][0].astype(BF)
     sent[1, step] = results[1][1].astype(BF)
     for copy in copies(step):
@@ -512,57 +504,40 @@
 
     @pl.when(step == last)
     def _():
-        for index, beat in enumerate(beats):
-            if spread[index] > 7:
-                for stage in beat:
-                    stage()
-        for index in range(WIDTH // width):
+        for index in range(steps):
             for copy in copies(index):
                 copy.wait()
 
 
-def attend_back(info, query, own, other, heads_grad, outputs, lse, cosine, sine, grads):
+def attend_back(info, query, own, other, heads_grad, outputs, lse, cosine, sine):
     rows = query.shape[0]
     pairs = WIDTH // (2 * HEAD_DIM)
     width = 2 * HEAD_DIM
     tile = pl.BlockSpec((rows, width), lambda i: (0, i))
     fixed = pl.BlockSpec((rows, width), lambda i: (0, 0))
-    reduces = len(grads)
     dma = pltpu.SemaphoreType.DMA
-    spread = (0, 1, 2, 4, 5, 6, 7) + (8,) * 8
-    scratch = []
-    for grad in grads:
-        for _ in range(grad.shape[1]):
-            scratch += Reduce.scratch(*grad.shape[2:])
-    outs = pl.pallas_call(
-        functools.partial(attend_back_kernel, reduces, spread),
+    return pl.pallas_call(
+        attend_back_kernel,
         grid=(pairs,),
         in_specs=[pl.BlockSpec(memory_space=pltpu.SMEM)]
         + [tile] * 7
-        + [pl.BlockSpec((2, 1, rows), lambda i: (i, 0, 0)), fixed, fixed]
-        + [ANY] * reduces,
-        out_specs=[tile] * 3 + [ANY] * 2 + [ANY] * reduces,
+        + [pl.BlockSpec((2, 1, rows), lambda i: (i, 0, 0)), fixed, fixed],
+        out_specs=[tile] * 3 + [ANY] * 2,
         out_shape=[
             jax.ShapeDtypeStruct((rows, WIDTH), BF),
             jax.ShapeDtypeStruct((rows, WIDTH), F32),
             jax.ShapeDtypeStruct((rows, WIDTH), F32),
             jax.ShapeDtypeStruct((rows, WIDTH), BF),
             jax.ShapeDtypeStruct((rows, WIDTH), BF),
-        ]
-        + [jax.ShapeDtypeStruct(blocks(g.shape[1:]), BF) for g in grads],
+        ],
         scratch_shapes=[
             pltpu.VMEM((2, pairs, rows, width), BF),
             dma((2, pairs)),
             dma((2, pairs)),
-        ]
-        + scratch,
+        ],
         compiler_params=comm_params(3),
         name="attend_back",
-    )(
-        info, query, *own, *other, heads_grad, outputs, lse, cosine, sine,
-        *[g.reshape(blocks(g.shape)) for g in grads],
-    )
-    return outs[:5], [o.reshape((-1,) + g.shape[3:]) for o, g in zip(outs[5:], grads)]
+    )(info, query, *own, *other, heads_grad, outputs, lse, cosine, sine)
 
 
 def forward_kernel(
@@ -1001,12 +976,18 @@
     )(x, weights, cosine, sine, dq, dk, dv, dk_in, dv_in)
 
 
-def mlp_kernel(x_ref, g_ref, wu_ref, wd_ref, y_ref, dx_ref, du_ref, dd_ref, xt):
+def mlp_kernel(
+    x_ref, cot_ref, row_ref, mid_ref, sum_ref, heads_ref, out_w_ref, wu_ref, wd_ref,
+    layer_ref, mid_grad_ref, heads_grad_ref, out_grad_ref, sums_ref, du_ref, dd_ref,
+    xt, grad_ref, y_ref, dx_ref, attn_ref
+):
     step = pl.program_id(0)
+    last = pl.num_programs(0) - 1
 
     @pl.when(step == 0)
     def _():
         xt[...] = x_ref[...].T
+        grad_ref[...] = (row_ref[5:6] * cot_ref[...].astype(F32)).astype(BF)
 
     up = dot(x_ref[...], wu_ref[0])
     root = math.sqrt(2.0 / math.pi)
@@ -1015,7 +996,7 @@
     half = 0.5 * (1.0 + bent)
     slope = half + 0.5 * up * (1.0 - bent * bent) * root * (1.0 + 3 * 0.044715 * square)
     act = (up * half).astype(BF)
-    grad = g_ref[...]
+    grad = grad_ref[...]
     up_grad = (dot(grad, wd_ref[0], 1, 1) * slope).astype(BF)
     dd_ref[0] = dot(act, grad, 0, 0).astype(BF)
     du_ref[0] = dot(xt[...], up_grad).astype(BF)
@@ -1032,252 +1013,461 @@
         y_ref[...] += y
         dx_ref[...] += dx
 
-
-def mlp(x, grad, up_full, down_full):
+    @pl.when(step == last)
+    def _():
+        block = 128
+        totals = [jnp.zeros((1, WIDTH), F32) for _ in range(4)]
+        for first in range(0, x_ref.shape[0], block):
+            here = slice(first, first + block)
+            values, dx, y = mid_ref[here], dx_ref[here], y_ref[here]
+            out_grad = cot_ref[here].astype(F32)
+            layer_ref[here] = (values + row_ref[5:6] * y).astype(BF)
+            normed, inverse = norm_parts(values)
+            mid_grad = out_grad + norm_back(normed, inverse, row_ref[4:5], dx)
+            mid_grad_ref[here] = mid_grad
+            attn_ref[here] = (row_ref[2:3] * mid_grad).astype(BF)
+            for index, term in enumerate(
+                (sum_ref[here] * mid_grad, dx, dx * normed, out_grad * y)
+            ):
+                totals[index] += jnp.sum(term, axis=0, keepdims=True)
+        for index in range(4):
+            sums_ref[index : index + 1] = totals[index]
+        sums_ref[4:8] = jnp.zeros((4, WIDTH), F32)
+        heads_grad_ref[...] = dot(attn_ref[...], out_w_ref[...], 1, 1).astype(BF)
+        out_grad_ref[...] = dot(heads_ref[...], attn_ref[...], 0, 0).astype(BF)
+
+
+def mlp(x, cot, mod_rows, hidden_mid, attn_sum, heads_out, out_full, up_full, down_full):
     rows = x.shape[0]
     ranks, _, units = up_full.shape
-    whole = pl.BlockSpec((rows, WIDTH), lambda r: (0, 0))
+    one = lambda shape: pl.BlockSpec(shape, lambda r: (0, 0), pipeline_mode=pl.Buffered(1))
+    whole, square, row = one((rows, WIDTH)), one((WIDTH, WIDTH)), one((8, WIDTH))
     up_spec = pl.BlockSpec((1, WIDTH, units), lambda r: (r, 0, 0))
     down_spec = pl.BlockSpec((1, units, WIDTH), lambda r: (r, 0, 0))
+    frames = (rows, WIDTH)
     return pl.pallas_call(
         mlp_kernel,
         grid=(ranks,),
-        in_specs=[whole, whole, up_spec, down_spec],
-        out_specs=[whole, whole, up_spec, down_spec],
+        in_specs=[whole, whole, row, whole, whole, whole, square, up_spec, down_spec],
+        out_specs=[whole, whole, whole, square, row, up_spec, down_spec],
         out_shape=[
-            jax.ShapeDtypeStruct((rows, WIDTH), F32),
-            jax.ShapeDtypeStruct((rows, WIDTH), F32),
+            jax.ShapeDtypeStruct(frames, BF),
+            jax.ShapeDtypeStruct(frames, F32),
+            jax.ShapeDtypeStruct(frames, BF),
+            jax.ShapeDtypeStruct((WIDTH, WIDTH), BF),
+            jax.ShapeDtypeStruct((8, WIDTH), F32),
             jax.ShapeDtypeStruct(up_full.shape, BF),
             jax.ShapeDtypeStruct(down_full.shape, BF),
         ],
-        scratch_shapes=[pltpu.VMEM((WIDTH, rows), BF)],
+        scratch_shapes=[
+            pltpu.VMEM((WIDTH, rows), BF),
+            pltpu.VMEM(frames, BF),
+            pltpu.VMEM(frames, F32),
+            pltpu.VMEM(frames, F32),
+            pltpu.VMEM(frames, BF),
+        ],
         compiler_params=pltpu.CompilerParams(vmem_limit_bytes=VMEM_LIMIT),
         name="mlp",
-    )(x, grad, up_full, down_full)
-
-
-def tail_kernel(
-    info_ref, x_ref, w_ref, cos_ref, sin_ref, dq_ref, dk_ref, dv_ref, dki_ref, dvi_ref,
-    value_ref, mid_ref, scale_ref, feat_ref, mel_w_ref, text_w_ref, ids_ref, keep_ref,
-    mod_in_ref, proj_ref,
-    sums_ref, act_ref, mel_ref, mel_in_ref, qkv_out, misc_out,
-    xt, weights, total_ref, hidden_ref, text_ref, qkv_grads, misc_grads,
-    mod_ref, line, every, part_ref, load_sems, line_sends, line_recvs, every_sends, every_recvs,
-    act_sends, act_recvs, mel_sems, *scratch
+    )(x, cot, mod_rows, hidden_mid, attn_sum, heads_out, out_full, up_full, down_full)
+
+
+def backward_kernel(
+    q, k0, v0, k1, v1, do, o, lse, cos, sin, mine_ref, row_ref, extra_ref, mod_in_ref,
+    x_ref, w_ref, value_ref, mid_ref, feat_ref, mel_w_ref, text_w_ref, proj_ref, layer_ref, down_grads, up_grads, out_grads,
+    sums_ref, act_ref, mel_out, layer_out, qkv_out, misc_out, down_out, up_out, out_out,
+    dq_v, dk_v, dv_v, dki_v, dvi_v, sent, xt, tiles, total_ref, hidden_ref, text_ref, blocks_v,
+    feat_v, mel_wv, text_wv, qkv_grads, misc_grads, mel_v,
+    mod_ref, line, every, part_ref, acts, down_buffer, up_buffer, out_buffer,
+    kv_sends, kv_recvs, load_sems, tile_sems, block_sems, line_sends, line_recvs, every_sends,
+    every_recvs, act_sends, act_recvs, end_sends, end_recvs, *scratch
 ):
+    step = pl.program_id(0)
+    last = pl.num_programs(0) - 1
     place = Place()
     dp, tp = place.dp, place.tp
     partner = (flip(dp, 1), flip(tp, 1))
     moves = place.core != tp % 2
-    rows = x_ref.shape[0]
+    stays = jnp.logical_not(moves)
+    rows = dq_v.shape[0]
     ranks, width = w_ref.shape[0], w_ref.shape[3]
-    loads = [
-        pltpu.make_async_copy(w_ref.at[:, part], weights.at[part % 2], load_sems.at[part])
-        for part in range(3)
+    pair_width = 2 * HEAD_DIM
+    steps = WIDTH // pair_width
+    size = 9
+    early = [
+        Reduce(place, grads.at[:, h], out.at[h], scratch[size * j : size * (j + 1)], buffer)
+        for j, (grads, out, h, buffer) in enumerate(
+            (
+                (down_grads, down_out, 0, down_buffer),
+                (up_grads, up_out, 0, up_buffer),
+                (down_grads, down_out, 1, down_buffer),
+                (up_grads, up_out, 1, up_buffer),
+                (out_grads, out_out, 0, out_buffer),
+            )
+        )
     ]
-    loads[0].start()
-    loads[1].start()
-    greet(
-        [(flip3(dp, k), tp) for k in range(1, 8)]
-        + [place.ahead(step) for step in (1, 2, 3)]
-        + [(flip(dp, 1), flip(tp, 1))]
-    )
-    size = 9
-    items = [
-        Reduce(place, qkv_grads.at[part], qkv_out.at[part], scratch[size * part : size * part + size], True)
+    late = [
+        Reduce(place, qkv_grads.at[part], qkv_out.at[part], scratch[size * (5 + part) : size * (6 + part)])
         for part in range(3)
     ] + [
         Reduce(
-            place, misc_grads.at[h], misc_out.at[h],
-            scratch[size * (3 + h) : size * (4 + h)], True, True,
+            place, misc_grads.at[h], misc_out.at[h], scratch[size * (8 + h) : size * (9 + h)],
+            absolute=True,
         )
         for h in range(2)
     ]
+    loads = [
+        pltpu.make_async_copy(source, target, load_sems.at[index])
+        for index, (source, target) in enumerate(
+            (
+                (x_ref, hidden_ref),
+                (feat_ref, feat_v),
+                (mel_w_ref, mel_wv),
+                (text_w_ref, text_wv),
+            )
+        )
+    ]
+    def tile_load(part, rank):
+        number = part * ranks + rank
+        return pltpu.make_async_copy(
+            w_ref.at[rank, part], tiles.at[number % 2], tile_sems.at[number]
+        )
+
+    span = tiles.shape[2]
+    proj_loads = [
+        pltpu.make_async_copy(
+            proj_ref.at[:, pl.ds(index * span, span)], tiles.at[index % 2], tile_sems.at[3 * ranks + index]
+        )
+        for index in range(proj_ref.shape[1] // span)
+    ]
+    block = blocks_v.shape[2]
+    block_loads = [
+        [
+            pltpu.make_async_copy(
+                source.at[pl.ds(index * block, block)], blocks_v.at[index % 2, kind], block_sems.at[index, kind]
+            )
+            for kind, source in enumerate((value_ref, mid_ref))
+        ]
+        for index in range(rows // block)
+    ]
+
+    def outward(index, source, target):
+        away = remote(source, target, (end_sends, end_recvs), index, partner)
+        here = pltpu.make_async_copy(source, target, end_sends.at[2 + index])
+        return away, here
+
+    layer_load = pltpu.make_async_copy(layer_ref, dq_v, load_sems.at[4])
+    ends = [outward(0, dq_v, layer_out), outward(1, mel_v, mel_out)]
+    kv_copies = lambda index: sibling_copies(
+        sent, (dki_v, dvi_v), (kv_sends, kv_recvs), index, pair_width, sent.shape[1]
+    )
+
+    def send_outward(index):
+        @pl.when(moves)
+        def _():
+            ends[index][0].start()
+
+        @pl.when(stays)
+        def _():
+            ends[index][1].start()
+
+    @pl.when(step == 0)
+    def _():
+        for copy in loads:
+            copy.start()
+        for copy in [tile_load(0, 0), tile_load(0, 1)] + block_loads[0] + block_loads[1]:
+            copy.start()
+        greet(
+            [(flip3(dp, k), tp) for k in range(1, 8)]
+            + [place.ahead(step) for step in (1, 2, 3)]
+            + [partner]
+        )
+
     flow = Flow()
-    xt[...] = x_ref[...].T
-    for part in range(3):
-        loads[part].wait()
+    for index in range(steps):
+        if index in JOINS:
+            flow.add(early[JOINS.index(index)])
+        stages = flow.take()
+
+        @pl.when(step == index)
+        def _(stages=stages):
+            for stage in stages:
+                stage()
+
+    columns = pl.ds(pl.multiple_of(step * pair_width, pair_width), pair_width)
+    slots = sent.shape[1]
+    length = mine_ref[0:1, 1:2].astype(jnp.int32)
+    biases = [
+        key_bias(length, place.core * rows, rows),
+        key_bias(length, (1 - place.core) * rows, rows),
+    ]
+    dq, results = attend_back_pair(biases, q, k0, v0, k1, v1, do, o, lse)
+    dq_v[:, columns] = turn(dq, cos[...], -sin[...]).astype(BF)
+    dk_v[:, columns] = results[0][0].astype(dk_v.dtype)
+    dv_v[:, columns] = results[0][1].astype(dv_v.dtype)
+
+    @pl.when(step >= slots)
+    def _():
+        for copy in kv_copies(step - slots):
+            copy.wait_send()
+
+    sent[0, step % slots] = results[1][0].astype(BF)
+    sent[1, step % slots] = results[1][1].astype(BF)
+    for copy in kv_copies(step):
+        copy.start()
+
+    @pl.when(step == last)
+    def _():
+        for copy in loads:
+            copy.wait()
+        flow.beat()
+        xt[...] = hidden_ref[...].T
+        total_ref[...] = jnp.zeros_like(total_ref)
+        cosine = jnp.concatenate([cos[...]] * (width // pair_width), axis=1)
+        sine = -jnp.concatenate([sin[...]] * (width // pair_width), axis=1)
+        extras = extra_ref[...].astype(F32)
+        ids = (extras[1:2] * 256.0 + extras[2:3]).astype(jnp.int32)
+        keep_cond = (1.0 - extras[0:1]) * mine_ref[0:1, 2:3]
+        for part in range(3):
+            if part == 1:
+
+                @pl.loop(0, steps)
+                def _(index):
+                    for copy in kv_copies(index):
+                        copy.wait_recv()
+
+                @pl.loop(steps - slots, steps)
+                def _(index):
+                    for copy in kv_copies(index):
+                        copy.wait_send()
+
+            def one_rank(rank, part=part):
+                side = pl.ds(pl.multiple_of(rank * width, width), width)
+                if part == 0:
+                    grad = dq_v[:, side]
+                elif part == 1:
+                    grad = turn(
+                        dk_v[:, side].astype(F32) + dki_v[:, side].astype(F32), cosine, sine
+                    ).astype(BF)
+                else:
+                    grad = (dv_v[:, side].astype(F32) + dvi_v[:, side].astype(F32)).astype(BF)
+                number = part * ranks + rank
+                tile_load(part, rank).wait()
+                qkv_grads[part, rank] = (
+                    dot(xt[...], grad).astype(BF).reshape(qkv_grads.shape[2:])
+                )
+                total_ref[...] += dot(grad, tiles[number % 2], 1, 1)
+
+                @pl.when(number + 2 < 3 * ranks)
+                def _():
+                    tile_load((number + 2) // ranks, (number + 2) % ranks).start()
+
+            pl.loop(0, ranks // 2)(one_rank)
+            flow.beat()
+            pl.loop(ranks // 2, ranks)(one_rank)
+            if part == 0:
+                layer_load.start()
+            if part == 2:
+                layer_load.wait()
+                send_outward(0)
+            flow.add(late[part])
+            flow.beat()
+
+        chunks = mod_ref.shape[1]
+        lanes = mod_ref.shape[2]
+        totals = [jnp.zeros((1, WIDTH), F32) for _ in range(2)]
+        for index in range(rows // block):
+            here = slice(index * block, (index + 1) * block)
+            for copy in block_loads[index]:
+                copy.wait()
+            grad = total_ref[here]
+            normed, inverse = norm_parts(blocks_v[index % 2, 0])
+            hidden_ref[here] = (
+                blocks_v[index % 2, 1] + norm_back(normed, inverse, row_ref[1:2], grad)
+            ).astype(BF)
+            totals[0] += jnp.sum(grad, axis=0, keepdims=True)
+            totals[1] += jnp.sum(grad * normed, axis=0, keepdims=True)
+            if index + 2 < rows // block:
+                for copy in block_loads[index + 2]:
+                    copy.start()
+        for index in range(4):
+            totals.append(mod_in_ref[index : index + 1])
+        for index in range(6):
+            for chunk in range(WIDTH // lanes):
+                row = index * (WIDTH // lanes) + chunk
+                mod_ref[row // chunks, row % chunks : row % chunks + 1, :] = totals[index][
+                    :, chunk * lanes : (chunk + 1) * lanes
+                ]
+        line_copies = [
+            remote(
+                mod_ref.at[(tp + step) % 4], line.at[tp], (line_sends, line_recvs), step - 1, place.ahead(step)
+            )
+            for step in (1, 2, 3)
+        ]
+        every_copies = [
+            remote(line, every.at[dp], (every_sends, every_recvs), k - 1, (flip3(dp, k), tp))
+            for k in range(1, 8)
+        ]
+        act_copies = [
+            remote(part_ref, acts.at[tp], (act_sends, act_recvs), step - 1, place.ahead(step))
+            for step in (1, 2, 3)
+        ]
+        for copy in line_copies:
+            copy.start()
+        line[tp] = mod_ref[tp]
+        flow.beat()
+
+        text_ref[...] = dot(hidden_ref[...], text_wv[...], 1, 1).astype(BF) * mine_ref[0:1, 3:4].astype(BF)
+        table_rows = VOCABULARY // ranks
+        split = misc_grads.shape[-2] * 16
+        shape = misc_grads.shape[2:]
+
+        @pl.loop(0, ranks)
+        def _(rank):
+            row = lax.broadcasted_iota(jnp.int32, (split, rows), 0) + rank * table_rows
+            one_hot = (row == ids).astype(F32).astype(BF)
+            misc_grads[0, rank] = dot(one_hot, text_ref[...]).astype(BF).reshape(shape)
+
+        flow.add(late[3])
+        flow.beat()
+        for copy in line_copies:
+            copy.wait()
+        every[dp] = line[...]
+        for copy in every_copies:
+            copy.start()
+        feat_rows = feat_v.shape[1] // ranks
+        rest = table_rows - split
+
+        def rest_of(rank, share):
+            row = lax.broadcasted_iota(jnp.int32, (rest, rows), 0) + (rank * table_rows + split)
+            one_hot = (row == ids).astype(F32).astype(BF)
+            table = dot(one_hot, text_ref[...]).astype(BF)
+            misc_grads[1, rank] = jnp.concatenate(
+                [table, share[:, :TEXT_DIM], share[:, TEXT_DIM:]], axis=0
+            ).reshape(shape)
+
         for rank in range(ranks):
-            side = slice(rank * width, (rank + 1) * width)
-            if part == 0:
-                grad = dq_ref[:, side]
-            elif part == 1:
-                grad = turn(
-                    dk_ref[:, side] + dki_ref[:, side].astype(F32), cos_ref[...], -sin_ref[...]
-                ).astype(BF)
-            else:
-                grad = (dv_ref[:, side] + dvi_ref[:, side].astype(F32)).astype(BF)
-            qkv_grads[part, rank] = (
-                dot(xt[...], grad).astype(BF).reshape(qkv_grads.shape[2:])
-            )
-            term = dot(grad, weights[part % 2, rank], 1, 1)
-            if part == 0 and rank == 0:
-                total_ref[...] = term
-            else:
-                total_ref[...] += term
-        if part == 0:
-            loads[2].start()
-        flow.add(items[part])
+            side = slice(rank * feat_rows, (rank + 1) * feat_rows)
+            rest_of(rank, dot(feat_v[:, side], hidden_ref[...], 0, 0).astype(BF))
+        flow.add(late[4])
         flow.beat()
-
-    normed_grad = total_ref[...]
-    normed, inverse = norm_parts(value_ref[...])
-    inner = normed_grad * (1.0 + scale_ref[...])
-    first = jnp.mean(inner, axis=-1, keepdims=True)
-    second = jnp.mean(inner * normed, axis=-1, keepdims=True)
-    hidden_ref[...] = (
-        mid_ref[...] + inverse * (inner - first - normed * second)
-    ).astype(BF)
-    chunks = mod_ref.shape[1]
-    lanes = mod_ref.shape[2]
-    mod_ref[...] = mod_in_ref[...]
-    for index, sums in enumerate(
-        (jnp.sum(normed_grad, axis=0, keepdims=True), jnp.sum(normed_grad * normed, axis=0, keepdims=True))
-    ):
-        for chunk in range(WIDTH // lanes):
-            row = index * (WIDTH // lanes) + chunk
-            mod_ref[row // chunks, row % chunks : row % chunks + 1, :] = sums[
-                :, chunk * lanes : (chunk + 1) * lanes
-            ]
-    line_copies = [
-        remote(
-            mod_ref.at[(tp + step) % 4], line.at[tp], (line_sends, line_recvs), step - 1, place.ahead(step)
-        )
-        for step in (1, 2, 3)
-    ]
-    every_copies = [
-        remote(line, every.at[dp], (every_sends, every_recvs), k - 1, (flip3(dp, k), tp))
-        for k in range(1, 8)
-    ]
-    act_copies = [
-        remote(part_ref, act_ref.at[tp], (act_sends, act_recvs), step - 1, place.ahead(step))
-        for step in (1, 2, 3)
-    ]
-    for copy in line_copies:
-        copy.start()
-    line[tp] = mod_ref[tp]
-    flow.beat()
-
-    hidden = hidden_ref[...]
-    text_ref[...] = dot(hidden, text_w_ref[...], 1, 1).astype(BF) * info_ref[2].astype(BF)
-    table_rows = VOCABULARY // ranks
-    split = misc_grads.shape[-2] * 16
-    block = misc_grads.shape[2:]
-    for rank in range(ranks):
-        row = lax.broadcasted_iota(jnp.int32, (split, rows), 0) + rank * table_rows
-        one_hot = (row == ids_ref[...]).astype(F32).astype(BF)
-        misc_grads[0, rank] = dot(one_hot, text_ref[...]).astype(BF).reshape(block)
-    flow.add(items[3])
-    flow.beat()
-    for copy in line_copies:
-        copy.wait()
-    every[dp] = line[...]
-    for copy in every_copies:
-        copy.start()
-    feat_rows = feat_ref.shape[1] // ranks
-    rest = table_rows - split
-    for rank in range(ranks):
-        row = lax.broadcasted_iota(jnp.int32, (rest, rows), 0) + (rank * table_rows + split)
-        one_hot = (row == ids_ref[...]).astype(F32).astype(BF)
-        table = dot(one_hot, text_ref[...]).astype(BF)
-        share = dot(feat_ref[:, rank * feat_rows : (rank + 1) * feat_rows], hidden, 0, 0).astype(BF)
-        misc_grads[1, rank] = jnp.concatenate(
-            [table, share[:, :TEXT_DIM], share[:, TEXT_DIM:]], axis=0
-        ).reshape(block)
-    flow.add(items[4])
-    flow.beat()
-    mel_part = dot(mel_w_ref[...], hidden, 1, 1)
-    bins = mel_part.shape[0] // 2
-    mel_ref[...] = info_ref[0] * mel_part[:bins] + keep_ref[...] * mel_part[bins:]
-    mel_copy = pltpu.make_async_remote_copy(
-        src_ref=mel_ref, dst_ref=mel_in_ref, send_sem=mel_sems.at[0], recv_sem=mel_sems.at[1],
-        device_id=partner, device_id_type=MESH,
-    )
-
-    @pl.when(moves)
-    def _():
-        mel_copy.start()
-
-    flow.beat()
-    for copy in every_copies:
-        copy.wait()
-    for pair in range(4):
-        sums_ref[pair] = every[2 * pair] + every[2 * pair + 1]
-    total = None
-    for chunk in range(chunks):
-        held = sums_ref[:, :, chunk, :].reshape(16, lanes).astype(BF)
-        term = dot(held, proj_ref[:, chunk * lanes : (chunk + 1) * lanes], 1, 1)
-        total = term if total is None else total + term
-    part_ref[...] = total
-    act_ref[tp] = total
-    for copy in act_copies:
-        copy.start()
-    while flow.beat():
-        pass
-    for copy in act_copies:
-        copy.wait()
-
-    @pl.when(moves)
-    def _():
-        mel_copy.wait()
-
-
-def tail(
-    info, x, weights, cosine, sine, dq, dk, dv, dk_in, dv_in, values, mid_grad, scale,
-    feats, mel_w, text_w, ids, keep, mod_part, mod_proj,
+        for copy in proj_loads[:2]:
+            copy.start()
+        mel_part = dot(mel_wv[...], hidden_ref[...], 1, 1)
+        bins = mel_part.shape[0] // 2
+        mel_v[...] = mine_ref[0:1, 0:1] * mel_part[:bins] + keep_cond * mel_part[bins:]
+        send_outward(1)
+        flow.beat()
+        for copy in every_copies:
+            copy.wait()
+        for pair in range(4):
+            sums_ref[pair] = every[2 * pair] + every[2 * pair + 1]
+        total = None
+        for index, copy in enumerate(proj_loads):
+            copy.wait()
+            for lane in range(0, span, lanes):
+                chunk = (index * span + lane) // lanes
+                held = sums_ref[:, :, chunk, :].reshape(16, lanes).astype(BF)
+                term = dot(held, tiles[index % 2, :, lane : lane + lanes], 1, 1)
+                total = term if total is None else total + term
+            if index + 2 < len(proj_loads):
+                proj_loads[index + 2].start()
+        part_ref[...] = total
+        acts[tp] = total
+        for copy in act_copies:
+            copy.start()
+        while flow.beat():
+            pass
+        for copy in act_copies:
+            copy.wait()
+        act_ref[...] = acts[...]
+
+        @pl.when(moves)
+        def _():
+            for away, _ in ends:
+                away.wait()
+
+        @pl.when(stays)
+        def _():
+            for _, here in ends:
+                here.wait()
+
+
+def backward(
+    query, own, other, heads_grad, heads_out, lse, cosine, sine, mine, mod_rows, extra, mod_part,
+    x, weights, values, mid_grad, feats, mel_w, text_w, mod_proj, layer, down_grad, up_grad, out_grad,
 ):
     rows = x.shape[0]
     ranks, width = weights.shape[0], weights.shape[3]
     table_rows = VOCABULARY // ranks
     misc_rows = table_rows + 2 * (feats.shape[1] // ranks)
-    chunks = mod_part.shape[1]
+    chunks = mod_proj.shape[1] // 128
+    pairs = WIDTH // (2 * HEAD_DIM)
     qkv_block = blocks((WIDTH, width))
     misc_block = blocks((misc_rows // 2, TEXT_DIM))
     dma = pltpu.SemaphoreType.DMA
-    vmem = pl.BlockSpec(memory_space=pltpu.VMEM)
-    smem = pl.BlockSpec(memory_space=pltpu.SMEM)
+    vmem = lambda shape, t=BF: pltpu.VMEM(shape, t)
+    tile = pl.BlockSpec((rows, 2 * HEAD_DIM), lambda i: (0, i))
+    one = lambda v: pl.BlockSpec(v.shape, lambda i: (0,) * v.ndim, pipeline_mode=pl.Buffered(1))
+    parts = lambda v, count: v.reshape(
+        (ranks, count) + blocks((v.shape[1] // count, v.shape[2]))
+    )
+    early = (parts(down_grad, 2), parts(up_grad, 2), parts(out_grad, 1))
     scratch = []
+    for index in (0, 1, 0, 1, 2):
+        block = early[index].shape
+        scratch += Reduce.scratch(block[-2] * 16, block[-1])
     for _ in range(3):
-        scratch += Reduce.scratch(WIDTH, width, True)
+        scratch += Reduce.scratch(WIDTH, width)
     for _ in range(2):
-        scratch += Reduce.scratch(misc_rows // 2, TEXT_DIM, True)
-    mel_shape = jax.ShapeDtypeStruct((mel_w.shape[0] // 2, rows), F32)
+        scratch += Reduce.scratch(misc_rows // 2, TEXT_DIM)
+    frames = (rows, WIDTH)
+    mel_shape = (mel_w.shape[0] // 2, rows)
+    sums_shape = jax.ShapeDtypeStruct((4, 4, chunks, 128), F32)
+    act_shape = jax.ShapeDtypeStruct((4, 16, WIDTH), F32)
     outs = pl.pallas_call(
-        tail_kernel,
-        in_specs=[smem, vmem, ANY] + [vmem] * 17,
-        out_specs=[vmem] * 3 + [ANY] * 3,
+        backward_kernel,
+        grid=(pairs,),
+        in_specs=[tile] * 7
+        + [pl.BlockSpec((2, 1, rows), lambda i: (i, 0, 0))]
+        + [one(v) for v in (cosine, sine, mine, mod_rows, extra, mod_part)]
+        + [ANY] * 12,
+        out_specs=[one(sums_shape), one(act_shape)] + [ANY] * 7,
         out_shape=[
-            jax.ShapeDtypeStruct((4, 4, chunks, 128), F32),
-            jax.ShapeDtypeStruct((4, 16, WIDTH), F32),
-            mel_shape,
-            mel_shape,
+            sums_shape,
+            act_shape,
+            jax.ShapeDtypeStruct(mel_shape, F32),
+            jax.ShapeDtypeStruct(frames, BF),
             jax.ShapeDtypeStruct((3,) + qkv_block, BF),
             jax.ShapeDtypeStruct((2,) + misc_block, BF),
-        ],
+        ]
+        + [jax.ShapeDtypeStruct(v.shape[1:], BF) for v in early],
         scratch_shapes=[
-            pltpu.VMEM((WIDTH, rows), BF),
-            pltpu.VMEM((2, ranks, WIDTH, width), BF),
-            pltpu.VMEM((rows, WIDTH), F32),
-            pltpu.VMEM((rows, WIDTH), BF),
-            pltpu.VMEM((rows, TEXT_DIM), BF),
-            pltpu.VMEM((3, ranks) + qkv_block, BF),
-            pltpu.VMEM((2, ranks) + misc_block, BF),
-            pltpu.VMEM((4, chunks, 128), F32),
-            pltpu.VMEM((4, chunks, 128), F32),
-            pltpu.VMEM((8, 4, chunks, 128), F32),
-            pltpu.VMEM((16, WIDTH), F32),
-            dma((3,)), dma((3,)), dma((3,)), dma((7,)), dma((7,)), dma((3,)), dma((3,)), dma((2,)),
+            vmem(frames), vmem(frames), vmem(frames), vmem(frames), vmem(frames),
+            vmem((2, 4, rows, 2 * HEAD_DIM)), vmem((WIDTH, rows)), vmem((2, WIDTH, width)),
+            vmem(frames, F32), vmem(frames), vmem((rows, TEXT_DIM)), vmem((2, 2, 64, WIDTH), F32),
+            vmem(feats.shape), vmem(mel_w.shape), vmem(text_w.shape),
+            vmem((3, ranks) + qkv_block), vmem((2, ranks) + misc_block), vmem(mel_shape, F32),
+            vmem((4, chunks, 128), F32), vmem((4, chunks, 128), F32), vmem((8, 4, chunks, 128), F32),
+            vmem((16, WIDTH), F32), vmem((4, 16, WIDTH), F32),
+        ]
+        + [vmem((ranks,) + v.shape[3:]) for v in early]
+        + [
+            dma((2, pairs)), dma((2, pairs)), dma((5,)), dma((3 * ranks + mod_proj.shape[1] // width,)),
+            dma((rows // 64, 2)),
+            dma((3,)), dma((3,)), dma((7,)), dma((7,)), dma((3,)), dma((3,)), dma((4,)), dma((2,)),
         ]
         + scratch,
         compiler_params=comm_params(4),
-        name="tail",
+        name="backward",
     )(
-        info, x, weights, cosine, sine, dq, dk, dv, dk_in, dv_in, values, mid_grad, scale,
-        feats, mel_w, text_w, ids, keep, mod_part, mod_proj,
+        query, *own, *other, heads_grad, heads_out, lse, cosine, sine, mine, mod_rows, extra, mod_part,
+        x, weights, values, mid_grad, feats, mel_w, text_w, mod_proj, layer, *early,
     )
-    return list(outs[:4]) + [
-        outs[4].reshape(3, WIDTH, width), outs[5].reshape(misc_rows, TEXT_DIM)
-    ]
+    outs = list(outs)
+    outs[4] = outs[4].reshape(3, WIDTH, width)
+    outs[5] = outs[5].reshape(misc_rows, TEXT_DIM)
+    outs[6:] = [o.reshape(v.shape[1:]) for o, v in zip(outs[6:], (down_grad, up_grad, out_grad))]
+    return outs
 
 
 def time_features(flow_times, width):
@@ -1347,27 +1537,25 @@
     def gather(shard):
         return relative(lax.all_gather(shard, "tp", axis=0))
 
-    sinus_own = time_features(flow_times, TIME_DIM)
-    facts = jnp.concatenate(
-        [
-            sinus_own,
-            flow_times[:, None],
-            lengths.astype(F32)[:, None],
-            1.0 - audio_drop.astype(F32)[:, None],
-            1.0 - text_drop.astype(F32)[:, None],
-            jnp.zeros((per_group, 124), F32),
-        ],
-        axis=1,
-    )
+    lane = jnp.arange(TIME_DIM + 128, dtype=jnp.int32)[None, :]
+    half_dim = TIME_DIM // 2
+    frequency = jnp.exp((lane % half_dim).astype(F32) * (-math.log(10000.0) / (half_dim - 1)))
+    column = lambda v: v[:, None]
+    angles = 1000.0 * column(flow_times) * frequency
+    facts = jnp.where(lane < half_dim, jnp.sin(angles), jnp.cos(angles))
+    for index, fact in enumerate((flow_times, lengths, 1 - audio_drop, 1 - text_drop)):
+        facts = jnp.where(lane == TIME_DIM + index, column(fact).astype(F32), facts)
+    sinus_own = facts[:, :TIME_DIM]
     act_own = jax.nn.silu(dot(sinus_own.astype(BF), time_proj)).astype(BF)
     mod_cols = dot(act_own, mod_proj)
     spare = -MEL_BINS % 16
     bins = MEL_BINS + spare
-    extra = jnp.stack(
-        [span_mask.astype(BF), (text_ids // 256).astype(BF), (text_ids % 256).astype(BF)]
-        + [jnp.zeros((local_rows,), BF)] * 13,
-        axis=0,
-    )
+    line = jnp.arange(16, dtype=jnp.int32)[:, None]
+    extra = jnp.where(
+        line == 0,
+        span_mask[None, :],
+        jnp.where(line == 1, text_ids[None, :] // 256, jnp.where(line == 2, text_ids[None, :] % 256, 0)),
+    ).astype(BF)
     padded = lambda v: jnp.pad(v, ((0, spare), (0, 0)))
     mel, noise = padded(mel_frames.T), padded(noise_frames.T)
     mel_w = jnp.concatenate(
@@ -1376,8 +1564,8 @@
     text_w = in_proj[2 * MEL_BINS :]
     qkv_shard = qkv_proj.transpose(1, 0, 2)
     positions = half * local_rows + jnp.arange(local_rows, dtype=jnp.int32)
-    cosine, sine = rope_tables(positions, WIDTH // tp_size)
-    narrow = lambda table: table[:, : 2 * HEAD_DIM]
+    cosine, sine = rope_tables(positions, 2 * HEAD_DIM)
+    wide = lambda table: jnp.tile(table, (1, WIDTH // tp_size // (2 * HEAD_DIM)))
     if direct:
         pad = ((0, 8 - per_group), (0, 0))
         (
@@ -1385,27 +1573,24 @@
             attn_sum, hidden_mid, normed_mlp, feats, text_emb, hidden, normed_attn, query, key, value, key_in, value_in, heads_out, lse,
         ) = forward(
             mel, noise, extra, jnp.pad(facts, pad), jnp.pad(mod_cols, pad), cotangent, qkv_shard, out_proj, up_proj,
-            down_proj, text_table, mel_w, text_w, narrow(cosine), narrow(sine),
+            down_proj, text_table, mel_w, text_w, cosine, sine,
         )
         cot = jnp.where(stay, cotangent, cot)
         facts_all = facts_all[:, :per_group].reshape(utt_total, -1)
-        mod_row = mod_rows[:6].reshape(1, 6 * WIDTH)
-        mine = mine[:1]
     else:
         facts_all = lax.all_gather(facts, "dp", axis=0, tiled=True)
         near = lax.all_gather(lax.all_gather(mod_cols, "tp", axis=1, tiled=True), "dp", axis=0, tiled=True)
         mod_row = lax.dynamic_slice_in_dim(near, utterance, 1, 0)
         mel, noise, extra, cot = swap(mel), swap(noise), swap(extra), swap(cotangent)
         mine = lax.dynamic_slice_in_dim(facts_all, utterance, 1, 0)[:, TIME_DIM:]
-    shift_attn, scale_attn, gate_attn, shift_mlp, scale_mlp, gate_mlp = jnp.split(mod_row, 6, axis=1)
-    time_here, length, keep_audio, keep_text = (mine[0, i] for i in range(4))
-    length = length.astype(jnp.int32)
-    extra = extra[:3].astype(jnp.int32)
-    ids = extra[1] * 256 + extra[2]
-    out_grad = cot.astype(F32)
-    keep_cond = (1.0 - extra[0].astype(F32))[None, :] * keep_audio
-    info = jnp.stack([length, half * local_rows, (1 - half) * local_rows])
     if not direct:
+        shift_attn, scale_attn, gate_attn, shift_mlp, scale_mlp, gate_mlp = jnp.split(mod_row, 6, axis=1)
+        time_here, length, keep_audio, keep_text = (mine[0, i] for i in range(4))
+        length = length.astype(jnp.int32)
+        extra = extra[:3].astype(jnp.int32)
+        ids = extra[1] * 256 + extra[2]
+        keep_cond = (1.0 - extra[0].astype(F32))[None, :] * keep_audio
+        info = jnp.stack([length, half * local_rows, (1 - half) * local_rows])
         mel, noise = mel.astype(F32), noise.astype(F32)
         noisy = (1.0 - time_here) * noise + time_here * mel
         feats = jnp.concatenate([noisy, mel * keep_cond], axis=0).astype(BF)
@@ -1416,7 +1601,7 @@
         hidden = dot(features, in_proj)
         norm_a, inv_a = norm_parts(hidden)
         normed_attn = (norm_a * (1.0 + scale_attn) + shift_attn).astype(BF)
-        query, key, value, key_in, value_in = project_qkv(normed_attn, qkv_full, cosine, sine)
+        query, key, value, key_in, value_in = project_qkv(normed_attn, qkv_full, wide(cosine), wide(sine))
         heads_out, lse = attend(info, query, (key, value), (key_in, value_in))
         out_full, up_full, down_full = (gather(shard) for shard in (out_proj, up_proj, down_proj))
     own, other = (key, value), (key_in, value_in)
@@ -1424,32 +1609,13 @@
     if not direct:
         attn_sum = dot(heads_out, out_full)
         hidden_mid = hidden + gate_attn * attn_sum
-    norm_m, inv_m = norm_parts(hidden_mid)
-    if not direct:
-        normed_mlp = (norm_m * (1.0 + scale_mlp) + shift_mlp).astype(BF)
-    mlp_grad = (gate_mlp * out_grad).astype(BF)
-    mlp_sum, normed_mlp_grad, up_grad, down_grad = mlp(normed_mlp, mlp_grad, up_full, down_full)
-    layer_out = swap((hidden_mid + gate_mlp * mlp_sum).astype(BF))
-    mid_grad = out_grad + norm_back(norm_m, inv_m, scale_mlp, normed_mlp_grad)
-    attn_grad = (gate_attn * mid_grad).astype(BF)
-    out_grad_w = dot(heads_out, attn_grad, 0, 0).astype(BF).reshape(tp_size, -1, WIDTH)
-    heads_grad = dot(attn_grad, out_full, 1, 1).astype(BF)
-    halves = lambda v, count: v.reshape((tp_size, count, v.shape[1] // count) + v.shape[2:])
-    early = (halves(up_grad, 2), halves(down_grad, 2), halves(out_grad_w, 1))
-    (dq, dk, dv, dk_in, dv_in), early_out = attend_back(
-        info, query, own, other, heads_grad, heads_out, lse, narrow(cosine), narrow(sine),
-        early if direct else (),
+        normed, _ = norm_parts(hidden_mid)
+        normed_mlp = (normed * (1.0 + scale_mlp) + shift_mlp).astype(BF)
+        mod_rows = jnp.pad(mod_row.reshape(6, WIDTH), ((0, 2), (0, 0)))
+    layer, mid_grad, heads_grad, out_grad_w, mlp_sums, up_grad, down_grad = mlp(
+        normed_mlp, cot, mod_rows, hidden_mid, attn_sum, heads_out, out_full, up_full, down_full
     )
-    column_sum = lambda values: jnp.sum(values, axis=0, keepdims=True)
-    mod_rest = jnp.concatenate(
-        [
-            column_sum(attn_sum * mid_grad),
-            column_sum(normed_mlp_grad),
-            column_sum(normed_mlp_grad * norm_m),
-            column_sum(out_grad * mlp_sum),
-        ],
-        axis=1,
-    )
+    out_grad_w = out_grad_w.reshape(tp_size, -1, WIDTH)
     sinus = facts_all[:, :TIME_DIM].astype(BF)
     time_embed = dot(sinus, time_proj)
     time_act = jax.nn.silu(time_embed).astype(BF)
@@ -1467,20 +1633,25 @@
         axis=axis,
     )
     if direct:
-        sums, act_parts, mel_own, mel_came, qkv_out, misc_out = tail(
-            jnp.stack([time_here, keep_audio, keep_text, keep_text]),
-            normed_attn, qkv_full, cosine, sine, dq, dk, dv, dk_in, dv_in, hidden, mid_grad,
-            scale_attn, spaced(features, 1), mel_w, text_w, ids[None, :], keep_cond,
-            jnp.pad(mod_rest, ((0, 0), (2 * WIDTH, 0))).reshape(tp_size, -1, 128), mod_proj,
-        )
-        mel_grad = jnp.where(stay, mel_own, mel_came)[:MEL_BINS].T
+        sums, act_parts, mel_grad, layer_out, qkv_out, misc_out, *early_out = backward(
+            query, own, other, heads_grad, heads_out, lse, cosine, sine, mine, mod_rows, extra, mlp_sums,
+            normed_attn, qkv_full, hidden, mid_grad, spaced(features, 1), mel_w, text_w, mod_proj,
+            layer, down_grad, up_grad, out_grad_w,
+        )
+        mel_grad = mel_grad[:MEL_BINS].T
         order = lambda v: v.reshape((4, 2, 2) + v.shape[2:]).swapaxes(1, 2)
         mod_sums = order(sums).reshape(utt_total, -1).astype(BF)
         act_grad = jnp.sum(act_parts, axis=0)
         act_grad = order(act_grad.reshape(4, 4, WIDTH)).reshape(utt_total, WIDTH)
     else:
+        layer_out = swap(layer)
+        mod_rest = mlp_sums[:4].reshape(1, 4 * WIDTH)
+        column_sum = lambda values: jnp.sum(values, axis=0, keepdims=True)
+        dq, dk, dv, dk_in, dv_in = attend_back(
+            info, query, own, other, heads_grad, heads_out, lse, cosine, sine
+        )
         qkv_grad, normed_attn_grad = project_qkv_back(
-            normed_attn, qkv_full, cosine, sine, dq, dk, dv, dk_in, dv_in
+            normed_attn, qkv_full, wide(cosine), wide(sine), dq, dk, dv, dk_in, dv_in
         )
         hidden_grad = (mid_grad + norm_back(norm_a, inv_a, scale_attn, normed_attn_grad)).astype(BF)
         in_grad = dot(features, hidden_grad, 0, 0).astype(BF)
@@ -1510,7 +1681,7 @@
             )
 
         absolute = lambda values: jnp.roll(values, tp_rank, axis=0)
-        early_out = [reduce(absolute(values)) for values in (up_grad, down_grad, out_grad_w)]
+        early_out = [reduce(absolute(values)) for values in (down_grad, up_grad, out_grad_w)]
         qkv_out = reduce(absolute(qkv_grad))
         misc_out = reduce(misc)
     mod_grad = dot(time_act, mod_sums, 0, 0)
@@ -1518,7 +1689,7 @@
     time_rows = TIME_DIM // tp_size
     sinus_share = lax.dynamic_slice_in_dim(sinus, tp_rank * time_rows, time_rows, 1)
     time_grad = dot(sinus_share, embed_grad, 0, 0)
-    up_out, down_out, out_out = (values.astype(F32) for values in early_out)
+    down_out, up_out, out_out = (values.astype(F32) for values in early_out)
     misc_out = misc_out.astype(F32)
     right = table_rows + in_rows + in_pad
     in_out = jnp.concatenate(

time: 345 us -> 308 us (0.89)
  other arithmetic: 35 us -> 19.1 us
  local copies, waits for them, and re-layouts: 17.9 us -> 11 us
  matrix products: 14 us -> 7.43 us
    reduce_sum x4 -> x0, other arithmetic: 8.91 us -> none  [the longest x2 6.8 us: body(): column_sum = lambda values: jnp.sum(values, axis=0, keepdims=True)]
    dot_general x6 -> x4, matrix products: 14 us -> 7.43 us  [dot(): lax.dot_general(left, right, (((left_dim,), (right_dim,)), ((), ())), pre...]
    pallas_call x3 -> x2, Pallas kernels: 179 us -> 176 us  [the longest x1 147 us: backward(): pl.pallas_call(backward_kernel, grid=(pairs,), in_specs=[tile] * 7 + [pl....]
    convert_element_type x7 -> x6, other arithmetic: 7.03 us -> 7.13 us  [the longest x3 4.43 us: body(): down_out, up_out, out_out = (values.astype(F32) for values in early_out)]
  transfers between devices with their start and end apart: 1 -> 0, of which waited for: 0 -> 0; matrix products, arithmetic and copies ran while one was open for 10% -> 0% of each run, Pallas kernels for 46% -> 0%
where the time goes in v3:
time: 308 us; the launch traced here: 306 us
  Pallas kernels  268 us (87%)
  other arithmetic  19.1 us (6%)
  local copies, waits for them, and re-layouts  11 us (4%)
  matrix products  7.43 us (2%)
    pallas_call x1, Pallas kernels, backward(): pl.pallas_call(backward_kernel, grid=(pairs,), in_specs=[tile] * 7 + [pl....  147 us
    pallas_call x1, Pallas kernels, forward(): pl.pallas_call(forward_kernel, grid=(WIDTH // (2 * HEAD_DIM),), in_specs=...  91.4 us
    pallas_call x1, Pallas kernels, mlp(): pl.pallas_call(mlp_kernel, grid=(ranks,), in_specs=[whole, whole, row, wh...  29 us
    dot_general x4, matrix products, dot(): lax.dot_general(left, right, (((left_dim,), (right_dim,)), ((), ())), pre...  7.43 us

profile of v3, /device:TPU:0, one launch (start us, length us, event | category | flops | bytes accessed | tf_op | source)
XLA Modules:
  0.0 306.4 jit_solution(5722620947650164178)
XLA Ops:
  0.7 1.7 pad.35.mel
  2.4 1.5 pad.36.noise
  3.9 0.7 add_select_fusion.2
  4.6 1.4 select_convert_fusion.extra
  6.0 0.7 convert_element_type.106
  6.7 0.7 subtract_convert_fusion
  7.4 0.7 broadcast_multiply_fusion
  8.0 0.8 fusion.31
  8.8 0.6 pad.37.facts
  9.4 2.5 fusion.23
  11.9 0.6 pad.38.mods
  12.7 0.8 fusion.8.mel_w.mel_w_ref
  13.6 1.0 slice.58.text_w.text_w_ref
  14.6 1.8 fusion.9
  16.5 91.4 %forward.1 = (f32[8,8,384]{2,1,0:T(8,128)}, f32[8,1024]{1,0:T(8,128)}, f32[8,128]{1,0:T(8,128)}, bf16[16,512]{1,0:T(8,128)(2,1)}, bf16[512,1024]{1,0:T(8,128)(2,...) custom-call(bf16[112,512]{1,0:T(8,128)(2,1)} %pad.35.mel, ...), custom_call_target="tpu_custom_call" | custom-call | tf_op jit(solution)/shard_map/forward/pallas_call | solution.py:824
  107.9 1.1 broadcast_select_fusion.cot_ref
  109.0 29.0 %mlp.1 = (bf16[512,1024]{1,0:T(8,128)(2,1)}, f32[512,1024]{1,0:T(8,128)}, bf16[512,1024]{1,0:T(8,128)(2,1)}, bf16[1024,1024]{1,0:T(8,128)(2,1)}, f32[8,1024]{1,0...) custom-call(bf16[512,1024]{1,0:T(8,128)(2,1)} %get-tuple-element.54.x_ref, ...), custom_call_target="tpu_custom_call" | custom-call | tf_op jit(solution)/shard_map/mlp/pallas_call | solution.py:1048
  138.5 0.3 fusion.11
  138.7 1.2 fusion.5.feat_ref
  139.9 147.5 %backward.1 = (f32[4,4,12,128]{3,2,1,0:T(8,128)}, f32[4,16,1024]{2,1,0:T(8,128)}, f32[112,512]{1,0:T(8,128)}, bf16[512,1024]{1,0:T(8,128)(2,1)}, bf16[3,2,2,2,2,...) custom-call(bf16[512,1024]{1,0:T(8,128)(2,1)} %get-tuple-element.49., ...), custom_call_target="tpu_custom_call" | custom-call | tf_op jit(solution)/shard_map/backward/pallas_call | solution.py:1427
  287.4 1.6 slice_bitcast_fusion
  289.0 1.5 bitcast_convert_fusion.2
  290.6 0.9 pad_maximum_fusion
  291.5 1.1 slice.76
  292.7 0.9 slice.92
  294.0 1.0 fusion.18
  295.0 3.7 %fusion.15 = f32[1024,1536]{1,0:T(8,128)} fusion(bf16[2,8,12,128]{3,2,1,0:T(8,128)(2,1)S(1)} %bitcast.62, f32[16,1024]{1,0:T(8,128)S(1)} %fusion.44), kind=kOutput, calls=%fused_computation.37 | convolution fusion | flops 50413568 | bytes 6406144 | tf_op jit(solution)/shard_map/dot_general | solution.py:27
  298.7 2.0 convert_bitcast_fusion
  300.8 1.1 bitcast_convert_fusion.3
  301.9 1.7 bitcast_convert_fusion.1
  303.6 1.6 bitcast_convert_fusion
  305.2 1.0 copy.39
  (51 shorter events, 1.1 us)
Async XLA Ops:
  0.6 8.8 %copy-start = (bf16[256,1024]{1,0:T(8,128)(2,1)S(1)}, bf16[256,1024]{1,0:T(8,128)(2,1)}, u32[]{:S(2)}) copy-start(bf16[256,1024]{1,0:T(8,128)(2,1)} %param.27) | copy-start | bytes 1572868
  0.7 11.9 %copy-start.4 = (bf16[712,1024]{1,0:T(8,128)(2,1)S(1)}, bf16[712,1024]{1,0:T(8,128)(2,1)}, u32[]{:S(2)}) copy-start(bf16[712,1024]{1,0:T(8,128)(2,1)} %param.25) | copy-start | bytes 4374532
  8.8 3.9 %copy-start.13 = (pred[112]{0:T(512)(128)(4,1)S(1)}, pred[112]{0:T(512)(128)(4,1)}, u32[]{:S(2)}) copy-start(pred[112]{0:T(512)(128)(4,1)} %constant.129.clone.1) | copy-start | bytes 340
  16.5 91.4 %copy-start.1 = (bf16[512,1024]{1,0:T(8,128)(2,1)S(1)}, bf16[512,1024]{1,0:T(8,128)(2,1)}, u32[]{:S(2)}) copy-start(bf16[512,1024]{1,0:T(8,128)(2,1)} %cot.1) | copy-start | bytes 3145732
  109.0 29.0 %copy-start.2 = (bf16[512,512]{1,0:T(8,128)(2,1)S(1)}, bf16[512,512]{1,0:T(8,128)(2,1)}, u32[]{:S(2)}) copy-start(bf16[512,512]{1,0:T(8,128)(2,1)} %get-tuple-element.73) | copy-start | bytes 1572868
  109.0 29.2 %copy-start.10 = (bf16[224,512]{1,0:T(8,128)(2,1)S(1)}, bf16[224,512]{1,0:T(8,128)(2,1)}, u32[]{:S(2)}) copy-start(bf16[224,512]{1,0:T(8,128)(2,1)} %get-tuple-element.72) | copy-start | bytes 688132
  109.0 29.5 %copy-start.12 = (pred[192]{0:T(512)(128)(4,1)S(1)}, pred[192]{0:T(512)(128)(4,1)}, u32[]{:S(2)}) copy-start(pred[192]{0:T(512)(128)(4,1)} %constant.138.clone.1) | copy-start | bytes 580
  290.6 3.2 %copy-start.9 = (f32[4,16,1024]{2,1,0:T(8,128)S(1)}, f32[4,16,1024]{2,1,0:T(8,128)}, u32[]{:S(2)}) copy-start(f32[4,16,1024]{2,1,0:T(8,128)} %get-tuple-element.82) | copy-start | bytes 786436
  291.5 3.4 %copy-start.11 = (f32[4,4,12,128]{3,2,1,0:T(8,128)S(1)}, f32[4,4,12,128]{3,2,1,0:T(8,128)}, u32[]{:S(2)}) copy-start(f32[4,4,12,128]{3,2,1,0:T(8,128)} %get-tuple-element.83) | copy-start | bytes 294916
  295.0 3.7 %copy-start.3 = (bf16[3,2,2,2,2,64,256]{6,5,4,3,2,1,0:T(8,128)(2,1)S(1)}, bf16[3,2,2,2,2,64,256]{6,5,4,3,2,1,0:T(8,128)(2,1)}, u32[]{:S(2)}) copy-start(bf16[3,2,2,2,2,64,256]{6,5,4,3,2,1,0:T(8,128)(2,1)} %get-tuple-element.84) | copy-start | bytes 4718596
  298.7 2.0 copy-start.8
  298.7 3.2 %copy-start.6 = (bf16[2,2,2,2,2,32,512]{6,5,4,3,2,1,0:T(8,128)(2,1)S(1)}, bf16[2,2,2,2,2,32,512]{6,5,4,3,2,1,0:T(8,128)(2,1)}, u32[]{:S(2)}) copy-start(bf16[2,2,2,2,2,32,512]{6,5,4,3,2,1,0:T(8,128)(2,1)} %get-tuple-element.86) | copy-start | bytes 3145732
  300.8 2.8 copy-start.5
  303.6 1.6 copy-start.7
